TPU v7x, 256 devices: a whole 4x4x8 slice. The times are simulated.
256 devices in a mesh: row: 16 (over z, x_lo), col: 16 (over x_hi, y, core).
Axes of the slice: x: 4 (x_hi: 2, x_lo: 2; x = x_hi * 2 + x_lo), y: 4, z: 8, core: 2. Of those that a mesh axis runs over, the one named last changes fastest.
Arguments:
- replica_weights: float32 [16, 16, 128, 2048], P('row', 'col'), may hold values from -4.5 to 4.5
- replica_first: float32 [16, 16, 128, 2048], P('row', 'col'), may hold values from -3.9 to 3.9
- replica_second: float32 [16, 16, 128, 2048], P('row', 'col'), may hold values from 0.05 to 8
- replica_grads: float32 [16, 16, 128, 2048], P('row', 'col'), may hold values from -9 to 9
Outputs:
- mean_weights: float32 [128, 2048], replicated
- mean_first: float32 [128, 2048], replicated
- mean_second: float32 [128, 2048], replicated
All inputs are finite; a program needn't handle non-finite values.
Results may differ from a plain program's by a relative error of at most 0.00002.
Values sent between devices are 32-bit elements; how exact they have to be, the bound alone decides.
No kernel may reach another device: no remote copies, remote signals or barrier semaphores. Data moves between devices by JAX's collectives and lax.ppermute only.
A program may use at most 64 MiB of HBM per device.

v0:
```python
import jax
import jax.numpy as jnp
from jax import lax
from jax.sharding import PartitionSpec as P

bias_one = 0.9999734386011124
bias_two = 0.994079470779666


def row_reduce(arrays):
    sums = (
        lax.psum_scatter(arrays[0], "row", scatter_dimension=0, tiled=True),
        lax.psum_scatter(arrays[1], "row", scatter_dimension=0, tiled=True),
        lax.psum_scatter(arrays[2], "row", scatter_dimension=0, tiled=True),
    )
    scale = 1.0 / lax.axis_size("row")
    return tuple((total * scale for total in sums))


def row_expand(arrays):
    return lax.all_gather(arrays, "row", axis=0, tiled=True)


def col_reduce(arrays):
    sums = lax.psum_scatter(arrays, "col", scatter_dimension=1, tiled=True)
    scale = 1.0 / lax.axis_size("col")
    return tuple((total * scale for total in sums))


def col_expand(arrays):
    return lax.all_gather(arrays, "col", axis=1, tiled=True)


def on_device(replica_weights, replica_first, replica_second, replica_grads):
    old_weights = replica_weights[0, 0]
    gradient = replica_grads[0, 0]
    first = 0.9 * replica_first[0, 0] + 0.1 * gradient
    second = 0.95 * replica_second[0, 0] + 0.05 * gradient * gradient
    update = first / bias_one / (jnp.sqrt(second / bias_two) + 1e-08) + 0.1 * old_weights
    weights = old_weights - 0.003 * update
    arrays = (weights, first, second)
    arrays = row_expand(row_reduce(arrays))
    arrays = col_expand(col_reduce(arrays))
    return (arrays[0], arrays[1], arrays[2])


def solution(mesh):
    in_specs = (
        P("row", "col", None, None),
        P("row", "col", None, None),
        P("row", "col", None, None),
        P("row", "col", None, None),
    )
    out_specs = (P(), P(), P())
    return jax.shard_map(
        on_device, mesh=mesh, in_specs=in_specs, out_specs=out_specs, check_vma=False
    )
```

profile of v0, /device:TPU:1, one launch (start us, length us, event | category | flops | bytes accessed | tf_op | source)
XLA Modules:
  0.0 846.0 jit_solution(16731180733294012285)
XLA Ops:
  7.2 0.0 reduce-scatter.7.cloned.1.call-start
  7.2 4.4 bitcast_subtract_fusion
  11.6 0.0 reduce-scatter.7.cloned.1.call-update
  11.7 0.0 reduce-scatter.11.cloned.1.call-start
  11.7 0.7 reduce-scatter.11.cloned.1.call-update
  12.4 0.0 reduce-scatter.15.cloned.1.call-start
  12.5 0.7 reduce-scatter.15.cloned.1.call-update
  13.1 0.0 all-gather.7.cloned.1.call-start
  13.2 63.1 %reduce-scatter.7.cloned.1.call-done = f32[8,2048]{1,0:T(8,128)} async-done(((f32[128,2048]{1,0:T(8,128)}), f32[8,2048]{1,0:T(8,128)}) %reduce-scatter.7.cloned.1.call-update) | async-done | bytes 65552 | tf_op jit(solution)/shard_map/reduce_scatter | solution.py:12
  76.3 1.5 broadcast_multiply_fusion.5
  77.8 0.0 all-gather.7.cloned.1.call-update
  77.8 0.0 all-gather.11.cloned.1.call-start
  77.8 71.8 %reduce-scatter.11.cloned.1.call-done = f32[8,2048]{1,0:T(8,128)} async-done(((f32[128,2048]{1,0:T(8,128)}), f32[8,2048]{1,0:T(8,128)}) %reduce-scatter.11.cloned.1.call-update) | async-done | bytes 65552 | tf_op jit(solution)/shard_map/reduce_scatter | solution.py:13
  149.6 1.5 broadcast_multiply_fusion.4
  151.1 0.0 all-gather.11.cloned.1.call-update
  151.1 0.0 all-gather.15.cloned.1.call-start
  151.2 71.5 %reduce-scatter.15.cloned.1.call-done = f32[8,2048]{1,0:T(8,128)} async-done(((f32[128,2048]{1,0:T(8,128)}), f32[8,2048]{1,0:T(8,128)}) %reduce-scatter.15.cloned.1.call-update) | async-done | bytes 65552 | tf_op jit(solution)/shard_map/reduce_scatter | solution.py:14
  222.7 1.5 broadcast_multiply_fusion.3
  224.2 0.0 all-gather.15.cloned.1.call-update
  224.2 0.0 reduce-scatter.9.cloned.1.call-start
  224.3 69.1 %all-gather.7.cloned.1.call-done = f32[128,2048]{1,0:T(8,128)} async-done(((f32[8,2048]{1,0:T(8,128)}), f32[128,2048]{1,0:T(8,128)}) %all-gather.7.cloned.1.call-update) | async-done | bytes 1048592 | tf_op jit(solution)/shard_map/all_gather | solution.py:21
  293.4 0.0 reduce-scatter.9.cloned.1.call-update
  293.4 0.0 reduce-scatter.13.cloned.1.call-start
  293.5 71.5 %all-gather.11.cloned.1.call-done = f32[128,2048]{1,0:T(8,128)} async-done(((f32[8,2048]{1,0:T(8,128)}), f32[128,2048]{1,0:T(8,128)}) %all-gather.11.cloned.1.call-update) | async-done | bytes 1048592 | tf_op jit(solution)/shard_map/all_gather | solution.py:21
  365.0 0.0 reduce-scatter.13.cloned.1.call-update
  365.0 0.0 reduce-scatter.17.cloned.1.call-start
  365.1 71.5 %all-gather.15.cloned.1.call-done = f32[128,2048]{1,0:T(8,128)} async-done(((f32[8,2048]{1,0:T(8,128)}), f32[128,2048]{1,0:T(8,128)}) %all-gather.15.cloned.1.call-update) | async-done | bytes 1048592 | tf_op jit(solution)/shard_map/all_gather | solution.py:21
  436.6 0.0 reduce-scatter.17.cloned.1.call-update
  436.6 0.0 all-gather.9.cloned.1.call-start
  436.7 87.6 %reduce-scatter.9.cloned.1.call-done = f32[128,128]{1,0:T(8,128)} async-done(((f32[128,2048]{1,0:T(8,128)}), f32[128,128]{1,0:T(8,128)}) %reduce-scatter.9.cloned.1.call-update) | async-done | bytes 65552 | tf_op jit(solution)/shard_map/reduce_scatter | solution.py:25
  524.3 1.5 broadcast_multiply_fusion.2
  525.7 0.0 all-gather.9.cloned.1.call-update
  525.8 0.0 all-gather.13.cloned.1.call-start
  525.8 76.2 %reduce-scatter.13.cloned.1.call-done = f32[128,128]{1,0:T(8,128)} async-done(((f32[128,2048]{1,0:T(8,128)}), f32[128,128]{1,0:T(8,128)}) %reduce-scatter.13.cloned.1.call-update) | async-done | bytes 65552 | tf_op jit(solution)/shard_map/reduce_scatter | solution.py:25
  602.0 1.5 broadcast_multiply_fusion.1
  603.5 0.0 all-gather.13.cloned.1.call-update
  603.5 0.0 all-gather.17.cloned.1.call-start
  603.5 76.7 %reduce-scatter.17.cloned.1.call-done = f32[128,128]{1,0:T(8,128)} async-done(((f32[128,2048]{1,0:T(8,128)}), f32[128,128]{1,0:T(8,128)}) %reduce-scatter.17.cloned.1.call-update) | async-done | bytes 65552 | tf_op jit(solution)/shard_map/reduce_scatter | solution.py:25
  680.3 1.5 broadcast_multiply_fusion
  681.7 0.0 all-gather.17.cloned.1.call-update
  681.8 50.6 %all-gather.9.cloned.1.call-done = f32[128,2048]{1,0:T(8,128)} async-done(((f32[128,128]{1,0:T(8,128)}), f32[128,2048]{1,0:T(8,128)}) %all-gather.9.cloned.1.call-update) | async-done | bytes 1048592 | tf_op jit(solution)/shard_map/all_gather | solution.py:31
  732.4 51.0 %all-gather.13.cloned.1.call-done = f32[128,2048]{1,0:T(8,128)} async-done(((f32[128,128]{1,0:T(8,128)}), f32[128,2048]{1,0:T(8,128)}) %all-gather.13.cloned.1.call-update) | async-done | bytes 1048592 | tf_op jit(solution)/shard_map/all_gather | solution.py:31
  783.4 0.0 copy-start
  783.4 50.9 %all-gather.17.cloned.1.call-done = f32[128,2048]{1,0:T(8,128)} async-done(((f32[128,128]{1,0:T(8,128)}), f32[128,2048]{1,0:T(8,128)}) %all-gather.17.cloned.1.call-update) | async-done | bytes 1048592 | tf_op jit(solution)/shard_map/all_gather | solution.py:31
  834.3 2.3 copy.10
  836.6 0.0 copy-done
  836.6 0.0 copy-start.1
  836.6 1.0 copy.11
  837.6 0.6 copy-done.1
  838.2 1.0 copy.12
Async XLA Ops:
  7.2 69.1 %reduce-scatter.7.cloned.1.call-start = ((), (), s32[]{:S(2)}) async-start(), calls=%async_computation.6 | async-start | bytes 1114112 | tf_op jit(solution)/shard_map/reduce_scatter | solution.py:12
  11.7 138.0 %reduce-scatter.11.cloned.1.call-start = ((), (), s32[]{:S(2)}) async-start(), calls=%async_computation.10 | async-start | bytes 1114112 | tf_op jit(solution)/shard_map/reduce_scatter | solution.py:13
  12.4 210.3 %reduce-scatter.15.cloned.1.call-start = ((), (), s32[]{:S(2)}) async-start(), calls=%async_computation.14 | async-start | bytes 1114112 | tf_op jit(solution)/shard_map/reduce_scatter | solution.py:14
  13.1 280.3 %all-gather.7.cloned.1.call-start = ((), (), s32[]{:S(2)}) async-start(), calls=%async_computation.7 | async-start | bytes 1114112 | tf_op jit(solution)/shard_map/all_gather | solution.py:21
  77.8 287.2 %all-gather.11.cloned.1.call-start = ((), (), s32[]{:S(2)}) async-start(), calls=%async_computation.11 | async-start | bytes 1114112 | tf_op jit(solution)/shard_map/all_gather | solution.py:21
  151.1 285.5 %all-gather.15.cloned.1.call-start = ((), (), s32[]{:S(2)}) async-start(), calls=%async_computation.15 | async-start | bytes 1114112 | tf_op jit(solution)/shard_map/all_gather | solution.py:21
  224.2 300.1 %reduce-scatter.9.cloned.1.call-start = ((), (), s32[]{:S(2)}) async-start(), calls=%async_computation.8 | async-start | bytes 1114112 | tf_op jit(solution)/shard_map/reduce_scatter | solution.py:25
  293.4 308.6 %reduce-scatter.13.cloned.1.call-start = ((), (), s32[]{:S(2)}) async-start(), calls=%async_computation.12 | async-start | bytes 1114112 | tf_op jit(solution)/shard_map/reduce_scatter | solution.py:25
  365.0 315.2 %reduce-scatter.17.cloned.1.call-start = ((), (), s32[]{:S(2)}) async-start(), calls=%async_computation.16 | async-start | bytes 1114112 | tf_op jit(solution)/shard_map/reduce_scatter | solution.py:25
  436.6 295.8 %all-gather.9.cloned.1.call-start = ((), (), s32[]{:S(2)}) async-start(), calls=%async_computation.9 | async-start | bytes 1114112 | tf_op jit(solution)/shard_map/all_gather | solution.py:31
  525.8 257.7 %all-gather.13.cloned.1.call-start = ((), (), s32[]{:S(2)}) async-start(), calls=%async_computation.13 | async-start | bytes 1114112 | tf_op jit(solution)/shard_map/all_gather | solution.py:31
  603.5 230.8 %all-gather.17.cloned.1.call-start = ((), (), s32[]{:S(2)}) async-start(), calls=%async_computation.17 | async-start | bytes 1114112 | tf_op jit(solution)/shard_map/all_gather | solution.py:31
  783.4 53.2 %copy-start = (f32[128,2048]{1,0:T(8,128)S(1)}, f32[128,2048]{1,0:T(8,128)}, u32[]{:S(2)}) copy-start(f32[128,2048]{1,0:T(8,128)} %all-gather.13.cloned.1.call-done) | copy-start | bytes 3145732
  836.6 1.6 copy-start.1
Sparse Core Ops, SparseCore 0:
  11.8 64.4 reduce-scatter.6
  79.5 70.0 reduce-scatter.10
  152.7 69.9 reduce-scatter.14
  225.1 68.2 all-gather.6
  295.7 69.2 all-gather.10
  367.4 69.2 all-gather.14
  441.2 83.0 reduce-scatter.8
  528.3 73.6 reduce-scatter.12
  606.6 73.6 reduce-scatter.16
  683.3 49.1 all-gather.8
  735.6 47.8 all-gather.12
  786.4 47.8 all-gather.16
where the time goes:
time: 846 us
  waiting for transfers between devices  813 us (96%)
  between operations  14.2 us (2%)
  other arithmetic  13.3 us (2%)
    reduce_scatter x3, waiting for transfers between devices, col_reduce(): sums = lax.psum_scatter(arrays, 'col', scatter_dimension=1, tiled=True)  240 us
    all_gather x3, waiting for transfers between devices, row_expand(): return lax.all_gather(arrays, 'row', axis=0, tiled=True)  212 us
    all_gather x3, waiting for transfers between devices, col_expand(): return lax.all_gather(arrays, 'col', axis=1, tiled=True)  153 us
    reduce_scatter x1, waiting for transfers between devices, row_reduce(): lax.psum_scatter(arrays[1], 'row', scatter_dimension=0, tiled=True)  71.8 us
    reduce_scatter x1, waiting for transfers between devices, row_reduce(): lax.psum_scatter(arrays[2], 'row', scatter_dimension=0, tiled=True)  71.5 us
    reduce_scatter x1, waiting for transfers between devices, row_reduce(): lax.psum_scatter(arrays[0], 'row', scatter_dimension=0, tiled=True)  63.1 us
  transfers between devices with their start and end apart: 12, of which 12 were waited for; matrix products, arithmetic and copies ran while one was open for 1% of the time, Pallas kernels for 0%

commit v1 on v0

v1 whole, which is shorter than its diff:
```python
import jax
import jax.numpy as jnp
from jax import lax
from jax.experimental import pallas as pl
from jax.experimental.pallas import tpu as pltpu
from jax.sharding import Mesh, PartitionSpec as P

bias_one = 0.9999734386011124
bias_two = 0.994079470779666

PARTS = (("zh", 2), ("zm", 2), ("zl", 2), ("xl", 2), ("xh", 2), ("y", 4), ("c", 2))
NEAR = ("zl", "xh", "xl", "y")
PEERS = 32
ROWS, D = 128, 2048
HALF = ROWS // 2
WIDE = D // 4
STEPS = 4
STEP_ROWS = HALF // STEPS
STEP_PEERS = PEERS // STEPS


def adam_kernel(half, weights_ref, first_ref, second_ref, grads_ref, out_ref):
    gradient = grads_ref[0, 0]
    old = weights_ref[0, 0]
    first = 0.9 * first_ref[0, 0] + 0.1 * gradient
    second = 0.95 * second_ref[0, 0] + 0.05 * gradient * gradient
    bottom = bias_one * jnp.sqrt(second * (1.0 / bias_two)) + bias_one * 1e-08
    weights = old - 0.003 * (first / bottom + 0.1 * old)
    for k, value in enumerate((weights, first, second)):
        for p in range(STEP_PEERS):
            r, g = p // 4, p % 4
            out_ref[p, :, k * WIDE : (k + 1) * WIDE] = value[8 * r : 8 * r + 8, g * WIDE : (g + 1) * WIDE]


def adam_half(half, weights, first, second, grads):
    block = pl.BlockSpec((1, 1, STEP_ROWS, D), lambda i, half: (0, 0, half[0] * STEPS + i, 0))
    return pl.pallas_call(
        adam_kernel,
        grid_spec=pltpu.PrefetchScalarGridSpec(
            num_scalar_prefetch=1,
            grid=(STEPS,),
            in_specs=[block] * 4,
            out_specs=pl.BlockSpec((STEP_PEERS, 8, 3 * WIDE), lambda i, half: (i, 0, 0)),
        ),
        out_shape=jax.ShapeDtypeStruct((PEERS, 8, 3 * WIDE), jnp.float32),
        cost_estimate=pl.CostEstimate(flops=30 * HALF * D, bytes_accessed=28 * HALF * D, transcendentals=2 * HALF * D),
        name="adam_half",
    )(half, weights, first, second, grads)


def place_kernel(half, data_ref, *refs):
    outs = refs[-3:]
    for k in range(3):
        for p in range(STEP_PEERS):
            r, g = p // 4, p % 4
            outs[k][8 * r : 8 * r + 8, g * WIDE : (g + 1) * WIDE] = data_ref[p, :, k * WIDE : (k + 1) * WIDE]


def place_half(half, data, before=()):
    return pl.pallas_call(
        place_kernel,
        grid_spec=pltpu.PrefetchScalarGridSpec(
            num_scalar_prefetch=1,
            grid=(STEPS,),
            in_specs=[pl.BlockSpec((STEP_PEERS, 8, 3 * WIDE), lambda i, half: (i, 0, 0))]
            + [pl.BlockSpec(memory_space=pl.ANY)] * len(before),
            out_specs=[pl.BlockSpec((STEP_ROWS, D), lambda i, half: (half[0] * STEPS + i, 0))] * 3,
        ),
        out_shape=[jax.ShapeDtypeStruct((ROWS, D), jnp.float32)] * 3,
        input_output_aliases={2 + k: k for k in range(len(before))},
        cost_estimate=pl.CostEstimate(flops=0, bytes_accessed=24 * HALF * D, transcendentals=0),
        name="place_half",
    )(half, data, *before)


def across_cores(x):
    return lax.ppermute(x, "c", [(0, 1), (1, 0)])


FAR = "ppermute3"


def far_sum(x):
    if FAR == "ppermute2":
        x = x + lax.ppermute(x, "zm", [(0, 1), (1, 0)])
        return x + lax.ppermute(x, "zh", [(0, 1), (1, 0)])
    if FAR == "ppermute3":
        axes = ("zh", "zm")
        other = [lax.ppermute(x, axes, [(i, (i + d) % 4) for i in range(4)]) for d in (1, 3, 2)]
        return (x + other[2]) + (other[0] + other[1])
    y = lax.all_to_all(jnp.broadcast_to(x[None], (4,) + x.shape), ("zh", "zm"), 0, 0, tiled=True)
    return (y[0] + y[1]) + (y[2] + y[3])


def on_device(*arrays):
    core = lax.axis_index("c").astype(jnp.int32).reshape(1)
    theirs = adam_half(1 - core, *arrays)
    received = across_cores(theirs)
    mine = adam_half(core, *arrays)
    mine = mine + received
    pieces = lax.all_to_all(mine, NEAR, 0, 0, tiled=True)
    piece = far_sum(jnp.sum(pieces, axis=0)) * (1.0 / 256.0)
    mine = lax.all_to_all(jnp.broadcast_to(piece[None], (PEERS,) + piece.shape), NEAR, 0, 0, tiled=True)
    theirs = across_cores(mine)
    outs = place_half(core, mine)
    return tuple(place_half(1 - core, theirs, outs))


def solution(mesh):
    names, sizes = zip(*PARTS)
    parts = Mesh(mesh.devices.reshape(sizes), names)
    spec = P(("zh", "zm", "zl", "xl"), ("xh", "y", "c"), None, None)
    return jax.shard_map(on_device, mesh=parts, in_specs=(spec,) * 4, out_specs=(P(),) * 3, check_vma=False)
```

time: 846 us -> 91.1 us (0.11)
  waiting for transfers between devices: 813 us -> 3.63 us
  blocking collectives: 0 us -> 52.8 us
  starting transfers between devices: 0.48 us -> 15.6 us
  Pallas kernels: 0 us -> 14.9 us
  between operations: 14.2 us -> 0.66 us
  other arithmetic: 13.3 us -> 1.7 us
    reduce_scatter x6 -> x0, waiting for transfers between devices: 447 us -> none  [the longest x3 240 us: col_reduce(): sums = lax.psum_scatter(arrays, 'col', scatter_dimension=1, tiled=True)]
    all_gather x6 -> x0, waiting for transfers between devices: 365 us -> none  [the longest x3 212 us: row_expand(): return lax.all_gather(arrays, 'row', axis=0, tiled=True)]
    all_to_all x0 -> x2, blocking collectives: none -> 52.8 us  [the longest x1 28.2 us: on_device(): pieces = lax.all_to_all(mine, NEAR, 0, 0, tiled=True)]
    ppermute x0 -> x5, starting transfers between devices: none -> 15.6 us  [the longest x3 8.45 us: far_sum(): lax.ppermute(x, axes, [(i, (i + d) % 4) for i in range(4)])]
    pallas_call x0 -> x4, Pallas kernels: none -> 14.9 us  [the longest x2 7.84 us: adam_half(): pl.pallas_call(adam_kernel, grid_spec=pltpu.PrefetchScalarGridSpec(num_sc...]
    mul x6 -> x1, other arithmetic: 8.84 us -> 0.01 us  [on_device(): piece = far_sum(jnp.sum(pieces, axis=0)) * (1.0 / 256.0)]
  transfers between devices with their start and end apart: 12 -> 5, of which waited for: 12 -> 2; matrix products, arithmetic and copies ran while one was open for 1% -> 0% of each run, Pallas kernels for 0% -> 8%
where the time goes in v1:
time: 91.1 us; the launch traced here: 90.7 us
  blocking collectives  52.8 us (58%)
  starting transfers between devices  15.6 us (17%)
  Pallas kernels  14.9 us (16%)
  waiting for transfers between devices  3.63 us (4%)
  other arithmetic  1.7 us (2%)
  local copies, waits for them, and re-layouts  1.33 us (1%)
    all_to_all x1, blocking collectives, on_device(): pieces = lax.all_to_all(mine, NEAR, 0, 0, tiled=True)  28.2 us
    all_to_all x1, blocking collectives, on_device(): lax.all_to_all(jnp.broadcast_to(piece[None], (PEERS,) + piece.shape), NEA...  24.6 us
    ppermute x3, starting transfers between devices, far_sum(): lax.ppermute(x, axes, [(i, (i + d) % 4) for i in range(4)])  8.45 us
    pallas_call x2, Pallas kernels, adam_half(): pl.pallas_call(adam_kernel, grid_spec=pltpu.PrefetchScalarGridSpec(num_sc...  7.84 us
    ppermute x2, starting transfers between devices, across_cores(): return lax.ppermute(x, 'c', [(0, 1), (1, 0)])  7.18 us
    pallas_call x2, Pallas kernels, place_half(): pl.pallas_call(place_kernel, grid_spec=pltpu.PrefetchScalarGridSpec(num_s...  7.11 us
    ppermute x3, waiting for transfers between devices, far_sum(): lax.ppermute(x, axes, [(i, (i + d) % 4) for i in range(4)])  3.62 us
  transfers between devices with their start and end apart: 5, of which 2 were waited for; matrix products, arithmetic and copies ran while one was open for 0% of the time, Pallas kernels for 8%

profile of v1, /device:TPU:1, one launch (start us, length us, event | category | flops | bytes accessed | tf_op | source)
XLA Modules:
  0.0 90.7 jit_solution(3527694142308993969)
XLA Ops:
  0.6 3.9 %adam_half.3 = f32[32,8,1536]{2,1,0:T(8,128)} custom-call(s32[1]{0:T(128)S(6)} %sub.4.half, f32[1,1,128,2048]{3,2,1,0:T(8,128)} %weights_ref.3, f32[1,1,128,2048]{3,2,1,0:T(8,128)} %first_ref.3, f32[1,1,128,2048]{3,2,1,0:T(8,128)} %second_ref.3, f32[1,1,128,2048]{3,2,1,0:T(8,128)} %grads_ref.3), custom_call_target="tpu_custom_call" | custom-call | flops 3932160 | bytes 3670016 | tf_op jit(solution)/shard_map/adam_half/pallas_call | solution.py:37
  4.6 3.2 %collective-permute-start = (f32[32,8,1536]{2,1,0:T(8,128)}, f32[32,8,1536]{2,1,0:T(8,128)S(1)}, u32[]{:S(2)}, u32[]{:S(2)}) collective-permute-start(f32[32,8,1536]{2,1,0:T(8,128)} %adam_half.3), channel_id=1, source_target_pairs={{0,1},{1,0},{2,3},{3,2},{4,5},{5,4},{6,7},{7,6},{8,9},{9,8},{10,11... | collective-permute-start | bytes 4718600 | tf_op jit(solution)/shard_map/ppermute | solution.py:77
  7.8 3.9 %adam_half.2 = f32[32,8,1536]{2,1,0:T(8,128)} custom-call(s32[1]{0:T(128)} %bitcast.half, f32[1,1,128,2048]{3,2,1,0:T(8,128)} %weights_ref.3, f32[1,1,128,2048]{3,2,1,0:T(8,128)} %first_ref.3, f32[1,1,128,2048]{3,2,1,0:T(8,128)} %second_ref.3, f32[1,1,128,2048]{3,2,1,0:T(8,128)} %grads_ref.3), custom_call_target="tpu_custom_call" | custom-call | flops 3932160 | bytes 3670016 | tf_op jit(solution)/shard_map/adam_half/pallas_call | solution.py:37
  11.7 0.0 collective-permute-done
  11.7 1.6 %add.12 = f32[32,8,1536]{2,1,0:T(8,128)S(1)} add(f32[32,8,1536]{2,1,0:T(8,128)} %adam_half.2, f32[32,8,1536]{2,1,0:T(8,128)S(1)} %collective-permute-done) | non-fusion elementwise | flops 393216 | bytes 4718592 | tf_op jit(solution)/shard_map/add | solution.py:100
  13.3 28.2 %all_to_all.10 = f32[32,8,1536]{2,1,0:T(8,128)S(1)} all-to-all(f32[32,8,1536]{2,1,0:T(8,128)S(1)} %add.12), channel_id=1, replica_groups=mesh['zh'=2,'zm'=2,'zl'=2,'xl'=2,'xh'=2,'y'=4,'c'=2] {'zl','xh','xl','y'}, dimensions={0} | all-to-all | bytes 3145728 | tf_op jit(solution)/shard_map/all_to_all | solution.py:101
  41.5 0.1 reduce_sum.9
  41.6 5.2 %collective-permute-start.3 = (f32[8,1536]{1,0:T(8,128)S(1)}, f32[8,1536]{1,0:T(8,128)S(1)}, u32[]{:S(2)}, u32[]{:S(2)}) collective-permute-start(f32[8,1536]{1,0:T(8,128)S(1)} %reduce_sum.9), channel_id=1, source_target_pairs={{0,192},{64,0},{128,64},{192,128},{1,193},{65,1},{129,65},{193,129... | collective-permute-start | bytes 147464 | tf_op jit(solution)/shard_map/ppermute | solution.py:89
  46.8 0.0 collective-permute-start.2
  46.8 3.3 %collective-permute-start.1 = (f32[8,1536]{1,0:T(8,128)S(1)}, f32[8,1536]{1,0:T(8,128)S(1)}, u32[]{:S(2)}, u32[]{:S(2)}) collective-permute-start(f32[8,1536]{1,0:T(8,128)S(1)} %reduce_sum.9), channel_id=1, source_target_pairs={{0,128},{64,192},{128,0},{192,64},{1,129},{65,193},{129,1},{193,65... | collective-permute-start | bytes 147464 | tf_op jit(solution)/shard_map/ppermute | solution.py:89
  50.0 0.0 collective-permute-done.3
  50.0 2.0 %collective-permute-done.2 = f32[8,1536]{1,0:T(8,128)S(1)} collective-permute-done((f32[8,1536]{1,0:T(8,128)S(1)}, f32[8,1536]{1,0:T(8,128)S(1)}, u32[]{:S(2)}, u32[]{:S(2)}) %collective-permute-start.2) | collective-permute-done | bytes 49184 | tf_op jit(solution)/shard_map/ppermute | solution.py:89
  52.0 1.6 %collective-permute-done.1 = f32[8,1536]{1,0:T(8,128)S(1)} collective-permute-done((f32[8,1536]{1,0:T(8,128)S(1)}, f32[8,1536]{1,0:T(8,128)S(1)}, u32[]{:S(2)}, u32[]{:S(2)}) %collective-permute-start.1) | collective-permute-done | bytes 49184 | tf_op jit(solution)/shard_map/ppermute | solution.py:89
  53.7 0.2 broadcast_in_dim.2
  53.8 24.6 %all_to_all.11.data_ref = f32[32,8,1536]{2,1,0:T(8,128)S(1)} all-to-all(f32[32,8,1536]{2,1,0:T(8,128)S(1)} %broadcast_in_dim.2), channel_id=1, replica_groups=mesh['zh'=2,'zm'=2,'zl'=2,'xl'=2,'xh'=2,'y'=4,'c'=2] {'zl','xh','xl','y'}, dimensions={0} | all-to-all | bytes 3145728 | tf_op jit(solution)/shard_map/all_to_all | solution.py:103
  78.4 0.0 copy-start
  78.4 3.9 %collective-permute-start.4 = (f32[32,8,1536]{2,1,0:T(8,128)S(1)}, f32[32,8,1536]{2,1,0:T(8,128)S(1)}, u32[]{:S(2)}, u32[]{:S(2)}) collective-permute-start(f32[32,8,1536]{2,1,0:T(8,128)S(1)} %all_to_all.11.data_ref), channel_id=1, source_target_pairs={{0,1},{1,0},{2,3},{3,2},{4,5},{5,4},{6,7},{7,6},{8,9},{9,8},{10,11... | collective-permute-start | bytes 4718600 | tf_op jit(solution)/shard_map/ppermute | solution.py:77
  82.4 0.0 copy-done
  82.4 3.6 %place_half.2 = (f32[128,2048]{1,0:T(8,128)}, f32[128,2048]{1,0:T(8,128)}, f32[128,2048]{1,0:T(8,128)}) custom-call(s32[1]{0:T(128)} %bitcast.half, f32[32,8,1536]{2,1,0:T(8,128)} %copy-done), custom_call_target="tpu_custom_call" | custom-call | bytes 3145728 | tf_op jit(solution)/shard_map/place_half/pallas_call | solution.py:60
  85.9 0.0 collective-permute-done.4.data_ref
  85.9 0.0 copy-start.1
  85.9 1.2 %copy-done.1 = f32[32,8,1536]{2,1,0:T(8,128)} copy-done((f32[32,8,1536]{2,1,0:T(8,128)}, f32[32,8,1536]{2,1,0:T(8,128)S(1)}, u32[]{:S(2)}) %copy-start.1) | copy-done | bytes 1572888
  87.1 3.6 %place_half.3 = (f32[128,2048]{1,0:T(8,128)}, f32[128,2048]{1,0:T(8,128)}, f32[128,2048]{1,0:T(8,128)}) custom-call(s32[1]{0:T(128)S(6)} %sub.4.half, f32[32,8,1536]{2,1,0:T(8,128)} %copy-done.1, f32[128,2048]{1,0:T(8,128)} %get-tuple-element.6.refs_0_, ...), custom_call_target="tpu_custom_call", output_to_operand_aliasing={{0}: (2, {}), {1}: (3, {}), {2}: (4, {})} | custom-call | bytes 3145728 | tf_op jit(solution)/shard_map/place_half/pallas_call | solution.py:60
  (1 shorter events, 0.0 us)
Async XLA Ops:
  4.6 7.1 %collective-permute-start = (f32[32,8,1536]{2,1,0:T(8,128)}, f32[32,8,1536]{2,1,0:T(8,128)S(1)}, u32[]{:S(2)}, u32[]{:S(2)}) collective-permute-start(f32[32,8,1536]{2,1,0:T(8,128)} %adam_half.3), channel_id=1, source_target_pairs={{0,1},{1,0},{2,3},{3,2},{4,5},{5,4},{6,7},{7,6},{8,9},{9,8},{10,11... | collective-permute-start | bytes 4718600 | tf_op jit(solution)/shard_map/ppermute | solution.py:77
  41.6 8.5 %collective-permute-start.3 = (f32[8,1536]{1,0:T(8,128)S(1)}, f32[8,1536]{1,0:T(8,128)S(1)}, u32[]{:S(2)}, u32[]{:S(2)}) collective-permute-start(f32[8,1536]{1,0:T(8,128)S(1)} %reduce_sum.9), channel_id=1, source_target_pairs={{0,192},{64,0},{128,64},{192,128},{1,193},{65,1},{129,65},{193,129... | collective-permute-start | bytes 147464 | tf_op jit(solution)/shard_map/ppermute | solution.py:89
  46.8 5.3 %collective-permute-start.2 = (f32[8,1536]{1,0:T(8,128)S(1)}, f32[8,1536]{1,0:T(8,128)S(1)}, u32[]{:S(2)}, u32[]{:S(2)}) collective-permute-start(f32[8,1536]{1,0:T(8,128)S(1)} %reduce_sum.9), channel_id=1, source_target_pairs={{0,64},{64,128},{128,192},{192,0},{1,65},{65,129},{129,193},{193,1... | collective-permute-start | bytes 147464 | tf_op jit(solution)/shard_map/ppermute | solution.py:89
  46.8 6.9 %collective-permute-start.1 = (f32[8,1536]{1,0:T(8,128)S(1)}, f32[8,1536]{1,0:T(8,128)S(1)}, u32[]{:S(2)}, u32[]{:S(2)}) collective-permute-start(f32[8,1536]{1,0:T(8,128)S(1)} %reduce_sum.9), channel_id=1, source_target_pairs={{0,128},{64,192},{128,0},{192,64},{1,129},{65,193},{129,1},{193,65... | collective-permute-start | bytes 147464 | tf_op jit(solution)/shard_map/ppermute | solution.py:89
  78.4 3.9 %copy-start = (f32[32,8,1536]{2,1,0:T(8,128)}, f32[32,8,1536]{2,1,0:T(8,128)S(1)}, u32[]{:S(2)}) copy-start(f32[32,8,1536]{2,1,0:T(8,128)S(1)} %all_to_all.11.data_ref) | copy-start | bytes 4718596
  78.4 7.5 %collective-permute-start.4 = (f32[32,8,1536]{2,1,0:T(8,128)S(1)}, f32[32,8,1536]{2,1,0:T(8,128)S(1)}, u32[]{:S(2)}, u32[]{:S(2)}) collective-permute-start(f32[32,8,1536]{2,1,0:T(8,128)S(1)} %all_to_all.11.data_ref), channel_id=1, source_target_pairs={{0,1},{1,0},{2,3},{3,2},{4,5},{5,4},{6,7},{7,6},{8,9},{9,8},{10,11... | collective-permute-start | bytes 4718600 | tf_op jit(solution)/shard_map/ppermute | solution.py:77
  85.9 1.2 %copy-start.1 = (f32[32,8,1536]{2,1,0:T(8,128)}, f32[32,8,1536]{2,1,0:T(8,128)S(1)}, u32[]{:S(2)}) copy-start(f32[32,8,1536]{2,1,0:T(8,128)S(1)} %collective-permute-done.4.data_ref) | copy-start | bytes 4718596

commit v2 on v0

v2 whole, which is shorter than its diff:
```python
import jax
import jax.numpy as jnp
from jax import lax
from jax.experimental import pallas as pl
from jax.experimental.pallas import tpu as pltpu
from jax.sharding import PartitionSpec as P

bias_one = 0.9999734386011124
bias_two = 0.994079470779666

AXES = ("row", "col")
SHIFT = (0, 0)


def device(x, y, z, core):
    return (z % 8 * 2 + x % 2) * 16 + x // 2 * 8 + y * 2 + core


def place(core, along, pair, across, far):
    x, y = (along, across) if core == 0 else (across, along)
    return device(x, y, 2 * far + pair + SHIFT[core], core)


def ring(change):
    return [
        (place(core, along, pair, across, far), place(core, (along + change) % 4, pair, across, far))
        for core in range(2) for along in range(4) for pair in range(2) for across in range(4) for far in range(4)
    ]


SECOND = [
    [place(core, along, pair, across, far) for across in range(4) for pair in range(2)]
    for core in range(2) for along in range(4) for far in range(4)
]


def far_pairs(change):
    return [
        (device(x, y, 2 * far + pair + SHIFT[core], core), device(x, y, 2 * change(far) + pair + SHIFT[core], core))
        for core in range(2) for far in range(4) for pair in range(2) for x in range(4) for y in range(4)
    ]


PEERS = 32
ROWS, D = 128, 2048
HALF = ROWS // 2
WIDE = D // 4
STEPS = 4
ROOM_A = 60 << 20
ROOM_B = 8 << 20
VMEM = 8 << 20
STEP_ROWS = HALF // STEPS
STEP_PEERS = PEERS // STEPS


def place_kernel(rows, *refs):
    outs, sems = refs[-4:-1], refs[-1]
    copies = [
        pltpu.make_async_copy(
            refs[i].at[:, g, :, pl.ds(k * WIDE, WIDE)],
            outs[k].at[pl.ds(rows[i], 2), :, pl.ds(g * WIDE, WIDE)],
            sems.at[i, k, g],
        )
        for i in range(sems.shape[0])
        for k in range(3)
        for g in range(4)
    ]
    for copy in copies:
        copy.start()
    for copy in copies:
        copy.wait()


def place_chunks(rows, chunks, before):
    anywhere = pl.BlockSpec(memory_space=pl.ANY)
    n = len(chunks)
    return pl.pallas_call(
        place_kernel,
        in_specs=[pl.BlockSpec(memory_space=pltpu.SMEM)] + [anywhere] * (n + len(before)),
        out_specs=[anywhere] * 3,
        out_shape=[jax.ShapeDtypeStruct((ROWS // 8, 8, D), jnp.float32)] * 3,
        scratch_shapes=[pltpu.SemaphoreType.DMA((n, 3, 4))],
        input_output_aliases={1 + n + k: k for k in range(len(before))},
        compiler_params=pltpu.CompilerParams(vmem_limit_bytes=8 << 20),
        cost_estimate=pl.CostEstimate(flops=0, bytes_accessed=n * 24 * 16 * D, transcendentals=0),
        name="place_chunks",
    )(jnp.stack(rows).astype(jnp.int32), *(chunk.reshape(2, 4, 8, 3 * WIDE) for chunk in chunks), *before)


def across_cores(x):
    return lax.ppermute(x, AXES, [(i, i ^ 1) for i in range(256)])


def exchange(x, groups):
    return lax.all_to_all(x, AXES, 0, 0, axis_index_groups=groups, tiled=True)


def repeat(x, groups):
    return jnp.broadcast_to(x[None], (len(groups[0]),) + x.shape)


def far_sum(x):
    x = x + lax.ppermute(x, AXES, far_pairs(lambda far: far ^ 1))
    return x + lax.ppermute(x, AXES, far_pairs(lambda far: far ^ 3))


def adam(half, arrays):
    old, first, second, gradient = (lax.dynamic_slice_in_dim(x[0, 0], half * HALF, HALF, 0) for x in arrays)
    first = 0.9 * first + 0.1 * gradient
    second = 0.95 * second + 0.05 * gradient * gradient
    bottom = bias_one * jnp.sqrt(second * (1.0 / bias_two)) + bias_one * 1e-08
    return old - 0.003 * (first / bottom + 0.1 * old), first, second


def join_kernel(at, *refs):
    for d in range(4):

        @pl.when(pl.program_id(0) == d)
        def _():
            for k in range(3):
                for p in range(8):
                    part = (slice(8 * (p // 4), 8 * (p // 4) + 8), slice(p % 4 * WIDE, (p % 4 + 1) * WIDE))
                    refs[6 + d][p, :, k * WIDE : (k + 1) * WIDE] = refs[k][part] + refs[3 + k][part]


def join(at, mine, theirs):
    return pl.pallas_call(
        join_kernel,
        grid_spec=pltpu.PrefetchScalarGridSpec(
            num_scalar_prefetch=1,
            grid=(4,),
            in_specs=[pl.BlockSpec((16, D), lambda i, at: (lax.rem(at[0] + i, 4), 0))] * 6,
            out_specs=[pl.BlockSpec((8, 8, 3 * WIDE), lambda i, at: (0, 0, 0))] * 4,
        ),
        out_shape=[jax.ShapeDtypeStruct((8, 8, 3 * WIDE), jnp.float32)] * 4,
        compiler_params=pltpu.CompilerParams(vmem_limit_bytes=16 << 20),
        cost_estimate=pl.CostEstimate(flops=3 * HALF * D, bytes_accessed=36 * HALF * D, transcendentals=0),
        name="join",
    )(at, *mine, *theirs)


def on_device(*arrays):
    row, col = lax.axis_index("row").astype(jnp.int32), lax.axis_index("col").astype(jnp.int32)
    core = lax.rem(col, 2)
    x, y = col // 8 * 2 + lax.rem(row, 2), lax.rem(col // 2, 4)
    mine_at, their_at = jnp.where(core == 0, x, y), jnp.where(core == 0, y, x)
    sent = adam(1 - core, arrays)
    theirs = [across_cores(a) for a in sent]
    arrays, _ = lax.optimization_barrier((arrays, sent))
    chunks = join(mine_at.reshape(1), adam(core, arrays), theirs)
    other = [lax.ppermute(chunks[d], AXES, ring(d)) for d in (1, 2, 3)]
    mine = (chunks[0] + other[1]) + (other[0] + other[2])
    mine = jnp.sum(exchange(mine, SECOND), axis=0)
    mine = far_sum(mine) * (1.0 / 256.0)
    mine = exchange(repeat(mine, SECOND), SECOND)
    chunks = [mine] + [lax.ppermute(mine, AXES, ring(d)) for d in (1, 2, 3)]
    rows = [core * 8 + lax.rem(mine_at + 4 - d, 4) * 2 for d in range(4)]
    their_rows = [(1 - core) * 8 + lax.rem(their_at + 4 - d, 4) * 2 for d in range(4)]
    theirs, outs = [across_cores(chunks[0])], ()
    for d in range(1, 4):
        ready = [(rows[d - 1], chunks[d - 1])] + [(their_rows[d - 2], theirs[d - 2])] * (d >= 2)
        outs = place_chunks(*zip(*ready), outs)
        chunk, outs = lax.optimization_barrier((chunks[d], outs))
        theirs.append(across_cores(chunk))
        chunks[d] = chunk
    outs = place_chunks((rows[3], their_rows[2]), (chunks[3], theirs[2]), outs)
    outs = place_chunks((their_rows[3],), (theirs[3],), outs)
    return tuple(out.reshape(ROWS, D) for out in outs)


def solution(mesh):
    spec = P("row", "col", None, None)
    return jax.shard_map(on_device, mesh=mesh, in_specs=(spec,) * 4, out_specs=(P(),) * 3, check_vma=False)
```

time: 846 us -> 79.4 us (0.09)
  waiting for transfers between devices: 813 us -> 13.6 us
  starting transfers between devices: 0.48 us -> 32.4 us
  blocking collectives: 0 us -> 20.6 us
  between operations: 14.2 us -> 0.74 us
    reduce_scatter x6 -> x0, waiting for transfers between devices: 447 us -> none  [the longest x3 240 us: col_reduce(): sums = lax.psum_scatter(arrays, 'col', scatter_dimension=1, tiled=True)]
    all_gather x6 -> x0, waiting for transfers between devices: 365 us -> none  [the longest x3 212 us: row_expand(): return lax.all_gather(arrays, 'row', axis=0, tiled=True)]
    ppermute x0 -> x15, starting transfers between devices: none -> 32.4 us  [the longest x7 19 us: across_cores(): return lax.ppermute(x, AXES, [(i, i ^ 1) for i in range(256)])]
    all_to_all x0 -> x2, blocking collectives: none -> 20.6 us  [exchange(): return lax.all_to_all(x, AXES, 0, 0, axis_index_groups=groups, tiled=True)]
    ppermute x0 -> x15, waiting for transfers between devices: none -> 13.6 us  [the longest x3 8.79 us: on_device(): other = [lax.ppermute(chunks[d], AXES, ring(d)) for d in (1, 2, 3)]]
    mul x6 -> x1, other arithmetic: 8.84 us -> 0.01 us  [on_device(): mine = far_sum(mine) * (1.0 / 256.0)]
  transfers between devices with their start and end apart: 12 -> 15, of which waited for: 12 -> 7; matrix products, arithmetic and copies ran while one was open for 1% -> 3% of each run, Pallas kernels for 0% -> 7%
where the time goes in v2:
time: 79.4 us; the launch traced here: 79.2 us
  starting transfers between devices  32.4 us (41%)
  blocking collectives  20.6 us (26%)
  waiting for transfers between devices  13.6 us (17%)
  Pallas kernels  6.79 us (9%)
  other arithmetic  5.08 us (6%)
    all_to_all x2, blocking collectives, exchange(): return lax.all_to_all(x, AXES, 0, 0, axis_index_groups=groups, tiled=True)  20.6 us
    ppermute x7, starting transfers between devices, across_cores(): return lax.ppermute(x, AXES, [(i, i ^ 1) for i in range(256)])  19 us
    ppermute x3, waiting for transfers between devices, on_device(): other = [lax.ppermute(chunks[d], AXES, ring(d)) for d in (1, 2, 3)]  8.79 us
    pallas_call x5, Pallas kernels, place_chunks(): pl.pallas_call(place_kernel, in_specs=[pl.BlockSpec(memory_space=pltpu.SM...  6.52 us
    sub x2, other arithmetic, adam(): return (old - 0.003 * (first / bottom + 0.1 * old), first, second)  4.74 us
    ppermute x1, starting transfers between devices, far_sum(): return x + lax.ppermute(x, AXES, far_pairs(lambda far: far ^ 3))  4.59 us
    ppermute x3, starting transfers between devices, on_device(): other = [lax.ppermute(chunks[d], AXES, ring(d)) for d in (1, 2, 3)]  3.94 us
    ppermute x1, starting transfers between devices, far_sum(): x = x + lax.ppermute(x, AXES, far_pairs(lambda far: far ^ 1))  3.08 us
  transfers between devices with their start and end apart: 15, of which 7 were waited for; matrix products, arithmetic and copies ran while one was open for 3% of the time, Pallas kernels for 7%

profile of v2, /device:TPU:1, one launch (start us, length us, event | category | flops | bytes accessed | tf_op | source)
XLA Modules:
  0.0 79.2 jit_solution(7781443348054904793)
XLA Ops:
  0.6 0.0 copy-start
  0.6 3.0 %bitcast_subtract_fusion.1 = (f32[64,2048]{1,0:T(8,128)}, f32[64,2048]{1,0:T(8,128)S(1)}, f32[64,2048]{1,0:T(8,128)}) fusion(f32[1,1,128,2048]{3,2,1,0:T(8,128)} %param.4, s32[]{:T(128)S(6)} %select_n.30, f32[1,1,128,2048]{3,2,1,0:T(8,128)} %param.7, f32[1,1,128,2048]{3,2,1,0:T(8,128)} %param.6, f32[1,1,128,2048]{3,2,1,0:T(8,128)} %param.5), kind=kLoop, calls=%fused_computation.12 | loop fusion | flops 1966080 | bytes 3670020 | tf_op jit(solution)/shard_map/sub | solution.py:112
  3.6 3.2 %collective-permute-start = (f32[64,2048]{1,0:T(8,128)}, f32[64,2048]{1,0:T(8,128)S(1)}, u32[]{:S(2)}, u32[]{:S(2)}) collective-permute-start(f32[64,2048]{1,0:T(8,128)} %get-tuple-element.76), channel_id=1, source_target_pairs={{0,1},{1,0},{2,3},{3,2},{4,5},{5,4},{6,7},{7,6},{8,9},{9,8},{10,11... | collective-permute-start | bytes 1572872 | tf_op jit(solution)/shard_map/ppermute | solution.py:91
  6.9 0.0 collective-permute-start.1
  6.9 0.5 collective-permute-start.2
  7.4 0.0 copy-done
  7.4 1.8 %bitcast_subtract_fusion = (f32[64,2048]{1,0:T(8,128)S(1)}, f32[64,2048]{1,0:T(8,128)S(1)}, f32[64,2048]{1,0:T(8,128)S(1)}) fusion(f32[1,1,128,2048]{3,2,1,0:T(8,128)S(1)} %copy-done, s32[]{:T(128)S(6)} %select_n.31, f32[1,1,128,2048]{3,2,1,0:T(8,128)} %param.7, f32[1,1,128,2048]{3,2,1,0:T(8,128)} %param.6, f32[1,1,128,2048]{3,2,1,0:T(8,128)} %param.5), kind=kLoop, calls=%fused_computation.6 | loop fusion | flops 1966080 | bytes 3670020 | tf_op jit(solution)/shard_map/sub | solution.py:112
  9.1 0.0 collective-permute-done.refs_3_
  9.2 1.0 %collective-permute-done.1.refs_4_ = f32[64,2048]{1,0:T(8,128)S(1)} collective-permute-done((f32[64,2048]{1,0:T(8,128)}, f32[64,2048]{1,0:T(8,128)S(1)}, u32[]{:S(2)}, u32[]{:S(2)}) %collective-permute-start.1) | collective-permute-done | bytes 524320 | tf_op jit(solution)/shard_map/ppermute | solution.py:91
  10.1 0.0 collective-permute-done.2.refs_5_
  10.1 0.3 join.1
  10.4 1.3 %collective-permute-start.3 = (f32[8,8,1536]{2,1,0:T(8,128)S(1)}, f32[8,8,1536]{2,1,0:T(8,128)S(1)}, u32[]{:S(2)}, u32[]{:S(2)}) collective-permute-start(f32[8,8,1536]{2,1,0:T(8,128)S(1)} %get-tuple-element.43), channel_id=1, source_target_pairs={{0,8},{64,72},{128,136},{192,200},{2,10},{66,74},{130,138},{194,20... | collective-permute-start | bytes 1179656 | tf_op jit(solution)/shard_map/ppermute | solution.py:151
  11.6 0.4 collective-permute-start.4
  12.0 2.3 %collective-permute-start.5 = (f32[8,8,1536]{2,1,0:T(8,128)S(1)}, f32[8,8,1536]{2,1,0:T(8,128)S(1)}, u32[]{:S(2)}, u32[]{:S(2)}) collective-permute-start(f32[8,8,1536]{2,1,0:T(8,128)S(1)} %get-tuple-element.45), channel_id=1, source_target_pairs={{0,24},{64,88},{128,152},{192,216},{2,26},{66,90},{130,154},{194,2... | collective-permute-start | bytes 1179656 | tf_op jit(solution)/shard_map/ppermute | solution.py:151
  14.3 4.6 %collective-permute-done.3 = f32[8,8,1536]{2,1,0:T(8,128)S(1)} collective-permute-done((f32[8,8,1536]{2,1,0:T(8,128)S(1)}, f32[8,8,1536]{2,1,0:T(8,128)S(1)}, u32[]{:S(2)}, u32[]{:S(2)}) %collective-permute-start.3) | collective-permute-done | bytes 393248 | tf_op jit(solution)/shard_map/ppermute | solution.py:151
  18.9 4.2 %collective-permute-done.4 = f32[8,8,1536]{2,1,0:T(8,128)S(1)} collective-permute-done((f32[8,8,1536]{2,1,0:T(8,128)S(1)}, f32[8,8,1536]{2,1,0:T(8,128)S(1)}, u32[]{:S(2)}, u32[]{:S(2)}) %collective-permute-start.4) | collective-permute-done | bytes 393248 | tf_op jit(solution)/shard_map/ppermute | solution.py:151
  23.1 0.0 collective-permute-done.5
  23.1 0.1 add_add_fusion
  23.2 10.8 %all_to_all.10 = f32[8,8,1536]{2,1,0:T(8,128)S(1)} all-to-all(f32[8,8,1536]{2,1,0:T(8,128)S(1)} %add_add_fusion), channel_id=1, replica_groups={{0,32,2,34,4,36,6,38},{64,96,66,98,68,100,70,102},{128,160,130,162,132,..., dimensions={0} | all-to-all | bytes 786432 | tf_op jit(solution)/shard_map/all_to_all | solution.py:95
  34.0 3.1 %collective-permute-start.6 = (f32[8,1536]{1,0:T(8,128)S(1)}, f32[8,1536]{1,0:T(8,128)S(1)}, u32[]{:S(2)}, u32[]{:S(2)}) collective-permute-start(f32[8,1536]{1,0:T(8,128)S(1)} %reduce_sum.9), channel_id=1, source_target_pairs={{0,64},{2,66},{4,68},{6,70},{16,80},{18,82},{20,84},{22,86},{8,72}... | collective-permute-start | bytes 147464 | tf_op jit(solution)/shard_map/ppermute | solution.py:103
  37.1 1.5 %collective-permute-done.6 = f32[8,1536]{1,0:T(8,128)S(1)} collective-permute-done((f32[8,1536]{1,0:T(8,128)S(1)}, f32[8,1536]{1,0:T(8,128)S(1)}, u32[]{:S(2)}, u32[]{:S(2)}) %collective-permute-start.6) | collective-permute-done | bytes 49184 | tf_op jit(solution)/shard_map/ppermute | solution.py:103
  38.6 4.6 %collective-permute-start.7 = (f32[8,1536]{1,0:T(8,128)S(1)}, f32[8,1536]{1,0:T(8,128)S(1)}, u32[]{:S(2)}, u32[]{:S(2)}) collective-permute-start(f32[8,1536]{1,0:T(8,128)S(1)} %add.125), channel_id=1, source_target_pairs={{0,192},{2,194},{4,196},{6,198},{16,208},{18,210},{20,212},{22,214... | collective-permute-start | bytes 147464 | tf_op jit(solution)/shard_map/ppermute | solution.py:104
  43.2 2.0 %collective-permute-done.7 = f32[8,1536]{1,0:T(8,128)S(1)} collective-permute-done((f32[8,1536]{1,0:T(8,128)S(1)}, f32[8,1536]{1,0:T(8,128)S(1)}, u32[]{:S(2)}, u32[]{:S(2)}) %collective-permute-start.7) | collective-permute-done | bytes 49184 | tf_op jit(solution)/shard_map/ppermute | solution.py:104
  45.2 9.8 %all_to_all.11 = f32[8,8,1536]{2,1,0:T(8,128)S(1)} all-to-all(f32[8,8,1536]{2,1,0:T(8,128)S(1)} %broadcast_in_dim.2), channel_id=1, replica_groups={{0,32,2,34,4,36,6,38},{64,96,66,98,68,100,70,102},{128,160,130,162,132,..., dimensions={0} | all-to-all | bytes 786432 | tf_op jit(solution)/shard_map/all_to_all | solution.py:95
  55.0 0.2 collective-permute-start.10
  55.2 6.1 %collective-permute-start.11 = (f32[8,8,1536]{2,1,0:T(8,128)S(1)}, f32[8,8,1536]{2,1,0:T(8,128)S(1)}, u32[]{:S(2)}, u32[]{:S(2)}) collective-permute-start(f32[8,8,1536]{2,1,0:T(8,128)S(1)} %all_to_all.11), channel_id=1, source_target_pairs={{0,1},{1,0},{2,3},{3,2},{4,5},{5,4},{6,7},{7,6},{8,9},{9,8},{10,11... | collective-permute-start | bytes 1179656 | tf_op jit(solution)/shard_map/ppermute | solution.py:91
  61.3 0.8 %place_chunks.5 = (f32[16,8,2048]{2,1,0:T(8,128)}, f32[16,8,2048]{2,1,0:T(8,128)}, f32[16,8,2048]{2,1,0:T(8,128)}) custom-call(s32[1]{0:T(128)} %bitcast.14.rows, f32[2,4,8,1536]{3,2,1,0:T(8,128)S(1)} %bitcast.64), custom_call_target="tpu_custom_call" | custom-call | bytes 786432 | tf_op jit(solution)/shard_map/place_chunks/pallas_call | solution.py:77
  62.1 1.0 %collective-permute-start.9 = (f32[8,8,1536]{2,1,0:T(8,128)S(1)}, f32[8,8,1536]{2,1,0:T(8,128)S(1)}, u32[]{:S(2)}, u32[]{:S(2)}) collective-permute-start(f32[8,8,1536]{2,1,0:T(8,128)S(1)} %all_to_all.11), channel_id=1, source_target_pairs={{0,8},{64,72},{128,136},{192,200},{2,10},{66,74},{130,138},{194,20... | collective-permute-start | bytes 1179656 | tf_op jit(solution)/shard_map/ppermute | solution.py:156
  63.1 0.1 collective-permute-done.10
  63.2 5.6 %collective-permute-start.12 = (f32[8,8,1536]{2,1,0:T(8,128)S(1)}, f32[8,8,1536]{2,1,0:T(8,128)S(1)}, u32[]{:S(2)}, u32[]{:S(2)}) collective-permute-start(f32[8,8,1536]{2,1,0:T(8,128)S(1)} %collective-permute-done.10), channel_id=1, source_target_pairs={{0,1},{1,0},{2,3},{3,2},{4,5},{5,4},{6,7},{7,6},{8,9},{9,8},{10,11... | collective-permute-start | bytes 1179656 | tf_op jit(solution)/shard_map/ppermute | solution.py:91
  68.8 0.6 collective-permute-start.8
  69.4 0.1 pad_add_fusion.1.rows
  69.5 0.1 pad_add_fusion.rows
  69.6 0.0 collective-permute-done.11
  69.6 1.6 %place_chunks.6 = (f32[16,8,2048]{2,1,0:T(8,128)}, f32[16,8,2048]{2,1,0:T(8,128)}, f32[16,8,2048]{2,1,0:T(8,128)}) custom-call(s32[2]{0:T(128)S(1)} %pad_add_fusion.1.rows, f32[2,4,8,1536]{3,2,1,0:T(8,128)S(1)} %bitcast.67, f32[2,4,8,1536]{3,2,1,0:T(8,128)S(1)} %bitcast.68, ...), custom_call_target="tpu_custom_call", output_to_operand_aliasing={{0}: (3, {}), {1}: (4, {}), {2}: (5, {})} | custom-call | bytes 1572864 | tf_op jit(solution)/shard_map/place_chunks/pallas_call | solution.py:77
  71.2 0.0 collective-permute-done.9
  71.2 2.7 %collective-permute-start.14 = (f32[8,8,1536]{2,1,0:T(8,128)S(1)}, f32[8,8,1536]{2,1,0:T(8,128)S(1)}, u32[]{:S(2)}, u32[]{:S(2)}) collective-permute-start(f32[8,8,1536]{2,1,0:T(8,128)S(1)} %collective-permute-done.9), channel_id=1, source_target_pairs={{0,1},{1,0},{2,3},{3,2},{4,5},{5,4},{6,7},{7,6},{8,9},{9,8},{10,11... | collective-permute-start | bytes 1179656 | tf_op jit(solution)/shard_map/ppermute | solution.py:91
  74.0 0.0 collective-permute-done.12
  74.0 1.6 %place_chunks.7 = (f32[16,8,2048]{2,1,0:T(8,128)}, f32[16,8,2048]{2,1,0:T(8,128)}, f32[16,8,2048]{2,1,0:T(8,128)}) custom-call(s32[2]{0:T(128)S(1)} %pad_add_fusion.rows, f32[2,4,8,1536]{3,2,1,0:T(8,128)S(1)} %bitcast.66, f32[2,4,8,1536]{3,2,1,0:T(8,128)S(1)} %bitcast.69, ...), custom_call_target="tpu_custom_call", output_to_operand_aliasing={{0}: (3, {}), {1}: (4, {}), {2}: (5, {})} | custom-call | bytes 1572864 | tf_op jit(solution)/shard_map/place_chunks/pallas_call | solution.py:77
  75.6 0.2 collective-permute-done.8
  75.8 0.9 %collective-permute-start.13 = (f32[8,8,1536]{2,1,0:T(8,128)S(1)}, f32[8,8,1536]{2,1,0:T(8,128)S(1)}, u32[]{:S(2)}, u32[]{:S(2)}) collective-permute-start(f32[8,8,1536]{2,1,0:T(8,128)S(1)} %collective-permute-done.8), channel_id=1, source_target_pairs={{0,1},{1,0},{2,3},{3,2},{4,5},{5,4},{6,7},{7,6},{8,9},{9,8},{10,11... | collective-permute-start | bytes 1179656 | tf_op jit(solution)/shard_map/ppermute | solution.py:91
  76.6 0.1 pad_add_fusion.2.rows
  76.7 0.0 collective-permute-done.14
  76.7 1.6 %place_chunks.8 = (f32[16,8,2048]{2,1,0:T(8,128)}, f32[16,8,2048]{2,1,0:T(8,128)}, f32[16,8,2048]{2,1,0:T(8,128)}) custom-call(s32[2]{0:T(128)S(1)} %pad_add_fusion.2.rows, f32[2,4,8,1536]{3,2,1,0:T(8,128)S(1)} %bitcast.65, f32[2,4,8,1536]{3,2,1,0:T(8,128)S(1)} %bitcast.70, ...), custom_call_target="tpu_custom_call", output_to_operand_aliasing={{0}: (3, {}), {1}: (4, {}), {2}: (5, {})} | custom-call | bytes 1572864 | tf_op jit(solution)/shard_map/place_chunks/pallas_call | solution.py:77
  78.3 0.0 collective-permute-done.13
  78.3 0.8 %place_chunks.9 = (f32[16,8,2048]{2,1,0:T(8,128)}, f32[16,8,2048]{2,1,0:T(8,128)}, f32[16,8,2048]{2,1,0:T(8,128)}) custom-call(s32[1]{0:T(128)} %bitcast.rows, f32[2,4,8,1536]{3,2,1,0:T(8,128)S(1)} %bitcast.71, f32[16,8,2048]{2,1,0:T(8,128)} %get-tuple-element.67.refs_1_, ...), custom_call_target="tpu_custom_call", output_to_operand_aliasing={{0}: (2, {}), {1}: (3, {}), {2}: (4, {})} | custom-call | bytes 786432 | tf_op jit(solution)/shard_map/place_chunks/pallas_call | solution.py:77
  (4 shorter events, 0.1 us)
Async XLA Ops:
  0.6 6.7 %copy-start = (f32[1,1,128,2048]{3,2,1,0:T(8,128)S(1)}, f32[1,1,128,2048]{3,2,1,0:T(8,128)}, u32[]{:S(2)}) copy-start(f32[1,1,128,2048]{3,2,1,0:T(8,128)} %param.4) | copy-start | bytes 3145732
  3.6 5.5 %collective-permute-start = (f32[64,2048]{1,0:T(8,128)}, f32[64,2048]{1,0:T(8,128)S(1)}, u32[]{:S(2)}, u32[]{:S(2)}) collective-permute-start(f32[64,2048]{1,0:T(8,128)} %get-tuple-element.76), channel_id=1, source_target_pairs={{0,1},{1,0},{2,3},{3,2},{4,5},{5,4},{6,7},{7,6},{8,9},{9,8},{10,11... | collective-permute-start | bytes 1572872 | tf_op jit(solution)/shard_map/ppermute | solution.py:91
  6.9 3.2 %collective-permute-start.1 = (f32[64,2048]{1,0:T(8,128)}, f32[64,2048]{1,0:T(8,128)S(1)}, u32[]{:S(2)}, u32[]{:S(2)}) collective-permute-start(f32[64,2048]{1,0:T(8,128)} %get-tuple-element.78), channel_id=1, source_target_pairs={{0,1},{1,0},{2,3},{3,2},{4,5},{5,4},{6,7},{7,6},{8,9},{9,8},{10,11... | collective-permute-start | bytes 1572872 | tf_op jit(solution)/shard_map/ppermute | solution.py:91
  6.9 3.2 %collective-permute-start.2 = (f32[64,2048]{1,0:T(8,128)S(1)}, f32[64,2048]{1,0:T(8,128)S(1)}, u32[]{:S(2)}, u32[]{:S(2)}) collective-permute-start(f32[64,2048]{1,0:T(8,128)S(1)} %get-tuple-element.77), channel_id=1, source_target_pairs={{0,1},{1,0},{2,3},{3,2},{4,5},{5,4},{6,7},{7,6},{8,9},{9,8},{10,11... | collective-permute-start | bytes 1572872 | tf_op jit(solution)/shard_map/ppermute | solution.py:91
  10.4 8.6 %collective-permute-start.3 = (f32[8,8,1536]{2,1,0:T(8,128)S(1)}, f32[8,8,1536]{2,1,0:T(8,128)S(1)}, u32[]{:S(2)}, u32[]{:S(2)}) collective-permute-start(f32[8,8,1536]{2,1,0:T(8,128)S(1)} %get-tuple-element.43), channel_id=1, source_target_pairs={{0,8},{64,72},{128,136},{192,200},{2,10},{66,74},{130,138},{194,20... | collective-permute-start | bytes 1179656 | tf_op jit(solution)/shard_map/ppermute | solution.py:151
  11.6 11.5 %collective-permute-start.4 = (f32[8,8,1536]{2,1,0:T(8,128)S(1)}, f32[8,8,1536]{2,1,0:T(8,128)S(1)}, u32[]{:S(2)}, u32[]{:S(2)}) collective-permute-start(f32[8,8,1536]{2,1,0:T(8,128)S(1)} %get-tuple-element.44), channel_id=1, source_target_pairs={{0,16},{64,80},{128,144},{192,208},{2,18},{66,82},{130,146},{194,2... | collective-permute-start | bytes 1179656 | tf_op jit(solution)/shard_map/ppermute | solution.py:151
  12.0 11.1 %collective-permute-start.5 = (f32[8,8,1536]{2,1,0:T(8,128)S(1)}, f32[8,8,1536]{2,1,0:T(8,128)S(1)}, u32[]{:S(2)}, u32[]{:S(2)}) collective-permute-start(f32[8,8,1536]{2,1,0:T(8,128)S(1)} %get-tuple-element.45), channel_id=1, source_target_pairs={{0,24},{64,88},{128,152},{192,216},{2,26},{66,90},{130,154},{194,2... | collective-permute-start | bytes 1179656 | tf_op jit(solution)/shard_map/ppermute | solution.py:151
  34.0 4.6 %collective-permute-start.6 = (f32[8,1536]{1,0:T(8,128)S(1)}, f32[8,1536]{1,0:T(8,128)S(1)}, u32[]{:S(2)}, u32[]{:S(2)}) collective-permute-start(f32[8,1536]{1,0:T(8,128)S(1)} %reduce_sum.9), channel_id=1, source_target_pairs={{0,64},{2,66},{4,68},{6,70},{16,80},{18,82},{20,84},{22,86},{8,72}... | collective-permute-start | bytes 147464 | tf_op jit(solution)/shard_map/ppermute | solution.py:103
  38.6 6.6 %collective-permute-start.7 = (f32[8,1536]{1,0:T(8,128)S(1)}, f32[8,1536]{1,0:T(8,128)S(1)}, u32[]{:S(2)}, u32[]{:S(2)}) collective-permute-start(f32[8,1536]{1,0:T(8,128)S(1)} %add.125), channel_id=1, source_target_pairs={{0,192},{2,194},{4,196},{6,198},{16,208},{18,210},{20,212},{22,214... | collective-permute-start | bytes 147464 | tf_op jit(solution)/shard_map/ppermute | solution.py:104
  55.0 8.2 %collective-permute-start.10 = (f32[8,8,1536]{2,1,0:T(8,128)S(1)}, f32[8,8,1536]{2,1,0:T(8,128)S(1)}, u32[]{:S(2)}, u32[]{:S(2)}) collective-permute-start(f32[8,8,1536]{2,1,0:T(8,128)S(1)} %all_to_all.11), channel_id=1, source_target_pairs={{0,16},{64,80},{128,144},{192,208},{2,18},{66,82},{130,146},{194,2... | collective-permute-start | bytes 1179656 | tf_op jit(solution)/shard_map/ppermute | solution.py:156
  55.2 14.4 %collective-permute-start.11 = (f32[8,8,1536]{2,1,0:T(8,128)S(1)}, f32[8,8,1536]{2,1,0:T(8,128)S(1)}, u32[]{:S(2)}, u32[]{:S(2)}) collective-permute-start(f32[8,8,1536]{2,1,0:T(8,128)S(1)} %all_to_all.11), channel_id=1, source_target_pairs={{0,1},{1,0},{2,3},{3,2},{4,5},{5,4},{6,7},{7,6},{8,9},{9,8},{10,11... | collective-permute-start | bytes 1179656 | tf_op jit(solution)/shard_map/ppermute | solution.py:91
  62.1 9.1 %collective-permute-start.9 = (f32[8,8,1536]{2,1,0:T(8,128)S(1)}, f32[8,8,1536]{2,1,0:T(8,128)S(1)}, u32[]{:S(2)}, u32[]{:S(2)}) collective-permute-start(f32[8,8,1536]{2,1,0:T(8,128)S(1)} %all_to_all.11), channel_id=1, source_target_pairs={{0,8},{64,72},{128,136},{192,200},{2,10},{66,74},{130,138},{194,20... | collective-permute-start | bytes 1179656 | tf_op jit(solution)/shard_map/ppermute | solution.py:156
  63.2 10.7 %collective-permute-start.12 = (f32[8,8,1536]{2,1,0:T(8,128)S(1)}, f32[8,8,1536]{2,1,0:T(8,128)S(1)}, u32[]{:S(2)}, u32[]{:S(2)}) collective-permute-start(f32[8,8,1536]{2,1,0:T(8,128)S(1)} %collective-permute-done.10), channel_id=1, source_target_pairs={{0,1},{1,0},{2,3},{3,2},{4,5},{5,4},{6,7},{7,6},{8,9},{9,8},{10,11... | collective-permute-start | bytes 1179656 | tf_op jit(solution)/shard_map/ppermute | solution.py:91
  68.8 6.9 %collective-permute-start.8 = (f32[8,8,1536]{2,1,0:T(8,128)S(1)}, f32[8,8,1536]{2,1,0:T(8,128)S(1)}, u32[]{:S(2)}, u32[]{:S(2)}) collective-permute-start(f32[8,8,1536]{2,1,0:T(8,128)S(1)} %all_to_all.11), channel_id=1, source_target_pairs={{0,24},{64,88},{128,152},{192,216},{2,26},{66,90},{130,154},{194,2... | collective-permute-start | bytes 1179656 | tf_op jit(solution)/shard_map/ppermute | solution.py:156
  71.2 5.5 %collective-permute-start.14 = (f32[8,8,1536]{2,1,0:T(8,128)S(1)}, f32[8,8,1536]{2,1,0:T(8,128)S(1)}, u32[]{:S(2)}, u32[]{:S(2)}) collective-permute-start(f32[8,8,1536]{2,1,0:T(8,128)S(1)} %collective-permute-done.9), channel_id=1, source_target_pairs={{0,1},{1,0},{2,3},{3,2},{4,5},{5,4},{6,7},{7,6},{8,9},{9,8},{10,11... | collective-permute-start | bytes 1179656 | tf_op jit(solution)/shard_map/ppermute | solution.py:91
  75.8 2.6 %collective-permute-start.13 = (f32[8,8,1536]{2,1,0:T(8,128)S(1)}, f32[8,8,1536]{2,1,0:T(8,128)S(1)}, u32[]{:S(2)}, u32[]{:S(2)}) collective-permute-start(f32[8,8,1536]{2,1,0:T(8,128)S(1)} %collective-permute-done.8), channel_id=1, source_target_pairs={{0,1},{1,0},{2,3},{3,2},{4,5},{5,4},{6,7},{7,6},{8,9},{9,8},{10,11... | collective-permute-start | bytes 1179656 | tf_op jit(solution)/shard_map/ppermute | solution.py:91

commit v3 on v2

v3 whole, which is shorter than its diff:
```python
import functools

import jax
import jax.numpy as jnp
from jax import lax
from jax.experimental import pallas as pl
from jax.experimental.pallas import tpu as pltpu
from jax.sharding import PartitionSpec as P

bias_one = 0.9999734386011124
bias_two = 0.994079470779666

AXES = ("row", "col")
SHIFT = (0, 0)
WAYS = (2, 1, 3)


def device(x, y, z, core):
    return (z % 8 * 2 + x % 2) * 16 + x // 2 * 8 + y * 2 + core


def place(core, along, pair, across, far):
    x, y = (along, across) if core == 0 else (across, along)
    return device(x, y, 2 * far + pair + SHIFT[core], core)


def ring(change):
    return [
        (place(core, along, pair, across, far), place(core, (along + change) % 4, pair, across, far))
        for core in range(2) for along in range(4) for pair in range(2) for across in range(4) for far in range(4)
    ]


SECOND = [
    [place(core, along, pair, across, far) for across in range(4) for pair in range(2)]
    for core in range(2) for along in range(4) for far in range(4)
]


def far_pairs(change):
    return [
        (device(x, y, 2 * far + pair + SHIFT[core], core), device(x, y, 2 * change(far) + pair + SHIFT[core], core))
        for core in range(2) for far in range(4) for pair in range(2) for x in range(4) for y in range(4)
    ]


PEERS = 32
ROWS, D = 128, 2048
HALF = ROWS // 2
WIDE = D // 4
STEPS = 4
ROOM_A = 60 << 20
ROOM_B = 8 << 20
VMEM = 8 << 20
STEP_ROWS = HALF // STEPS
STEP_PEERS = PEERS // STEPS


def place_kernel(which, at, *refs):
    outs, sems = refs[-4:-1], refs[-1]
    copies = [
        pltpu.make_async_copy(
            refs[i].at[:, g, :, pl.ds(k * WIDE, WIDE)],
            outs[k].at[pl.ds(at[8 + which[i]], 2), :, pl.ds(g * WIDE, WIDE)],
            sems.at[i, k, g],
        )
        for i in range(sems.shape[0])
        for k in range(3)
        for g in range(4)
    ]
    for copy in copies:
        copy.start()
    for copy in copies:
        copy.wait()


def place_chunks(at, every, which, before):
    chunks = [every[i] for i in which]
    anywhere = pl.BlockSpec(memory_space=pl.ANY)
    n = len(chunks)
    return pl.pallas_call(
        functools.partial(place_kernel, which),
        in_specs=[pl.BlockSpec(memory_space=pltpu.SMEM)] + [anywhere] * (n + len(before)),
        out_specs=[anywhere] * 3,
        out_shape=[jax.ShapeDtypeStruct((ROWS // 8, 8, D), jnp.float32)] * 3,
        scratch_shapes=[pltpu.SemaphoreType.DMA((n, 3, 4))],
        input_output_aliases={1 + n + k: k for k in range(len(before))},
        compiler_params=pltpu.CompilerParams(vmem_limit_bytes=8 << 20),
        name="place_chunks",
    )(at, *(chunk.reshape(2, 4, 8, 3 * WIDE) for chunk in chunks), *before)


def across_cores(x):
    return lax.ppermute(x, AXES, [(i, i ^ 1) for i in range(256)])


def exchange(x, groups):
    return lax.all_to_all(x, AXES, 0, 0, axis_index_groups=groups, tiled=True)


def repeat(x, groups):
    return jnp.broadcast_to(x[None], (len(groups[0]),) + x.shape)


def far_sum(x):
    x = x + lax.ppermute(x, AXES, far_pairs(lambda far: far ^ 1))
    return x + lax.ppermute(x, AXES, far_pairs(lambda far: far ^ 3))


def adam(arrays):
    old, first, second, gradient = (x[0, 0] for x in arrays)
    first = 0.9 * first + 0.1 * gradient
    second = 0.95 * second + 0.05 * gradient * gradient
    scaled = second * (1.0 / bias_two)
    bottom = bias_one * (scaled * lax.rsqrt(scaled)) + bias_one * 1e-08
    return old - 0.003 * (first / bottom + 0.1 * old), first, second


def arrange(block, out_ref, added=None):
    for k in range(3):
        for p in range(8):
            value = block[k][8 * (p // 4) : 8 * (p // 4) + 8, p % 4 * WIDE : (p % 4 + 1) * WIDE]
            place = (p, slice(None), slice(k * WIDE, (k + 1) * WIDE))
            out_ref[place] = value if added is None else value + added[place]


def send_kernel(at, *refs):
    for i in range(len(refs) - 3):

        @pl.when(pl.program_id(0) == i)
        def _():
            arrange(refs[:3], refs[3 + i])


def join_kernel(at, weights, first, second, added, out):
    arrange((weights, first, second), out, added)


CHUNK = (8, 8, 3 * WIDE)


def send_chunks(at, arrays, order):
    steps = len(order)

    def source(i, at):
        where = at[4 + order[-1]]
        for n in range(steps - 1):
            where = jnp.where(i == n, at[4 + order[n]], where)
        return where, 0

    return pl.pallas_call(
        send_kernel,
        grid_spec=pltpu.PrefetchScalarGridSpec(
            num_scalar_prefetch=1,
            grid=(steps,),
            in_specs=[pl.BlockSpec((16, D), source)] * 3,
            out_specs=[pl.BlockSpec(CHUNK, lambda i, at: (0, 0, 0))] * steps,
        ),
        out_shape=[jax.ShapeDtypeStruct(CHUNK, jnp.float32)] * steps,
        compiler_params=pltpu.CompilerParams(vmem_limit_bytes=12 << 20),
        name="send_chunks",
    )(at, *arrays)


def join_chunk(at, arrays, received, d):
    return pl.pallas_call(
        join_kernel,
        grid_spec=pltpu.PrefetchScalarGridSpec(
            num_scalar_prefetch=1,
            grid=(1,),
            in_specs=[pl.BlockSpec((16, D), lambda i, at: (at[d], 0))] * 3 + [pl.BlockSpec(CHUNK, lambda i, at: (0, 0, 0))],
            out_specs=pl.BlockSpec(CHUNK, lambda i, at: (0, 0, 0)),
        ),
        out_shape=jax.ShapeDtypeStruct(CHUNK, jnp.float32),
        compiler_params=pltpu.CompilerParams(vmem_limit_bytes=8 << 20),
        name="join_chunk",
    )(at, *arrays, received)


def on_device(*arrays):
    row, col = lax.axis_index("row").astype(jnp.int32), lax.axis_index("col").astype(jnp.int32)
    core = lax.rem(col, 2)
    x, y = col // 8 * 2 + lax.rem(row, 2), lax.rem(col // 2, 4)
    mine_at, their_at = jnp.where(core == 0, x, y), jnp.where(core == 0, y, x)
    ahead = [core * 4 + lax.rem(mine_at + d, 4) for d in range(4)] + [(1 - core) * 4 + lax.rem(their_at + d, 4) for d in range(4)]
    behind = [core * 8 + lax.rem(mine_at + 4 - d, 4) * 2 for d in (0,) + WAYS]
    behind += [(1 - core) * 8 + lax.rem(their_at + 4 - d, 4) * 2 for d in (0,) + WAYS]
    at = jnp.stack(ahead + behind).astype(jnp.int32)
    arrays = adam(arrays)
    order = WAYS + (0,)
    received = [across_cores(chunk) for chunk in send_chunks(at, arrays, order)]
    sums = [join_chunk(at, arrays, theirs, d) for theirs, d in zip(received, order)]
    other = [lax.ppermute(chunk, AXES, ring(d)) for chunk, d in zip(sums, WAYS)]
    mine = (sums[3] + other[0]) + (other[1] + other[2])
    mine = jnp.sum(exchange(mine, SECOND), axis=0)
    mine = far_sum(mine) * (1.0 / 256.0)
    mine = exchange(repeat(mine, SECOND), SECOND)
    chunks = [mine] + [lax.ppermute(mine, AXES, ring(d)) for d in WAYS]
    chunks += [across_cores(chunk) for chunk in chunks]
    outs = place_chunks(at, chunks, (0, 1, 2, 3, 4, 5), ())
    outs = place_chunks(at, chunks, (6, 7), outs)
    return tuple(out.reshape(ROWS, D) for out in outs)


def solution(mesh):
    spec = P("row", "col", None, None)
    return jax.shard_map(on_device, mesh=mesh, in_specs=(spec,) * 4, out_specs=(P(),) * 3, check_vma=False)
```

time: 79.4 us -> 78.1 us (0.984)
  waiting for transfers between devices: 13.6 us -> 11.1 us
  other arithmetic: 5.08 us -> 2.93 us
  starting transfers between devices: 32.4 us -> 34.4 us
    ppermute x6, waiting for transfers between devices: 9.1 us -> 6.86 us  [the longest x3 6.85 us: on_device(): other = [lax.ppermute(chunk, AXES, ring(d)) for chunk, d in zip(sums, WAYS)]]
    sub x2 -> x1, other arithmetic: 4.74 us -> 2.81 us  [adam(): return (old - 0.003 * (first / bottom + 0.1 * old), first, second)]
    ppermute x6, starting transfers between devices: 5.69 us -> 7.43 us  [the longest x3 4.1 us: on_device(): other = [lax.ppermute(chunk, AXES, ring(d)) for chunk, d in zip(sums, WAYS)]]
    pallas_call x6 -> x7, Pallas kernels: 6.79 us -> 7.28 us  [the longest x2 4.17 us: place_chunks(): pl.pallas_call(functools.partial(place_kernel, which), in_specs=[pl.Block...]
    ppermute x7 -> x8, starting transfers between devices: 19 us -> 19.3 us  [across_cores(): return lax.ppermute(x, AXES, [(i, i ^ 1) for i in range(256)])]
  transfers between devices with their start and end apart: 15 -> 16, of which waited for: 7 -> 5; matrix products, arithmetic and copies ran while one was open for 3% -> 0% of each run, Pallas kernels for 7% -> 6%
where the time goes in v3:
time: 78.1 us; the launch traced here: 77.3 us
  starting transfers between devices  34.4 us (44%)
  blocking collectives  20.6 us (26%)
  waiting for transfers between devices  11.1 us (14%)
  Pallas kernels  7.28 us (9%)
  other arithmetic  2.93 us (4%)
  between operations  0.88 us (1%)
    all_to_all x2, blocking collectives, exchange(): return lax.all_to_all(x, AXES, 0, 0, axis_index_groups=groups, tiled=True)  20.6 us
    ppermute x8, starting transfers between devices, across_cores(): return lax.ppermute(x, AXES, [(i, i ^ 1) for i in range(256)])  19.3 us
    ppermute x3, waiting for transfers between devices, on_device(): other = [lax.ppermute(chunk, AXES, ring(d)) for chunk, d in zip(sums, WAYS)]  6.85 us
    ppermute x1, starting transfers between devices, far_sum(): return x + lax.ppermute(x, AXES, far_pairs(lambda far: far ^ 3))  4.61 us
    pallas_call x2, Pallas kernels, place_chunks(): pl.pallas_call(functools.partial(place_kernel, which), in_specs=[pl.Block...  4.17 us
    ppermute x3, starting transfers between devices, on_device(): other = [lax.ppermute(chunk, AXES, ring(d)) for chunk, d in zip(sums, WAYS)]  4.1 us
    ppermute x3, starting transfers between devices, on_device(): chunks = [mine] + [lax.ppermute(mine, AXES, ring(d)) for d in WAYS]  3.33 us
    ppermute x1, starting transfers between devices, far_sum(): x = x + lax.ppermute(x, AXES, far_pairs(lambda far: far ^ 1))  3.08 us
  transfers between devices with their start and end apart: 16, of which 5 were waited for; matrix products, arithmetic and copies ran while one was open for 0% of the time, Pallas kernels for 6%

profile of v3, /device:TPU:1, one launch (start us, length us, event | category | flops | bytes accessed | tf_op | source)
XLA Modules:
  0.0 77.3 jit_solution(1825301910531696447)
XLA Ops:
  0.8 2.8 %fusion.6 = (f32[128,2048]{1,0:T(8,128)S(1)}, f32[128,2048]{1,0:T(8,128)S(1)}, f32[128,2048]{1,0:T(8,128)S(1)}) fusion(f32[1,1,128,2048]{3,2,1,0:T(8,128)} %param.4, f32[1,1,128,2048]{3,2,1,0:T(8,128)} %param.7, f32[1,1,128,2048]{3,2,1,0:T(8,128)} %param.6, f32[1,1,128,2048]{3,2,1,0:T(8,128)} %param.5), kind=kLoop, calls=%fused_computation.8 | loop fusion | flops 4194304 | bytes 7340032 | tf_op jit(solution)/shard_map/sub | solution.py:116
  3.6 0.1 stack.67.at
  3.7 0.8 %send_chunks.1 = (f32[8,8,1536]{2,1,0:T(8,128)S(1)}, f32[8,8,1536]{2,1,0:T(8,128)S(1)}, f32[8,8,1536]{2,1,0:T(8,128)S(1)}, f32[8,8,1536]{2,1,0:T(8,128)S(1)}) custom-call(s32[16]{0:T(128)S(1)} %stack.67.at, f32[128,2048]{1,0:T(8,128)S(1)} %get-tuple-element.23.refs_0_.weights, f32[128,2048]{1,0:T(8,128)S(1)} %get-tuple-element.25.refs_1_.first, ...), custom_call_target="tpu_custom_call" | custom-call | tf_op jit(solution)/shard_map/send_chunks/pallas_call | solution.py:151
  4.5 3.3 %collective-permute-start.1 = (f32[8,8,1536]{2,1,0:T(8,128)S(1)}, f32[8,8,1536]{2,1,0:T(8,128)S(1)}, u32[]{:S(2)}, u32[]{:S(2)}) collective-permute-start(f32[8,8,1536]{2,1,0:T(8,128)S(1)} %get-tuple-element.14), channel_id=1, source_target_pairs={{0,1},{1,0},{2,3},{3,2},{4,5},{5,4},{6,7},{7,6},{8,9},{9,8},{10,11... | collective-permute-start | bytes 1179656 | tf_op jit(solution)/shard_map/ppermute | solution.py:94
  7.8 0.1 collective-permute-start.3
  7.9 0.4 collective-permute-start.5
  8.3 0.1 collective-permute-start
  8.4 0.7 collective-permute-done.1.added
  9.1 0.6 join_chunk.5
  9.7 1.3 %collective-permute-start.2 = (f32[8,8,1536]{2,1,0:T(8,128)S(1)}, f32[8,8,1536]{2,1,0:T(8,128)S(1)}, u32[]{:S(2)}, u32[]{:S(2)}) collective-permute-start(f32[8,8,1536]{2,1,0:T(8,128)S(1)} %join_chunk.5), channel_id=1, source_target_pairs={{0,8},{64,72},{128,136},{192,200},{2,10},{66,74},{130,138},{194,20... | collective-permute-start | bytes 1179656 | tf_op jit(solution)/shard_map/ppermute | solution.py:193
  11.0 0.0 collective-permute-done.3.added
  11.0 0.6 join_chunk.6
  11.6 0.5 collective-permute-start.4
  12.1 0.0 collective-permute-done.5.added
  12.1 0.6 join_chunk.7
  12.7 2.4 %collective-permute-start.6 = (f32[8,8,1536]{2,1,0:T(8,128)S(1)}, f32[8,8,1536]{2,1,0:T(8,128)S(1)}, u32[]{:S(2)}, u32[]{:S(2)}) collective-permute-start(f32[8,8,1536]{2,1,0:T(8,128)S(1)} %join_chunk.7), channel_id=1, source_target_pairs={{0,24},{64,88},{128,152},{192,216},{2,26},{66,90},{130,154},{194,2... | collective-permute-start | bytes 1179656 | tf_op jit(solution)/shard_map/ppermute | solution.py:193
  15.0 0.0 collective-permute-done.added
  15.0 0.6 join_chunk.4
  15.6 2.7 %collective-permute-done.2 = f32[8,8,1536]{2,1,0:T(8,128)S(1)} collective-permute-done((f32[8,8,1536]{2,1,0:T(8,128)S(1)}, f32[8,8,1536]{2,1,0:T(8,128)S(1)}, u32[]{:S(2)}, u32[]{:S(2)}) %collective-permute-start.2) | collective-permute-done | bytes 393248 | tf_op jit(solution)/shard_map/ppermute | solution.py:193
  18.3 4.2 %collective-permute-done.4 = f32[8,8,1536]{2,1,0:T(8,128)S(1)} collective-permute-done((f32[8,8,1536]{2,1,0:T(8,128)S(1)}, f32[8,8,1536]{2,1,0:T(8,128)S(1)}, u32[]{:S(2)}, u32[]{:S(2)}) %collective-permute-start.4) | collective-permute-done | bytes 393248 | tf_op jit(solution)/shard_map/ppermute | solution.py:193
  22.5 0.0 collective-permute-done.6
  22.5 0.1 add_add_fusion
  22.5 10.8 %all_to_all.10 = f32[8,8,1536]{2,1,0:T(8,128)S(1)} all-to-all(f32[8,8,1536]{2,1,0:T(8,128)S(1)} %add_add_fusion), channel_id=1, replica_groups={{0,32,2,34,4,36,6,38},{64,96,66,98,68,100,70,102},{128,160,130,162,132,..., dimensions={0} | all-to-all | bytes 786432 | tf_op jit(solution)/shard_map/all_to_all | solution.py:98
  33.3 3.1 %collective-permute-start.7 = (f32[8,1536]{1,0:T(8,128)S(1)}, f32[8,1536]{1,0:T(8,128)S(1)}, u32[]{:S(2)}, u32[]{:S(2)}) collective-permute-start(f32[8,1536]{1,0:T(8,128)S(1)} %reduce_sum.9), channel_id=1, source_target_pairs={{0,64},{2,66},{4,68},{6,70},{16,80},{18,82},{20,84},{22,86},{8,72}... | collective-permute-start | bytes 147464 | tf_op jit(solution)/shard_map/ppermute | solution.py:106
  36.4 1.5 %collective-permute-done.7 = f32[8,1536]{1,0:T(8,128)S(1)} collective-permute-done((f32[8,1536]{1,0:T(8,128)S(1)}, f32[8,1536]{1,0:T(8,128)S(1)}, u32[]{:S(2)}, u32[]{:S(2)}) %collective-permute-start.7) | collective-permute-done | bytes 49184 | tf_op jit(solution)/shard_map/ppermute | solution.py:106
  37.9 4.6 %collective-permute-start.8 = (f32[8,1536]{1,0:T(8,128)S(1)}, f32[8,1536]{1,0:T(8,128)S(1)}, u32[]{:S(2)}, u32[]{:S(2)}) collective-permute-start(f32[8,1536]{1,0:T(8,128)S(1)} %add.164), channel_id=1, source_target_pairs={{0,192},{2,194},{4,196},{6,198},{16,208},{18,210},{20,212},{22,214... | collective-permute-start | bytes 147464 | tf_op jit(solution)/shard_map/ppermute | solution.py:107
  42.5 2.0 %collective-permute-done.8 = f32[8,1536]{1,0:T(8,128)S(1)} collective-permute-done((f32[8,1536]{1,0:T(8,128)S(1)}, f32[8,1536]{1,0:T(8,128)S(1)}, u32[]{:S(2)}, u32[]{:S(2)}) %collective-permute-start.8) | collective-permute-done | bytes 49184 | tf_op jit(solution)/shard_map/ppermute | solution.py:107
  44.6 9.8 %all_to_all.11 = f32[8,8,1536]{2,1,0:T(8,128)S(1)} all-to-all(f32[8,8,1536]{2,1,0:T(8,128)S(1)} %broadcast_in_dim.2), channel_id=1, replica_groups={{0,32,2,34,4,36,6,38},{64,96,66,98,68,100,70,102},{128,160,130,162,132,..., dimensions={0} | all-to-all | bytes 786432 | tf_op jit(solution)/shard_map/all_to_all | solution.py:98
  54.4 1.9 %collective-permute-start.13 = (f32[8,8,1536]{2,1,0:T(8,128)S(1)}, f32[8,8,1536]{2,1,0:T(8,128)S(1)}, u32[]{:S(2)}, u32[]{:S(2)}) collective-permute-start(f32[8,8,1536]{2,1,0:T(8,128)S(1)} %all_to_all.11), channel_id=1, source_target_pairs={{0,8},{64,72},{128,136},{192,200},{2,10},{66,74},{130,138},{194,20... | collective-permute-start | bytes 1179656 | tf_op jit(solution)/shard_map/ppermute | solution.py:198
  56.3 0.7 collective-permute-start.11
  57.0 0.8 %collective-permute-start.9 = (f32[8,8,1536]{2,1,0:T(8,128)S(1)}, f32[8,8,1536]{2,1,0:T(8,128)S(1)}, u32[]{:S(2)}, u32[]{:S(2)}) collective-permute-start(f32[8,8,1536]{2,1,0:T(8,128)S(1)} %all_to_all.11), channel_id=1, source_target_pairs={{0,16},{64,80},{128,144},{192,208},{2,18},{66,82},{130,146},{194,2... | collective-permute-start | bytes 1179656 | tf_op jit(solution)/shard_map/ppermute | solution.py:198
  57.7 6.4 %collective-permute-start.14 = (f32[8,8,1536]{2,1,0:T(8,128)S(1)}, f32[8,8,1536]{2,1,0:T(8,128)S(1)}, u32[]{:S(2)}, u32[]{:S(2)}) collective-permute-start(f32[8,8,1536]{2,1,0:T(8,128)S(1)} %all_to_all.11), channel_id=1, source_target_pairs={{0,1},{1,0},{2,3},{3,2},{4,5},{5,4},{6,7},{7,6},{8,9},{9,8},{10,11... | collective-permute-start | bytes 1179656 | tf_op jit(solution)/shard_map/ppermute | solution.py:94
  64.2 0.0 collective-permute-done.13
  64.2 4.2 %collective-permute-start.15 = (f32[8,8,1536]{2,1,0:T(8,128)S(1)}, f32[8,8,1536]{2,1,0:T(8,128)S(1)}, u32[]{:S(2)}, u32[]{:S(2)}) collective-permute-start(f32[8,8,1536]{2,1,0:T(8,128)S(1)} %collective-permute-done.13), channel_id=1, source_target_pairs={{0,1},{1,0},{2,3},{3,2},{4,5},{5,4},{6,7},{7,6},{8,9},{9,8},{10,11... | collective-permute-start | bytes 1179656 | tf_op jit(solution)/shard_map/ppermute | solution.py:94
  68.4 0.0 collective-permute-done.11
  68.4 4.7 %collective-permute-start.12 = (f32[8,8,1536]{2,1,0:T(8,128)S(1)}, f32[8,8,1536]{2,1,0:T(8,128)S(1)}, u32[]{:S(2)}, u32[]{:S(2)}) collective-permute-start(f32[8,8,1536]{2,1,0:T(8,128)S(1)} %collective-permute-done.11), channel_id=1, source_target_pairs={{0,1},{1,0},{2,3},{3,2},{4,5},{5,4},{6,7},{7,6},{8,9},{9,8},{10,11... | collective-permute-start | bytes 1179656 | tf_op jit(solution)/shard_map/ppermute | solution.py:94
  73.1 0.0 collective-permute-done.9
  73.1 0.0 collective-permute-start.10
  73.1 0.0 collective-permute-done.14
  73.1 0.0 collective-permute-done.15
  73.1 2.6 %place_chunks.2 = (f32[16,8,2048]{2,1,0:T(8,128)}, f32[16,8,2048]{2,1,0:T(8,128)}, f32[16,8,2048]{2,1,0:T(8,128)}) custom-call(s32[16]{0:T(128)S(1)} %stack.67.at, f32[2,4,8,1536]{3,2,1,0:T(8,128)S(1)} %bitcast.45, f32[2,4,8,1536]{3,2,1,0:T(8,128)S(1)} %bitcast.46, f32[2,4,8,1536]{3,2,1,0:T(8,128)S(1)} %bitcast.48, f32[2,4,8,1536]{3,2,1,0:T(8,128)S(1)} %bitcast.47, ...), custom_call_target="tpu_custom_call" | custom-call | tf_op jit(solution)/shard_map/place_chunks/pallas_call | solution.py:81
  75.6 0.0 collective-permute-done.12
  75.7 0.0 collective-permute-done.10
  75.7 1.6 %place_chunks.3 = (f32[16,8,2048]{2,1,0:T(8,128)}, f32[16,8,2048]{2,1,0:T(8,128)}, f32[16,8,2048]{2,1,0:T(8,128)}) custom-call(s32[16]{0:T(128)S(1)} %stack.67.at, f32[2,4,8,1536]{3,2,1,0:T(8,128)S(1)} %bitcast.51, f32[2,4,8,1536]{3,2,1,0:T(8,128)S(1)} %bitcast.49, ...), custom_call_target="tpu_custom_call", output_to_operand_aliasing={{0}: (3, {}), {1}: (4, {}), {2}: (5, {})} | custom-call | tf_op jit(solution)/shard_map/place_chunks/pallas_call | solution.py:81
  (4 shorter events, 0.1 us)
Async XLA Ops:
  4.5 4.7 %collective-permute-start.1 = (f32[8,8,1536]{2,1,0:T(8,128)S(1)}, f32[8,8,1536]{2,1,0:T(8,128)S(1)}, u32[]{:S(2)}, u32[]{:S(2)}) collective-permute-start(f32[8,8,1536]{2,1,0:T(8,128)S(1)} %get-tuple-element.14), channel_id=1, source_target_pairs={{0,1},{1,0},{2,3},{3,2},{4,5},{5,4},{6,7},{7,6},{8,9},{9,8},{10,11... | collective-permute-start | bytes 1179656 | tf_op jit(solution)/shard_map/ppermute | solution.py:94
  7.8 3.2 %collective-permute-start.3 = (f32[8,8,1536]{2,1,0:T(8,128)S(1)}, f32[8,8,1536]{2,1,0:T(8,128)S(1)}, u32[]{:S(2)}, u32[]{:S(2)}) collective-permute-start(f32[8,8,1536]{2,1,0:T(8,128)S(1)} %get-tuple-element.15), channel_id=1, source_target_pairs={{0,1},{1,0},{2,3},{3,2},{4,5},{5,4},{6,7},{7,6},{8,9},{9,8},{10,11... | collective-permute-start | bytes 1179656 | tf_op jit(solution)/shard_map/ppermute | solution.py:94
  7.9 4.2 %collective-permute-start.5 = (f32[8,8,1536]{2,1,0:T(8,128)S(1)}, f32[8,8,1536]{2,1,0:T(8,128)S(1)}, u32[]{:S(2)}, u32[]{:S(2)}) collective-permute-start(f32[8,8,1536]{2,1,0:T(8,128)S(1)} %get-tuple-element.16), channel_id=1, source_target_pairs={{0,1},{1,0},{2,3},{3,2},{4,5},{5,4},{6,7},{7,6},{8,9},{9,8},{10,11... | collective-permute-start | bytes 1179656 | tf_op jit(solution)/shard_map/ppermute | solution.py:94
  8.3 6.7 %collective-permute-start = (f32[8,8,1536]{2,1,0:T(8,128)S(1)}, f32[8,8,1536]{2,1,0:T(8,128)S(1)}, u32[]{:S(2)}, u32[]{:S(2)}) collective-permute-start(f32[8,8,1536]{2,1,0:T(8,128)S(1)} %get-tuple-element.13), channel_id=1, source_target_pairs={{0,1},{1,0},{2,3},{3,2},{4,5},{5,4},{6,7},{7,6},{8,9},{9,8},{10,11... | collective-permute-start | bytes 1179656 | tf_op jit(solution)/shard_map/ppermute | solution.py:94
  9.7 8.6 %collective-permute-start.2 = (f32[8,8,1536]{2,1,0:T(8,128)S(1)}, f32[8,8,1536]{2,1,0:T(8,128)S(1)}, u32[]{:S(2)}, u32[]{:S(2)}) collective-permute-start(f32[8,8,1536]{2,1,0:T(8,128)S(1)} %join_chunk.5), channel_id=1, source_target_pairs={{0,8},{64,72},{128,136},{192,200},{2,10},{66,74},{130,138},{194,20... | collective-permute-start | bytes 1179656 | tf_op jit(solution)/shard_map/ppermute | solution.py:193
  11.6 10.9 %collective-permute-start.4 = (f32[8,8,1536]{2,1,0:T(8,128)S(1)}, f32[8,8,1536]{2,1,0:T(8,128)S(1)}, u32[]{:S(2)}, u32[]{:S(2)}) collective-permute-start(f32[8,8,1536]{2,1,0:T(8,128)S(1)} %join_chunk.6), channel_id=1, source_target_pairs={{0,16},{64,80},{128,144},{192,208},{2,18},{66,82},{130,146},{194,2... | collective-permute-start | bytes 1179656 | tf_op jit(solution)/shard_map/ppermute | solution.py:193
  12.7 9.8 %collective-permute-start.6 = (f32[8,8,1536]{2,1,0:T(8,128)S(1)}, f32[8,8,1536]{2,1,0:T(8,128)S(1)}, u32[]{:S(2)}, u32[]{:S(2)}) collective-permute-start(f32[8,8,1536]{2,1,0:T(8,128)S(1)} %join_chunk.7), channel_id=1, source_target_pairs={{0,24},{64,88},{128,152},{192,216},{2,26},{66,90},{130,154},{194,2... | collective-permute-start | bytes 1179656 | tf_op jit(solution)/shard_map/ppermute | solution.py:193
  33.3 4.6 %collective-permute-start.7 = (f32[8,1536]{1,0:T(8,128)S(1)}, f32[8,1536]{1,0:T(8,128)S(1)}, u32[]{:S(2)}, u32[]{:S(2)}) collective-permute-start(f32[8,1536]{1,0:T(8,128)S(1)} %reduce_sum.9), channel_id=1, source_target_pairs={{0,64},{2,66},{4,68},{6,70},{16,80},{18,82},{20,84},{22,86},{8,72}... | collective-permute-start | bytes 147464 | tf_op jit(solution)/shard_map/ppermute | solution.py:106
  37.9 6.6 %collective-permute-start.8 = (f32[8,1536]{1,0:T(8,128)S(1)}, f32[8,1536]{1,0:T(8,128)S(1)}, u32[]{:S(2)}, u32[]{:S(2)}) collective-permute-start(f32[8,1536]{1,0:T(8,128)S(1)} %add.164), channel_id=1, source_target_pairs={{0,192},{2,194},{4,196},{6,198},{16,208},{18,210},{20,212},{22,214... | collective-permute-start | bytes 147464 | tf_op jit(solution)/shard_map/ppermute | solution.py:107
  54.4 9.8 %collective-permute-start.13 = (f32[8,8,1536]{2,1,0:T(8,128)S(1)}, f32[8,8,1536]{2,1,0:T(8,128)S(1)}, u32[]{:S(2)}, u32[]{:S(2)}) collective-permute-start(f32[8,8,1536]{2,1,0:T(8,128)S(1)} %all_to_all.11), channel_id=1, source_target_pairs={{0,8},{64,72},{128,136},{192,200},{2,10},{66,74},{130,138},{194,20... | collective-permute-start | bytes 1179656 | tf_op jit(solution)/shard_map/ppermute | solution.py:198
  56.3 12.1 %collective-permute-start.11 = (f32[8,8,1536]{2,1,0:T(8,128)S(1)}, f32[8,8,1536]{2,1,0:T(8,128)S(1)}, u32[]{:S(2)}, u32[]{:S(2)}) collective-permute-start(f32[8,8,1536]{2,1,0:T(8,128)S(1)} %all_to_all.11), channel_id=1, source_target_pairs={{0,24},{64,88},{128,152},{192,216},{2,26},{66,90},{130,154},{194,2... | collective-permute-start | bytes 1179656 | tf_op jit(solution)/shard_map/ppermute | solution.py:198
  57.0 16.1 %collective-permute-start.9 = (f32[8,8,1536]{2,1,0:T(8,128)S(1)}, f32[8,8,1536]{2,1,0:T(8,128)S(1)}, u32[]{:S(2)}, u32[]{:S(2)}) collective-permute-start(f32[8,8,1536]{2,1,0:T(8,128)S(1)} %all_to_all.11), channel_id=1, source_target_pairs={{0,16},{64,80},{128,144},{192,208},{2,18},{66,82},{130,146},{194,2... | collective-permute-start | bytes 1179656 | tf_op jit(solution)/shard_map/ppermute | solution.py:198
  57.7 15.3 %collective-permute-start.14 = (f32[8,8,1536]{2,1,0:T(8,128)S(1)}, f32[8,8,1536]{2,1,0:T(8,128)S(1)}, u32[]{:S(2)}, u32[]{:S(2)}) collective-permute-start(f32[8,8,1536]{2,1,0:T(8,128)S(1)} %all_to_all.11), channel_id=1, source_target_pairs={{0,1},{1,0},{2,3},{3,2},{4,5},{5,4},{6,7},{7,6},{8,9},{9,8},{10,11... | collective-permute-start | bytes 1179656 | tf_op jit(solution)/shard_map/ppermute | solution.py:94
  64.2 8.9 %collective-permute-start.15 = (f32[8,8,1536]{2,1,0:T(8,128)S(1)}, f32[8,8,1536]{2,1,0:T(8,128)S(1)}, u32[]{:S(2)}, u32[]{:S(2)}) collective-permute-start(f32[8,8,1536]{2,1,0:T(8,128)S(1)} %collective-permute-done.13), channel_id=1, source_target_pairs={{0,1},{1,0},{2,3},{3,2},{4,5},{5,4},{6,7},{7,6},{8,9},{9,8},{10,11... | collective-permute-start | bytes 1179656 | tf_op jit(solution)/shard_map/ppermute | solution.py:94
  68.4 7.3 %collective-permute-start.12 = (f32[8,8,1536]{2,1,0:T(8,128)S(1)}, f32[8,8,1536]{2,1,0:T(8,128)S(1)}, u32[]{:S(2)}, u32[]{:S(2)}) collective-permute-start(f32[8,8,1536]{2,1,0:T(8,128)S(1)} %collective-permute-done.11), channel_id=1, source_target_pairs={{0,1},{1,0},{2,3},{3,2},{4,5},{5,4},{6,7},{7,6},{8,9},{9,8},{10,11... | collective-permute-start | bytes 1179656 | tf_op jit(solution)/shard_map/ppermute | solution.py:94
  73.1 2.6 %collective-permute-start.10 = (f32[8,8,1536]{2,1,0:T(8,128)S(1)}, f32[8,8,1536]{2,1,0:T(8,128)S(1)}, u32[]{:S(2)}, u32[]{:S(2)}) collective-permute-start(f32[8,8,1536]{2,1,0:T(8,128)S(1)} %collective-permute-done.9), channel_id=1, source_target_pairs={{0,1},{1,0},{2,3},{3,2},{4,5},{5,4},{6,7},{7,6},{8,9},{9,8},{10,11... | collective-permute-start | bytes 1179656 | tf_op jit(solution)/shard_map/ppermute | solution.py:94

commit v4 on v2

v4 whole, which is shorter than its diff:
```python
import functools

import jax
import jax.numpy as jnp
from jax import lax
from jax.experimental import pallas as pl
from jax.experimental.pallas import tpu as pltpu
from jax.sharding import PartitionSpec as P

bias_one = 0.9999734386011124
bias_two = 0.994079470779666

AXES = ("row", "col")
SHIFT = (0, 0)
WAYS = (2, 1, 3)
SPLIT = 6


def device(x, y, z, core):
    return (z % 8 * 2 + x % 2) * 16 + x // 2 * 8 + y * 2 + core


def place(core, along, pair, across, far):
    x, y = (along, across) if core == 0 else (across, along)
    return device(x, y, 2 * far + pair + SHIFT[core], core)


def ring(change):
    return [
        (place(core, along, pair, across, far), place(core, (along + change) % 4, pair, across, far))
        for core in range(2) for along in range(4) for pair in range(2) for across in range(4) for far in range(4)
    ]


SECOND = [
    [place(core, along, pair, across, far) for across in range(4) for pair in range(2)]
    for core in range(2) for along in range(4) for far in range(4)
]


def far_pairs(change):
    return [
        (device(x, y, 2 * far + pair + SHIFT[core], core), device(x, y, 2 * change(far) + pair + SHIFT[core], core))
        for core in range(2) for far in range(4) for pair in range(2) for x in range(4) for y in range(4)
    ]


PEERS = 32
ROWS, D = 128, 2048
HALF = ROWS // 2
WIDE = D // 4
STEPS = 4
ROOM_A = 60 << 20
ROOM_B = 8 << 20
VMEM = 8 << 20
STEP_ROWS = HALF // STEPS
STEP_PEERS = PEERS // STEPS


def spots():
    row, col = lax.axis_index("row"), lax.axis_index("col")
    core = lax.rem(col, 2)
    x, y = col // 8 * 2 + lax.rem(row, 2), lax.rem(col // 2, 4)
    return core, jnp.where(core == 0, x, y), jnp.where(core == 0, y, x)


def chunk_ahead(d, own):
    core, mine, theirs = spots()
    return core * 4 + lax.rem(mine + d, 4) if own else (1 - core) * 4 + lax.rem(theirs + d, 4)


def place_kernel(which, *refs):
    outs, sems = refs[-4:-1], refs[-1]
    copies = []
    for i, (own, d) in enumerate(which):
        at = chunk_ahead(4 - d, own) * 2
        for k in range(3):
            for g in range(4):
                copies.append(
                    pltpu.make_async_copy(
                        refs[i].at[:, g, :, pl.ds(k * WIDE, WIDE)],
                        outs[k].at[pl.ds(at, 2), :, pl.ds(g * WIDE, WIDE)],
                        sems.at[i, k, g],
                    )
                )
    for copy in copies:
        copy.start()
    for copy in copies:
        copy.wait()


def place_chunks(every, which, before):
    anywhere = pl.BlockSpec(memory_space=pl.ANY)
    chunks = [every[name] for name in which]
    n = len(chunks)
    return pl.pallas_call(
        functools.partial(place_kernel, which),
        in_specs=[anywhere] * (n + len(before)),
        out_specs=[anywhere] * 3,
        out_shape=[jax.ShapeDtypeStruct((ROWS // 8, 8, D), jnp.float32)] * 3,
        scratch_shapes=[pltpu.SemaphoreType.DMA((n, 3, 4))],
        input_output_aliases={n + k: k for k in range(len(before))},
        compiler_params=pltpu.CompilerParams(vmem_limit_bytes=8 << 20),
        name="place_chunks",
    )(*(chunk.reshape(2, 4, 8, 3 * WIDE) for chunk in chunks), *before)


def across_cores(x):
    return lax.ppermute(x, AXES, [(i, i ^ 1) for i in range(256)])


def exchange(x, groups):
    return lax.all_to_all(x, AXES, 0, 0, axis_index_groups=groups, tiled=True)


def repeat(x, groups):
    return jnp.broadcast_to(x[None], (len(groups[0]),) + x.shape)


def far_sum(x):
    x = x + lax.ppermute(x, AXES, far_pairs(lambda far: far ^ 1))
    return x + lax.ppermute(x, AXES, far_pairs(lambda far: far ^ 3))


def adam(arrays):
    old, first, second, gradient = (x[0, 0] for x in arrays)
    first = 0.9 * first + 0.1 * gradient
    second = 0.95 * second + 0.05 * gradient * gradient
    scaled = second * (1.0 / bias_two)
    bottom = bias_one * (scaled * lax.rsqrt(scaled)) + bias_one * 1e-08
    return old - 0.003 * (first / bottom + 0.1 * old), first, second


def lay_kernel(*refs):
    for i in range(len(refs) - 3):

        @pl.when(pl.program_id(0) == i)
        def _():
            for k in range(3):
                for p in range(8):
                    value = refs[k][8 * (p // 4) : 8 * (p // 4) + 8, p % 4 * WIDE : (p % 4 + 1) * WIDE]
                    refs[3 + i][p, :, k * WIDE : (k + 1) * WIDE] = value


def lay_chunks(arrays, own):
    chunk = (8, 8, 3 * WIDE)

    def source(i):
        return chunk_ahead(jnp.where(i == 0, WAYS[0], jnp.where(i == 1, WAYS[1], jnp.where(i == 2, WAYS[2], 0))), own), 0

    return pl.pallas_call(
        lay_kernel,
        grid=(4,),
        in_specs=[pl.BlockSpec((16, D), source)] * 3,
        out_specs=[pl.BlockSpec(chunk, lambda i: (0, 0, 0))] * 4,
        out_shape=[jax.ShapeDtypeStruct(chunk, jnp.float32)] * 4,
        compiler_params=pltpu.CompilerParams(vmem_limit_bytes=12 << 20),
        name="lay_chunks",
    )(*arrays)


def on_device(*arrays):
    arrays = adam(arrays)
    received = [across_cores(chunk) for chunk in lay_chunks(arrays, False)]
    sums = [own + theirs for own, theirs in zip(lay_chunks(arrays, True), received)]
    other = [lax.ppermute(chunk, AXES, ring(d)) for chunk, d in zip(sums, WAYS)]
    mine = (sums[3] + other[0]) + (other[1] + other[2])
    mine = jnp.sum(exchange(mine, SECOND), axis=0)
    mine = far_sum(mine) * (1.0 / 256.0)
    mine = exchange(repeat(mine, SECOND), SECOND)
    chunks = {(True, 0): mine}
    chunks.update({(True, d): lax.ppermute(mine, AXES, ring(d)) for d in WAYS})
    chunks.update({(False, d): across_cores(chunks[True, d]) for d in (0,) + WAYS})
    names = [(own, d) for own in (True, False) for d in (0,) + WAYS]
    outs = place_chunks(chunks, names[:SPLIT], ())
    outs = place_chunks(chunks, names[SPLIT:], outs)
    return tuple(out.reshape(ROWS, D) for out in outs)


def solution(mesh):
    spec = P("row", "col", None, None)
    return jax.shard_map(on_device, mesh=mesh, in_specs=(spec,) * 4, out_specs=(P(),) * 3, check_vma=False)
```

time: 79.4 us -> 75.1 us (0.946)
  Pallas kernels: 6.79 us -> 3.73 us
  other arithmetic: 5.08 us -> 3.12 us
  starting transfers between devices: 32.4 us -> 34.3 us
  waiting for transfers between devices: 13.6 us -> 12 us
    pallas_call x6 -> x4, Pallas kernels: 6.79 us -> 3.73 us  [the longest x2 3.14 us: place_chunks(): pl.pallas_call(functools.partial(place_kernel, which), in_specs=[anywhere...]
    sub x2 -> x1, other arithmetic: 4.74 us -> 2.83 us  [adam(): return (old - 0.003 * (first / bottom + 0.1 * old), first, second)]
    ppermute x6, starting transfers between devices: 5.69 us -> 6.98 us  [the longest x3 4.1 us: on_device(): other = [lax.ppermute(chunk, AXES, ring(d)) for chunk, d in zip(sums, WAYS)]]
    ppermute x7 -> x8, starting transfers between devices: 19 us -> 19.6 us  [across_cores(): return lax.ppermute(x, AXES, [(i, i ^ 1) for i in range(256)])]
  transfers between devices with their start and end apart: 15 -> 16, of which waited for: 7 -> 5; matrix products, arithmetic and copies ran while one was open for 3% -> 0% of each run, Pallas kernels for 7% -> 3%
where the time goes in v4:
time: 75.1 us; the launch traced here: 74.8 us
  starting transfers between devices  34.3 us (46%)
  blocking collectives  20.9 us (28%)
  waiting for transfers between devices  12 us (16%)
  Pallas kernels  3.73 us (5%)
  other arithmetic  3.12 us (4%)
    all_to_all x2, blocking collectives, exchange(): return lax.all_to_all(x, AXES, 0, 0, axis_index_groups=groups, tiled=True)  20.9 us
    ppermute x8, starting transfers between devices, across_cores(): return lax.ppermute(x, AXES, [(i, i ^ 1) for i in range(256)])  19.6 us
    ppermute x3, waiting for transfers between devices, on_device(): other = [lax.ppermute(chunk, AXES, ring(d)) for chunk, d in zip(sums, WAYS)]  8.52 us
    ppermute x1, starting transfers between devices, far_sum(): return x + lax.ppermute(x, AXES, far_pairs(lambda far: far ^ 3))  4.58 us
    ppermute x3, starting transfers between devices, on_device(): other = [lax.ppermute(chunk, AXES, ring(d)) for chunk, d in zip(sums, WAYS)]  4.1 us
    pallas_call x2, Pallas kernels, place_chunks(): pl.pallas_call(functools.partial(place_kernel, which), in_specs=[anywhere...  3.14 us
    ppermute x1, starting transfers between devices, far_sum(): x = x + lax.ppermute(x, AXES, far_pairs(lambda far: far ^ 1))  3.08 us
    ppermute x3, starting transfers between devices, on_device(): chunks.update({(True, d): lax.ppermute(mine, AXES, ring(d)) for d in WAYS})  2.89 us
  transfers between devices with their start and end apart: 16, of which 5 were waited for; matrix products, arithmetic and copies ran while one was open for 0% of the time, Pallas kernels for 3%

profile of v4, /device:TPU:1, one launch (start us, length us, event | category | flops | bytes accessed | tf_op | source)
XLA Modules:
  0.0 74.8 jit_solution(10248443360463256315)
XLA Ops:
  0.6 2.8 %fusion.6 = (f32[128,2048]{1,0:T(8,128)S(1)}, f32[128,2048]{1,0:T(8,128)S(1)}, f32[128,2048]{1,0:T(8,128)S(1)}) fusion(f32[1,1,128,2048]{3,2,1,0:T(8,128)} %param.4, f32[1,1,128,2048]{3,2,1,0:T(8,128)} %param.7, f32[1,1,128,2048]{3,2,1,0:T(8,128)} %param.6, f32[1,1,128,2048]{3,2,1,0:T(8,128)} %param.5), kind=kLoop, calls=%fused_computation.8 | loop fusion | flops 4194304 | bytes 7340032 | tf_op jit(solution)/shard_map/sub | solution.py:131
  3.5 0.3 lay_chunks.3
  3.8 3.3 %collective-permute-start.1 = (f32[8,8,1536]{2,1,0:T(8,128)S(1)}, f32[8,8,1536]{2,1,0:T(8,128)S(1)}, u32[]{:S(2)}, u32[]{:S(2)}) collective-permute-start(f32[8,8,1536]{2,1,0:T(8,128)S(1)} %get-tuple-element.20), channel_id=1, source_target_pairs={{0,1},{1,0},{2,3},{3,2},{4,5},{5,4},{6,7},{7,6},{8,9},{9,8},{10,11... | collective-permute-start | bytes 1179656 | tf_op jit(solution)/shard_map/ppermute | solution.py:109
  7.1 0.1 collective-permute-start.3
  7.2 0.4 collective-permute-start.5
  7.6 0.1 collective-permute-start
  7.7 0.3 lay_chunks.2
  8.0 0.5 collective-permute-done.1
  8.5 1.3 %collective-permute-start.2 = (f32[8,8,1536]{2,1,0:T(8,128)S(1)}, f32[8,8,1536]{2,1,0:T(8,128)S(1)}, u32[]{:S(2)}, u32[]{:S(2)}) collective-permute-start(f32[8,8,1536]{2,1,0:T(8,128)S(1)} %add.48), channel_id=1, source_target_pairs={{0,8},{64,72},{128,136},{192,200},{2,10},{66,74},{130,138},{194,20... | collective-permute-start | bytes 1179656 | tf_op jit(solution)/shard_map/ppermute | solution.py:166
  9.8 0.0 collective-permute-done.3
  9.8 0.5 collective-permute-start.4
  10.3 0.0 collective-permute-done.5
  10.3 0.1 add.51
  10.4 2.4 %collective-permute-start.6 = (f32[8,8,1536]{2,1,0:T(8,128)S(1)}, f32[8,8,1536]{2,1,0:T(8,128)S(1)}, u32[]{:S(2)}, u32[]{:S(2)}) collective-permute-start(f32[8,8,1536]{2,1,0:T(8,128)S(1)} %add.51), channel_id=1, source_target_pairs={{0,24},{64,88},{128,152},{192,216},{2,26},{66,90},{130,154},{194,2... | collective-permute-start | bytes 1179656 | tf_op jit(solution)/shard_map/ppermute | solution.py:166
  12.7 0.0 collective-permute-done
  12.7 4.3 %collective-permute-done.2 = f32[8,8,1536]{2,1,0:T(8,128)S(1)} collective-permute-done((f32[8,8,1536]{2,1,0:T(8,128)S(1)}, f32[8,8,1536]{2,1,0:T(8,128)S(1)}, u32[]{:S(2)}, u32[]{:S(2)}) %collective-permute-start.2) | collective-permute-done | bytes 393248 | tf_op jit(solution)/shard_map/ppermute | solution.py:166
  17.1 4.2 %collective-permute-done.4 = f32[8,8,1536]{2,1,0:T(8,128)S(1)} collective-permute-done((f32[8,8,1536]{2,1,0:T(8,128)S(1)}, f32[8,8,1536]{2,1,0:T(8,128)S(1)}, u32[]{:S(2)}, u32[]{:S(2)}) %collective-permute-start.4) | collective-permute-done | bytes 393248 | tf_op jit(solution)/shard_map/ppermute | solution.py:166
  21.2 0.0 collective-permute-done.6
  21.2 0.1 add_add_fusion
  21.4 10.7 %all_to_all.10 = f32[8,8,1536]{2,1,0:T(8,128)S(1)} all-to-all(f32[8,8,1536]{2,1,0:T(8,128)S(1)} %add_add_fusion), channel_id=1, replica_groups={{0,32,2,34,4,36,6,38},{64,96,66,98,68,100,70,102},{128,160,130,162,132,..., dimensions={0} | all-to-all | bytes 786432 | tf_op jit(solution)/shard_map/all_to_all | solution.py:113
  32.0 3.1 %collective-permute-start.7 = (f32[8,1536]{1,0:T(8,128)S(1)}, f32[8,1536]{1,0:T(8,128)S(1)}, u32[]{:S(2)}, u32[]{:S(2)}) collective-permute-start(f32[8,1536]{1,0:T(8,128)S(1)} %reduce_sum.9), channel_id=1, source_target_pairs={{0,64},{2,66},{4,68},{6,70},{16,80},{18,82},{20,84},{22,86},{8,72}... | collective-permute-start | bytes 147464 | tf_op jit(solution)/shard_map/ppermute | solution.py:121
  35.1 1.5 %collective-permute-done.7 = f32[8,1536]{1,0:T(8,128)S(1)} collective-permute-done((f32[8,1536]{1,0:T(8,128)S(1)}, f32[8,1536]{1,0:T(8,128)S(1)}, u32[]{:S(2)}, u32[]{:S(2)}) %collective-permute-start.7) | collective-permute-done | bytes 49184 | tf_op jit(solution)/shard_map/ppermute | solution.py:121
  36.6 4.6 %collective-permute-start.8 = (f32[8,1536]{1,0:T(8,128)S(1)}, f32[8,1536]{1,0:T(8,128)S(1)}, u32[]{:S(2)}, u32[]{:S(2)}) collective-permute-start(f32[8,1536]{1,0:T(8,128)S(1)} %add.54), channel_id=1, source_target_pairs={{0,192},{2,194},{4,196},{6,198},{16,208},{18,210},{20,212},{22,214... | collective-permute-start | bytes 147464 | tf_op jit(solution)/shard_map/ppermute | solution.py:122
  41.2 1.5 %collective-permute-done.8 = f32[8,1536]{1,0:T(8,128)S(1)} collective-permute-done((f32[8,1536]{1,0:T(8,128)S(1)}, f32[8,1536]{1,0:T(8,128)S(1)}, u32[]{:S(2)}, u32[]{:S(2)}) %collective-permute-start.8) | collective-permute-done | bytes 49184 | tf_op jit(solution)/shard_map/ppermute | solution.py:122
  42.7 10.2 %all_to_all.11 = f32[8,8,1536]{2,1,0:T(8,128)S(1)} all-to-all(f32[8,8,1536]{2,1,0:T(8,128)S(1)} %broadcast_in_dim.2), channel_id=1, replica_groups={{0,32,2,34,4,36,6,38},{64,96,66,98,68,100,70,102},{128,160,130,162,132,..., dimensions={0} | all-to-all | bytes 786432 | tf_op jit(solution)/shard_map/all_to_all | solution.py:113
  53.0 1.1 %collective-permute-start.13 = (f32[8,8,1536]{2,1,0:T(8,128)S(1)}, f32[8,8,1536]{2,1,0:T(8,128)S(1)}, u32[]{:S(2)}, u32[]{:S(2)}) collective-permute-start(f32[8,8,1536]{2,1,0:T(8,128)S(1)} %all_to_all.11), channel_id=1, source_target_pairs={{0,8},{64,72},{128,136},{192,200},{2,10},{66,74},{130,138},{194,20... | collective-permute-start | bytes 1179656 | tf_op jit(solution)/shard_map/ppermute | solution.py:172
  54.0 1.8 %collective-permute-start.11 = (f32[8,8,1536]{2,1,0:T(8,128)S(1)}, f32[8,8,1536]{2,1,0:T(8,128)S(1)}, u32[]{:S(2)}, u32[]{:S(2)}) collective-permute-start(f32[8,8,1536]{2,1,0:T(8,128)S(1)} %all_to_all.11), channel_id=1, source_target_pairs={{0,24},{64,88},{128,152},{192,216},{2,26},{66,90},{130,154},{194,2... | collective-permute-start | bytes 1179656 | tf_op jit(solution)/shard_map/ppermute | solution.py:172
  55.9 0.0 collective-permute-start.9
  55.9 7.0 %collective-permute-start.14 = (f32[8,8,1536]{2,1,0:T(8,128)S(1)}, f32[8,8,1536]{2,1,0:T(8,128)S(1)}, u32[]{:S(2)}, u32[]{:S(2)}) collective-permute-start(f32[8,8,1536]{2,1,0:T(8,128)S(1)} %all_to_all.11), channel_id=1, source_target_pairs={{0,1},{1,0},{2,3},{3,2},{4,5},{5,4},{6,7},{7,6},{8,9},{9,8},{10,11... | collective-permute-start | bytes 1179656 | tf_op jit(solution)/shard_map/ppermute | solution.py:109
  62.9 0.0 collective-permute-done.13
  62.9 4.5 %collective-permute-start.15 = (f32[8,8,1536]{2,1,0:T(8,128)S(1)}, f32[8,8,1536]{2,1,0:T(8,128)S(1)}, u32[]{:S(2)}, u32[]{:S(2)}) collective-permute-start(f32[8,8,1536]{2,1,0:T(8,128)S(1)} %collective-permute-done.13), channel_id=1, source_target_pairs={{0,1},{1,0},{2,3},{3,2},{4,5},{5,4},{6,7},{7,6},{8,9},{9,8},{10,11... | collective-permute-start | bytes 1179656 | tf_op jit(solution)/shard_map/ppermute | solution.py:109
  67.4 0.0 collective-permute-done.11
  67.4 4.2 %collective-permute-start.12 = (f32[8,8,1536]{2,1,0:T(8,128)S(1)}, f32[8,8,1536]{2,1,0:T(8,128)S(1)}, u32[]{:S(2)}, u32[]{:S(2)}) collective-permute-start(f32[8,8,1536]{2,1,0:T(8,128)S(1)} %collective-permute-done.11), channel_id=1, source_target_pairs={{0,1},{1,0},{2,3},{3,2},{4,5},{5,4},{6,7},{7,6},{8,9},{9,8},{10,11... | collective-permute-start | bytes 1179656 | tf_op jit(solution)/shard_map/ppermute | solution.py:109
  71.6 0.0 collective-permute-done.9
  71.6 0.0 collective-permute-start.10
  71.6 0.0 collective-permute-done.14
  71.6 0.0 collective-permute-done.15
  71.6 2.0 %place_chunks.2 = (f32[16,8,2048]{2,1,0:T(8,128)}, f32[16,8,2048]{2,1,0:T(8,128)}, f32[16,8,2048]{2,1,0:T(8,128)}) custom-call(f32[2,4,8,1536]{3,2,1,0:T(8,128)S(1)} %bitcast.29, f32[2,4,8,1536]{3,2,1,0:T(8,128)S(1)} %bitcast.30, f32[2,4,8,1536]{3,2,1,0:T(8,128)S(1)} %bitcast.32, f32[2,4,8,1536]{3,2,1,0:T(8,128)S(1)} %bitcast.31, ...), custom_call_target="tpu_custom_call" | custom-call | tf_op jit(solution)/shard_map/place_chunks/pallas_call | solution.py:96
  73.6 0.0 collective-permute-done.12
  73.7 0.0 collective-permute-done.10
  73.7 1.1 %place_chunks.3 = (f32[16,8,2048]{2,1,0:T(8,128)}, f32[16,8,2048]{2,1,0:T(8,128)}, f32[16,8,2048]{2,1,0:T(8,128)}) custom-call(f32[2,4,8,1536]{3,2,1,0:T(8,128)S(1)} %bitcast.36, f32[2,4,8,1536]{3,2,1,0:T(8,128)S(1)} %bitcast.35, f32[16,8,2048]{2,1,0:T(8,128)} %get-tuple-element.25.refs_2_, ...), custom_call_target="tpu_custom_call", output_to_operand_aliasing={{0}: (2, {}), {1}: (3, {}), {2}: (4, {})} | custom-call | tf_op jit(solution)/shard_map/place_chunks/pallas_call | solution.py:96
  (6 shorter events, 0.2 us)
Async XLA Ops:
  3.8 4.7 %collective-permute-start.1 = (f32[8,8,1536]{2,1,0:T(8,128)S(1)}, f32[8,8,1536]{2,1,0:T(8,128)S(1)}, u32[]{:S(2)}, u32[]{:S(2)}) collective-permute-start(f32[8,8,1536]{2,1,0:T(8,128)S(1)} %get-tuple-element.20), channel_id=1, source_target_pairs={{0,1},{1,0},{2,3},{3,2},{4,5},{5,4},{6,7},{7,6},{8,9},{9,8},{10,11... | collective-permute-start | bytes 1179656 | tf_op jit(solution)/shard_map/ppermute | solution.py:109
  7.1 2.7 %collective-permute-start.3 = (f32[8,8,1536]{2,1,0:T(8,128)S(1)}, f32[8,8,1536]{2,1,0:T(8,128)S(1)}, u32[]{:S(2)}, u32[]{:S(2)}) collective-permute-start(f32[8,8,1536]{2,1,0:T(8,128)S(1)} %get-tuple-element.22), channel_id=1, source_target_pairs={{0,1},{1,0},{2,3},{3,2},{4,5},{5,4},{6,7},{7,6},{8,9},{9,8},{10,11... | collective-permute-start | bytes 1179656 | tf_op jit(solution)/shard_map/ppermute | solution.py:109
  7.2 3.1 %collective-permute-start.5 = (f32[8,8,1536]{2,1,0:T(8,128)S(1)}, f32[8,8,1536]{2,1,0:T(8,128)S(1)}, u32[]{:S(2)}, u32[]{:S(2)}) collective-permute-start(f32[8,8,1536]{2,1,0:T(8,128)S(1)} %get-tuple-element.24), channel_id=1, source_target_pairs={{0,1},{1,0},{2,3},{3,2},{4,5},{5,4},{6,7},{7,6},{8,9},{9,8},{10,11... | collective-permute-start | bytes 1179656 | tf_op jit(solution)/shard_map/ppermute | solution.py:109
  7.6 5.1 %collective-permute-start = (f32[8,8,1536]{2,1,0:T(8,128)S(1)}, f32[8,8,1536]{2,1,0:T(8,128)S(1)}, u32[]{:S(2)}, u32[]{:S(2)}) collective-permute-start(f32[8,8,1536]{2,1,0:T(8,128)S(1)} %get-tuple-element.18), channel_id=1, source_target_pairs={{0,1},{1,0},{2,3},{3,2},{4,5},{5,4},{6,7},{7,6},{8,9},{9,8},{10,11... | collective-permute-start | bytes 1179656 | tf_op jit(solution)/shard_map/ppermute | solution.py:109
  8.5 8.6 %collective-permute-start.2 = (f32[8,8,1536]{2,1,0:T(8,128)S(1)}, f32[8,8,1536]{2,1,0:T(8,128)S(1)}, u32[]{:S(2)}, u32[]{:S(2)}) collective-permute-start(f32[8,8,1536]{2,1,0:T(8,128)S(1)} %add.48), channel_id=1, source_target_pairs={{0,8},{64,72},{128,136},{192,200},{2,10},{66,74},{130,138},{194,20... | collective-permute-start | bytes 1179656 | tf_op jit(solution)/shard_map/ppermute | solution.py:166
  9.8 11.4 %collective-permute-start.4 = (f32[8,8,1536]{2,1,0:T(8,128)S(1)}, f32[8,8,1536]{2,1,0:T(8,128)S(1)}, u32[]{:S(2)}, u32[]{:S(2)}) collective-permute-start(f32[8,8,1536]{2,1,0:T(8,128)S(1)} %add.50), channel_id=1, source_target_pairs={{0,16},{64,80},{128,144},{192,208},{2,18},{66,82},{130,146},{194,2... | collective-permute-start | bytes 1179656 | tf_op jit(solution)/shard_map/ppermute | solution.py:166
  10.4 10.9 %collective-permute-start.6 = (f32[8,8,1536]{2,1,0:T(8,128)S(1)}, f32[8,8,1536]{2,1,0:T(8,128)S(1)}, u32[]{:S(2)}, u32[]{:S(2)}) collective-permute-start(f32[8,8,1536]{2,1,0:T(8,128)S(1)} %add.51), channel_id=1, source_target_pairs={{0,24},{64,88},{128,152},{192,216},{2,26},{66,90},{130,154},{194,2... | collective-permute-start | bytes 1179656 | tf_op jit(solution)/shard_map/ppermute | solution.py:166
  32.0 4.6 %collective-permute-start.7 = (f32[8,1536]{1,0:T(8,128)S(1)}, f32[8,1536]{1,0:T(8,128)S(1)}, u32[]{:S(2)}, u32[]{:S(2)}) collective-permute-start(f32[8,1536]{1,0:T(8,128)S(1)} %reduce_sum.9), channel_id=1, source_target_pairs={{0,64},{2,66},{4,68},{6,70},{16,80},{18,82},{20,84},{22,86},{8,72}... | collective-permute-start | bytes 147464 | tf_op jit(solution)/shard_map/ppermute | solution.py:121
  36.6 6.1 %collective-permute-start.8 = (f32[8,1536]{1,0:T(8,128)S(1)}, f32[8,1536]{1,0:T(8,128)S(1)}, u32[]{:S(2)}, u32[]{:S(2)}) collective-permute-start(f32[8,1536]{1,0:T(8,128)S(1)} %add.54), channel_id=1, source_target_pairs={{0,192},{2,194},{4,196},{6,198},{16,208},{18,210},{20,212},{22,214... | collective-permute-start | bytes 147464 | tf_op jit(solution)/shard_map/ppermute | solution.py:122
  53.0 9.9 %collective-permute-start.13 = (f32[8,8,1536]{2,1,0:T(8,128)S(1)}, f32[8,8,1536]{2,1,0:T(8,128)S(1)}, u32[]{:S(2)}, u32[]{:S(2)}) collective-permute-start(f32[8,8,1536]{2,1,0:T(8,128)S(1)} %all_to_all.11), channel_id=1, source_target_pairs={{0,8},{64,72},{128,136},{192,200},{2,10},{66,74},{130,138},{194,20... | collective-permute-start | bytes 1179656 | tf_op jit(solution)/shard_map/ppermute | solution.py:172
  54.0 13.3 %collective-permute-start.11 = (f32[8,8,1536]{2,1,0:T(8,128)S(1)}, f32[8,8,1536]{2,1,0:T(8,128)S(1)}, u32[]{:S(2)}, u32[]{:S(2)}) collective-permute-start(f32[8,8,1536]{2,1,0:T(8,128)S(1)} %all_to_all.11), channel_id=1, source_target_pairs={{0,24},{64,88},{128,152},{192,216},{2,26},{66,90},{130,154},{194,2... | collective-permute-start | bytes 1179656 | tf_op jit(solution)/shard_map/ppermute | solution.py:172
  55.9 15.7 %collective-permute-start.9 = (f32[8,8,1536]{2,1,0:T(8,128)S(1)}, f32[8,8,1536]{2,1,0:T(8,128)S(1)}, u32[]{:S(2)}, u32[]{:S(2)}) collective-permute-start(f32[8,8,1536]{2,1,0:T(8,128)S(1)} %all_to_all.11), channel_id=1, source_target_pairs={{0,16},{64,80},{128,144},{192,208},{2,18},{66,82},{130,146},{194,2... | collective-permute-start | bytes 1179656 | tf_op jit(solution)/shard_map/ppermute | solution.py:172
  55.9 15.7 %collective-permute-start.14 = (f32[8,8,1536]{2,1,0:T(8,128)S(1)}, f32[8,8,1536]{2,1,0:T(8,128)S(1)}, u32[]{:S(2)}, u32[]{:S(2)}) collective-permute-start(f32[8,8,1536]{2,1,0:T(8,128)S(1)} %all_to_all.11), channel_id=1, source_target_pairs={{0,1},{1,0},{2,3},{3,2},{4,5},{5,4},{6,7},{7,6},{8,9},{9,8},{10,11... | collective-permute-start | bytes 1179656 | tf_op jit(solution)/shard_map/ppermute | solution.py:109
  62.9 8.7 %collective-permute-start.15 = (f32[8,8,1536]{2,1,0:T(8,128)S(1)}, f32[8,8,1536]{2,1,0:T(8,128)S(1)}, u32[]{:S(2)}, u32[]{:S(2)}) collective-permute-start(f32[8,8,1536]{2,1,0:T(8,128)S(1)} %collective-permute-done.13), channel_id=1, source_target_pairs={{0,1},{1,0},{2,3},{3,2},{4,5},{5,4},{6,7},{7,6},{8,9},{9,8},{10,11... | collective-permute-start | bytes 1179656 | tf_op jit(solution)/shard_map/ppermute | solution.py:109
  67.4 6.3 %collective-permute-start.12 = (f32[8,8,1536]{2,1,0:T(8,128)S(1)}, f32[8,8,1536]{2,1,0:T(8,128)S(1)}, u32[]{:S(2)}, u32[]{:S(2)}) collective-permute-start(f32[8,8,1536]{2,1,0:T(8,128)S(1)} %collective-permute-done.11), channel_id=1, source_target_pairs={{0,1},{1,0},{2,3},{3,2},{4,5},{5,4},{6,7},{7,6},{8,9},{9,8},{10,11... | collective-permute-start | bytes 1179656 | tf_op jit(solution)/shard_map/ppermute | solution.py:109
  71.6 2.1 %collective-permute-start.10 = (f32[8,8,1536]{2,1,0:T(8,128)S(1)}, f32[8,8,1536]{2,1,0:T(8,128)S(1)}, u32[]{:S(2)}, u32[]{:S(2)}) collective-permute-start(f32[8,8,1536]{2,1,0:T(8,128)S(1)} %collective-permute-done.9), channel_id=1, source_target_pairs={{0,1},{1,0},{2,3},{3,2},{4,5},{5,4},{6,7},{7,6},{8,9},{9,8},{10,11... | collective-permute-start | bytes 1179656 | tf_op jit(solution)/shard_map/ppermute | solution.py:109

commit v5 on v4

--- a/solution.py
+++ b/solution.py
@@ -13,6 +13,7 @@
 AXES = ("row", "col")
 SHIFT = (0, 0)
 WAYS = (2, 1, 3)
+BACK = (1, 3, 2)
 SPLIT = 6
 
 
@@ -169,11 +170,14 @@
     mine = far_sum(mine) * (1.0 / 256.0)
     mine = exchange(repeat(mine, SECOND), SECOND)
     chunks = {(True, 0): mine}
-    chunks.update({(True, d): lax.ppermute(mine, AXES, ring(d)) for d in WAYS})
-    chunks.update({(False, d): across_cores(chunks[True, d]) for d in (0,) + WAYS})
-    names = [(own, d) for own in (True, False) for d in (0,) + WAYS]
-    outs = place_chunks(chunks, names[:SPLIT], ())
-    outs = place_chunks(chunks, names[SPLIT:], outs)
+    chunks.update({(True, d): lax.ppermute(mine, AXES, ring(d)) for d in BACK})
+    first, second, last = BACK
+    chunks[False, 0], chunks[False, first] = across_cores(mine), across_cores(chunks[True, first])
+    outs = place_chunks(chunks, [(True, 0), (True, first)], ())
+    chunks[True, second], outs = lax.optimization_barrier((chunks[True, second], outs))
+    chunks[False, second], chunks[False, last] = across_cores(chunks[True, second]), across_cores(chunks[True, last])
+    outs = place_chunks(chunks, [(True, second), (True, last), (False, 0), (False, first)], outs)
+    outs = place_chunks(chunks, [(False, second), (False, last)], outs)
     return tuple(out.reshape(ROWS, D) for out in outs)
 
 

time: 75.1 us -> 75 us (level)
  starting transfers between devices: 34.3 us -> 31.7 us
  waiting for transfers between devices: 12 us -> 14.2 us
    ppermute x8, starting transfers between devices: 19.6 us -> 18.3 us  [across_cores(): return lax.ppermute(x, AXES, [(i, i ^ 1) for i in range(256)])]
    ppermute x3, starting transfers between devices: 4.1 us -> 2.89 us  [on_device(): other = [lax.ppermute(chunk, AXES, ring(d)) for chunk, d in zip(sums, WAYS)]]
    ppermute x3, waiting for transfers between devices: 8.52 us -> 9.72 us  [on_device(): other = [lax.ppermute(chunk, AXES, ring(d)) for chunk, d in zip(sums, WAYS)]]
    pallas_call x2 -> x3, Pallas kernels: 3.14 us -> 3.71 us  [place_chunks(): pl.pallas_call(functools.partial(place_kernel, which), in_specs=[anywhere...]
  transfers between devices with their start and end apart: 16 -> 16, of which waited for: 5 -> 6; matrix products, arithmetic and copies ran while one was open for 0% -> 0% of each run, Pallas kernels for 3% -> 4%
where the time goes in v5:
time: 75 us; the launch traced here: 74.8 us
  starting transfers between devices  31.7 us (42%)
  blocking collectives  20.7 us (28%)
  waiting for transfers between devices  14.2 us (19%)
  Pallas kernels  4.3 us (6%)
  other arithmetic  3.12 us (4%)
    all_to_all x2, blocking collectives, exchange(): return lax.all_to_all(x, AXES, 0, 0, axis_index_groups=groups, tiled=True)  20.7 us
    ppermute x8, starting transfers between devices, across_cores(): return lax.ppermute(x, AXES, [(i, i ^ 1) for i in range(256)])  18.3 us
    ppermute x3, waiting for transfers between devices, on_device(): other = [lax.ppermute(chunk, AXES, ring(d)) for chunk, d in zip(sums, WAYS)]  9.72 us
    ppermute x1, starting transfers between devices, far_sum(): return x + lax.ppermute(x, AXES, far_pairs(lambda far: far ^ 3))  4.04 us
    pallas_call x3, Pallas kernels, place_chunks(): pl.pallas_call(functools.partial(place_kernel, which), in_specs=[anywhere...  3.71 us
    ppermute x3, starting transfers between devices, on_device(): chunks.update({(True, d): lax.ppermute(mine, AXES, ring(d)) for d in BACK})  3.39 us
    ppermute x1, starting transfers between devices, far_sum(): x = x + lax.ppermute(x, AXES, far_pairs(lambda far: far ^ 1))  3.08 us
    ppermute x3, starting transfers between devices, on_device(): other = [lax.ppermute(chunk, AXES, ring(d)) for chunk, d in zip(sums, WAYS)]  2.89 us
  transfers between devices with their start and end apart: 16, of which 6 were waited for; matrix products, arithmetic and copies ran while one was open for 0% of the time, Pallas kernels for 4%

profile of v5, /device:TPU:1, one launch (start us, length us, event | category | flops | bytes accessed | tf_op | source)
XLA Modules:
  0.0 74.8 jit_solution(18056087716088109033)
XLA Ops:
  0.6 2.8 %fusion.6 = (f32[128,2048]{1,0:T(8,128)S(1)}, f32[128,2048]{1,0:T(8,128)S(1)}, f32[128,2048]{1,0:T(8,128)S(1)}) fusion(f32[1,1,128,2048]{3,2,1,0:T(8,128)} %param.4, f32[1,1,128,2048]{3,2,1,0:T(8,128)} %param.7, f32[1,1,128,2048]{3,2,1,0:T(8,128)} %param.6, f32[1,1,128,2048]{3,2,1,0:T(8,128)} %param.5), kind=kLoop, calls=%fused_computation.8 | loop fusion | flops 4194304 | bytes 7340032 | tf_op jit(solution)/shard_map/sub | solution.py:132
  3.5 0.3 lay_chunks.3
  3.8 3.3 %collective-permute-start.1 = (f32[8,8,1536]{2,1,0:T(8,128)S(1)}, f32[8,8,1536]{2,1,0:T(8,128)S(1)}, u32[]{:S(2)}, u32[]{:S(2)}) collective-permute-start(f32[8,8,1536]{2,1,0:T(8,128)S(1)} %get-tuple-element.27), channel_id=1, source_target_pairs={{0,1},{1,0},{2,3},{3,2},{4,5},{5,4},{6,7},{7,6},{8,9},{9,8},{10,11... | collective-permute-start | bytes 1179656 | tf_op jit(solution)/shard_map/ppermute | solution.py:110
  7.1 0.1 collective-permute-start.5
  7.2 0.4 collective-permute-start.3
  7.6 0.1 collective-permute-start
  7.7 0.3 lay_chunks.2
  8.0 0.5 collective-permute-done.1
  8.5 1.3 %collective-permute-start.2 = (f32[8,8,1536]{2,1,0:T(8,128)S(1)}, f32[8,8,1536]{2,1,0:T(8,128)S(1)}, u32[]{:S(2)}, u32[]{:S(2)}) collective-permute-start(f32[8,8,1536]{2,1,0:T(8,128)S(1)} %add.48), channel_id=1, source_target_pairs={{0,8},{64,72},{128,136},{192,200},{2,10},{66,74},{130,138},{194,20... | collective-permute-start | bytes 1179656 | tf_op jit(solution)/shard_map/ppermute | solution.py:167
  9.8 0.0 collective-permute-done.5
  9.8 0.9 %collective-permute-start.6 = (f32[8,8,1536]{2,1,0:T(8,128)S(1)}, f32[8,8,1536]{2,1,0:T(8,128)S(1)}, u32[]{:S(2)}, u32[]{:S(2)}) collective-permute-start(f32[8,8,1536]{2,1,0:T(8,128)S(1)} %add.51), channel_id=1, source_target_pairs={{0,24},{64,88},{128,152},{192,216},{2,26},{66,90},{130,154},{194,2... | collective-permute-start | bytes 1179656 | tf_op jit(solution)/shard_map/ppermute | solution.py:167
  10.7 0.0 collective-permute-done.3
  10.7 0.1 add.50
  10.7 0.8 %collective-permute-start.4 = (f32[8,8,1536]{2,1,0:T(8,128)S(1)}, f32[8,8,1536]{2,1,0:T(8,128)S(1)}, u32[]{:S(2)}, u32[]{:S(2)}) collective-permute-start(f32[8,8,1536]{2,1,0:T(8,128)S(1)} %add.50), channel_id=1, source_target_pairs={{0,16},{64,80},{128,144},{192,208},{2,18},{66,82},{130,146},{194,2... | collective-permute-start | bytes 1179656 | tf_op jit(solution)/shard_map/ppermute | solution.py:167
  11.5 0.0 collective-permute-done
  11.5 5.6 %collective-permute-done.2 = f32[8,8,1536]{2,1,0:T(8,128)S(1)} collective-permute-done((f32[8,8,1536]{2,1,0:T(8,128)S(1)}, f32[8,8,1536]{2,1,0:T(8,128)S(1)}, u32[]{:S(2)}, u32[]{:S(2)}) %collective-permute-start.2) | collective-permute-done | bytes 393248 | tf_op jit(solution)/shard_map/ppermute | solution.py:167
  17.1 2.8 %collective-permute-done.6 = f32[8,8,1536]{2,1,0:T(8,128)S(1)} collective-permute-done((f32[8,8,1536]{2,1,0:T(8,128)S(1)}, f32[8,8,1536]{2,1,0:T(8,128)S(1)}, u32[]{:S(2)}, u32[]{:S(2)}) %collective-permute-start.6) | collective-permute-done | bytes 393248 | tf_op jit(solution)/shard_map/ppermute | solution.py:167
  19.9 1.4 %collective-permute-done.4 = f32[8,8,1536]{2,1,0:T(8,128)S(1)} collective-permute-done((f32[8,8,1536]{2,1,0:T(8,128)S(1)}, f32[8,8,1536]{2,1,0:T(8,128)S(1)}, u32[]{:S(2)}, u32[]{:S(2)}) %collective-permute-start.4) | collective-permute-done | bytes 393248 | tf_op jit(solution)/shard_map/ppermute | solution.py:167
  21.2 0.1 add_add_fusion
  21.3 11.2 %all_to_all.10 = f32[8,8,1536]{2,1,0:T(8,128)S(1)} all-to-all(f32[8,8,1536]{2,1,0:T(8,128)S(1)} %add_add_fusion), channel_id=1, replica_groups={{0,32,2,34,4,36,6,38},{64,96,66,98,68,100,70,102},{128,160,130,162,132,..., dimensions={0} | all-to-all | bytes 786432 | tf_op jit(solution)/shard_map/all_to_all | solution.py:114
  32.5 3.1 %collective-permute-start.7 = (f32[8,1536]{1,0:T(8,128)S(1)}, f32[8,1536]{1,0:T(8,128)S(1)}, u32[]{:S(2)}, u32[]{:S(2)}) collective-permute-start(f32[8,1536]{1,0:T(8,128)S(1)} %reduce_sum.9), channel_id=1, source_target_pairs={{0,64},{2,66},{4,68},{6,70},{16,80},{18,82},{20,84},{22,86},{8,72}... | collective-permute-start | bytes 147464 | tf_op jit(solution)/shard_map/ppermute | solution.py:122
  35.6 2.0 %collective-permute-done.7 = f32[8,1536]{1,0:T(8,128)S(1)} collective-permute-done((f32[8,1536]{1,0:T(8,128)S(1)}, f32[8,1536]{1,0:T(8,128)S(1)}, u32[]{:S(2)}, u32[]{:S(2)}) %collective-permute-start.7) | collective-permute-done | bytes 49184 | tf_op jit(solution)/shard_map/ppermute | solution.py:122
  37.6 4.0 %collective-permute-start.8 = (f32[8,1536]{1,0:T(8,128)S(1)}, f32[8,1536]{1,0:T(8,128)S(1)}, u32[]{:S(2)}, u32[]{:S(2)}) collective-permute-start(f32[8,1536]{1,0:T(8,128)S(1)} %add.54), channel_id=1, source_target_pairs={{0,192},{2,194},{4,196},{6,198},{16,208},{18,210},{20,212},{22,214... | collective-permute-start | bytes 147464 | tf_op jit(solution)/shard_map/ppermute | solution.py:123
  41.7 2.0 %collective-permute-done.8 = f32[8,1536]{1,0:T(8,128)S(1)} collective-permute-done((f32[8,1536]{1,0:T(8,128)S(1)}, f32[8,1536]{1,0:T(8,128)S(1)}, u32[]{:S(2)}, u32[]{:S(2)}) %collective-permute-start.8) | collective-permute-done | bytes 49184 | tf_op jit(solution)/shard_map/ppermute | solution.py:123
  43.7 9.6 %all_to_all.11 = f32[8,8,1536]{2,1,0:T(8,128)S(1)} all-to-all(f32[8,8,1536]{2,1,0:T(8,128)S(1)} %broadcast_in_dim.2), channel_id=1, replica_groups={{0,32,2,34,4,36,6,38},{64,96,66,98,68,100,70,102},{128,160,130,162,132,..., dimensions={0} | all-to-all | bytes 786432 | tf_op jit(solution)/shard_map/all_to_all | solution.py:114
  53.3 0.1 collective-permute-start.10
  53.4 2.5 %collective-permute-start.9 = (f32[8,8,1536]{2,1,0:T(8,128)S(1)}, f32[8,8,1536]{2,1,0:T(8,128)S(1)}, u32[]{:S(2)}, u32[]{:S(2)}) collective-permute-start(f32[8,8,1536]{2,1,0:T(8,128)S(1)} %all_to_all.11), channel_id=1, source_target_pairs={{0,24},{64,88},{128,152},{192,216},{2,26},{66,90},{130,154},{194,2... | collective-permute-start | bytes 1179656 | tf_op jit(solution)/shard_map/ppermute | solution.py:173
  56.0 0.7 collective-permute-start.12
  56.7 6.3 %collective-permute-start.14 = (f32[8,8,1536]{2,1,0:T(8,128)S(1)}, f32[8,8,1536]{2,1,0:T(8,128)S(1)}, u32[]{:S(2)}, u32[]{:S(2)}) collective-permute-start(f32[8,8,1536]{2,1,0:T(8,128)S(1)} %all_to_all.11), channel_id=1, source_target_pairs={{0,1},{1,0},{2,3},{3,2},{4,5},{5,4},{6,7},{7,6},{8,9},{9,8},{10,11... | collective-permute-start | bytes 1179656 | tf_op jit(solution)/shard_map/ppermute | solution.py:110
  63.0 0.0 collective-permute-done.10
  63.0 1.1 %place_chunks.3 = (f32[16,8,2048]{2,1,0:T(8,128)}, f32[16,8,2048]{2,1,0:T(8,128)}, f32[16,8,2048]{2,1,0:T(8,128)}) custom-call(f32[2,4,8,1536]{3,2,1,0:T(8,128)S(1)} %bitcast.29, f32[2,4,8,1536]{3,2,1,0:T(8,128)S(1)} %bitcast.34), custom_call_target="tpu_custom_call" | custom-call | tf_op jit(solution)/shard_map/place_chunks/pallas_call | solution.py:97
  64.1 4.2 %collective-permute-start.15 = (f32[8,8,1536]{2,1,0:T(8,128)S(1)}, f32[8,8,1536]{2,1,0:T(8,128)S(1)}, u32[]{:S(2)}, u32[]{:S(2)}) collective-permute-start(f32[8,8,1536]{2,1,0:T(8,128)S(1)} %collective-permute-done.10), channel_id=1, source_target_pairs={{0,1},{1,0},{2,3},{3,2},{4,5},{5,4},{6,7},{7,6},{8,9},{9,8},{10,11... | collective-permute-start | bytes 1179656 | tf_op jit(solution)/shard_map/ppermute | solution.py:110
  68.3 0.0 collective-permute-done.9
  68.3 2.6 %collective-permute-start.11 = (f32[8,8,1536]{2,1,0:T(8,128)S(1)}, f32[8,8,1536]{2,1,0:T(8,128)S(1)}, u32[]{:S(2)}, u32[]{:S(2)}) collective-permute-start(f32[8,8,1536]{2,1,0:T(8,128)S(1)} %collective-permute-done.9), channel_id=1, source_target_pairs={{0,1},{1,0},{2,3},{3,2},{4,5},{5,4},{6,7},{7,6},{8,9},{9,8},{10,11... | collective-permute-start | bytes 1179656 | tf_op jit(solution)/shard_map/ppermute | solution.py:110
  70.9 0.0 collective-permute-done.12
  70.9 1.2 %collective-permute-start.13 = (f32[8,8,1536]{2,1,0:T(8,128)S(1)}, f32[8,8,1536]{2,1,0:T(8,128)S(1)}, u32[]{:S(2)}, u32[]{:S(2)}) collective-permute-start(f32[8,8,1536]{2,1,0:T(8,128)S(1)} %collective-permute-done.12), channel_id=1, source_target_pairs={{0,1},{1,0},{2,3},{3,2},{4,5},{5,4},{6,7},{7,6},{8,9},{9,8},{10,11... | collective-permute-start | bytes 1179656 | tf_op jit(solution)/shard_map/ppermute | solution.py:110
  72.1 0.0 collective-permute-done.14
  72.1 0.0 collective-permute-done.15
  72.1 1.5 %place_chunks.4 = (f32[16,8,2048]{2,1,0:T(8,128)}, f32[16,8,2048]{2,1,0:T(8,128)}, f32[16,8,2048]{2,1,0:T(8,128)}) custom-call(f32[2,4,8,1536]{3,2,1,0:T(8,128)S(1)} %bitcast.30, f32[2,4,8,1536]{3,2,1,0:T(8,128)S(1)} %bitcast.31, f32[2,4,8,1536]{3,2,1,0:T(8,128)S(1)} %bitcast.32, ...), custom_call_target="tpu_custom_call", output_to_operand_aliasing={{0}: (4, {}), {1}: (5, {}), {2}: (6, {})} | custom-call | tf_op jit(solution)/shard_map/place_chunks/pallas_call | solution.py:97
  73.7 0.0 collective-permute-done.11
  73.7 0.0 collective-permute-done.13
  73.7 1.1 %place_chunks.5 = (f32[16,8,2048]{2,1,0:T(8,128)}, f32[16,8,2048]{2,1,0:T(8,128)}, f32[16,8,2048]{2,1,0:T(8,128)}) custom-call(f32[2,4,8,1536]{3,2,1,0:T(8,128)S(1)} %bitcast.35, f32[2,4,8,1536]{3,2,1,0:T(8,128)S(1)} %bitcast.36, f32[16,8,2048]{2,1,0:T(8,128)} %get-tuple-element.39.refs_2_, ...), custom_call_target="tpu_custom_call", output_to_operand_aliasing={{0}: (2, {}), {1}: (3, {}), {2}: (4, {})} | custom-call | tf_op jit(solution)/shard_map/place_chunks/pallas_call | solution.py:97
  (6 shorter events, 0.2 us)
Async XLA Ops:
  3.8 4.7 %collective-permute-start.1 = (f32[8,8,1536]{2,1,0:T(8,128)S(1)}, f32[8,8,1536]{2,1,0:T(8,128)S(1)}, u32[]{:S(2)}, u32[]{:S(2)}) collective-permute-start(f32[8,8,1536]{2,1,0:T(8,128)S(1)} %get-tuple-element.27), channel_id=1, source_target_pairs={{0,1},{1,0},{2,3},{3,2},{4,5},{5,4},{6,7},{7,6},{8,9},{9,8},{10,11... | collective-permute-start | bytes 1179656 | tf_op jit(solution)/shard_map/ppermute | solution.py:110
  7.1 2.7 %collective-permute-start.5 = (f32[8,8,1536]{2,1,0:T(8,128)S(1)}, f32[8,8,1536]{2,1,0:T(8,128)S(1)}, u32[]{:S(2)}, u32[]{:S(2)}) collective-permute-start(f32[8,8,1536]{2,1,0:T(8,128)S(1)} %get-tuple-element.31), channel_id=1, source_target_pairs={{0,1},{1,0},{2,3},{3,2},{4,5},{5,4},{6,7},{7,6},{8,9},{9,8},{10,11... | collective-permute-start | bytes 1179656 | tf_op jit(solution)/shard_map/ppermute | solution.py:110
  7.2 3.5 %collective-permute-start.3 = (f32[8,8,1536]{2,1,0:T(8,128)S(1)}, f32[8,8,1536]{2,1,0:T(8,128)S(1)}, u32[]{:S(2)}, u32[]{:S(2)}) collective-permute-start(f32[8,8,1536]{2,1,0:T(8,128)S(1)} %get-tuple-element.29), channel_id=1, source_target_pairs={{0,1},{1,0},{2,3},{3,2},{4,5},{5,4},{6,7},{7,6},{8,9},{9,8},{10,11... | collective-permute-start | bytes 1179656 | tf_op jit(solution)/shard_map/ppermute | solution.py:110
  7.6 3.9 %collective-permute-start = (f32[8,8,1536]{2,1,0:T(8,128)S(1)}, f32[8,8,1536]{2,1,0:T(8,128)S(1)}, u32[]{:S(2)}, u32[]{:S(2)}) collective-permute-start(f32[8,8,1536]{2,1,0:T(8,128)S(1)} %get-tuple-element.25), channel_id=1, source_target_pairs={{0,1},{1,0},{2,3},{3,2},{4,5},{5,4},{6,7},{7,6},{8,9},{9,8},{10,11... | collective-permute-start | bytes 1179656 | tf_op jit(solution)/shard_map/ppermute | solution.py:110
  8.5 8.6 %collective-permute-start.2 = (f32[8,8,1536]{2,1,0:T(8,128)S(1)}, f32[8,8,1536]{2,1,0:T(8,128)S(1)}, u32[]{:S(2)}, u32[]{:S(2)}) collective-permute-start(f32[8,8,1536]{2,1,0:T(8,128)S(1)} %add.48), channel_id=1, source_target_pairs={{0,8},{64,72},{128,136},{192,200},{2,10},{66,74},{130,138},{194,20... | collective-permute-start | bytes 1179656 | tf_op jit(solution)/shard_map/ppermute | solution.py:167
  9.8 10.1 %collective-permute-start.6 = (f32[8,8,1536]{2,1,0:T(8,128)S(1)}, f32[8,8,1536]{2,1,0:T(8,128)S(1)}, u32[]{:S(2)}, u32[]{:S(2)}) collective-permute-start(f32[8,8,1536]{2,1,0:T(8,128)S(1)} %add.51), channel_id=1, source_target_pairs={{0,24},{64,88},{128,152},{192,216},{2,26},{66,90},{130,154},{194,2... | collective-permute-start | bytes 1179656 | tf_op jit(solution)/shard_map/ppermute | solution.py:167
  10.7 10.5 %collective-permute-start.4 = (f32[8,8,1536]{2,1,0:T(8,128)S(1)}, f32[8,8,1536]{2,1,0:T(8,128)S(1)}, u32[]{:S(2)}, u32[]{:S(2)}) collective-permute-start(f32[8,8,1536]{2,1,0:T(8,128)S(1)} %add.50), channel_id=1, source_target_pairs={{0,16},{64,80},{128,144},{192,208},{2,18},{66,82},{130,146},{194,2... | collective-permute-start | bytes 1179656 | tf_op jit(solution)/shard_map/ppermute | solution.py:167
  32.5 5.1 %collective-permute-start.7 = (f32[8,1536]{1,0:T(8,128)S(1)}, f32[8,1536]{1,0:T(8,128)S(1)}, u32[]{:S(2)}, u32[]{:S(2)}) collective-permute-start(f32[8,1536]{1,0:T(8,128)S(1)} %reduce_sum.9), channel_id=1, source_target_pairs={{0,64},{2,66},{4,68},{6,70},{16,80},{18,82},{20,84},{22,86},{8,72}... | collective-permute-start | bytes 147464 | tf_op jit(solution)/shard_map/ppermute | solution.py:122
  37.6 6.1 %collective-permute-start.8 = (f32[8,1536]{1,0:T(8,128)S(1)}, f32[8,1536]{1,0:T(8,128)S(1)}, u32[]{:S(2)}, u32[]{:S(2)}) collective-permute-start(f32[8,1536]{1,0:T(8,128)S(1)} %add.54), channel_id=1, source_target_pairs={{0,192},{2,194},{4,196},{6,198},{16,208},{18,210},{20,212},{22,214... | collective-permute-start | bytes 147464 | tf_op jit(solution)/shard_map/ppermute | solution.py:123
  53.3 9.7 %collective-permute-start.10 = (f32[8,8,1536]{2,1,0:T(8,128)S(1)}, f32[8,8,1536]{2,1,0:T(8,128)S(1)}, u32[]{:S(2)}, u32[]{:S(2)}) collective-permute-start(f32[8,8,1536]{2,1,0:T(8,128)S(1)} %all_to_all.11), channel_id=1, source_target_pairs={{0,16},{64,80},{128,144},{192,208},{2,18},{66,82},{130,146},{194,2... | collective-permute-start | bytes 1179656 | tf_op jit(solution)/shard_map/ppermute | solution.py:173
  53.4 14.9 %collective-permute-start.9 = (f32[8,8,1536]{2,1,0:T(8,128)S(1)}, f32[8,8,1536]{2,1,0:T(8,128)S(1)}, u32[]{:S(2)}, u32[]{:S(2)}) collective-permute-start(f32[8,8,1536]{2,1,0:T(8,128)S(1)} %all_to_all.11), channel_id=1, source_target_pairs={{0,24},{64,88},{128,152},{192,216},{2,26},{66,90},{130,154},{194,2... | collective-permute-start | bytes 1179656 | tf_op jit(solution)/shard_map/ppermute | solution.py:173
  56.0 15.0 %collective-permute-start.12 = (f32[8,8,1536]{2,1,0:T(8,128)S(1)}, f32[8,8,1536]{2,1,0:T(8,128)S(1)}, u32[]{:S(2)}, u32[]{:S(2)}) collective-permute-start(f32[8,8,1536]{2,1,0:T(8,128)S(1)} %all_to_all.11), channel_id=1, source_target_pairs={{0,8},{64,72},{128,136},{192,200},{2,10},{66,74},{130,138},{194,20... | collective-permute-start | bytes 1179656 | tf_op jit(solution)/shard_map/ppermute | solution.py:173
  56.7 15.5 %collective-permute-start.14 = (f32[8,8,1536]{2,1,0:T(8,128)S(1)}, f32[8,8,1536]{2,1,0:T(8,128)S(1)}, u32[]{:S(2)}, u32[]{:S(2)}) collective-permute-start(f32[8,8,1536]{2,1,0:T(8,128)S(1)} %all_to_all.11), channel_id=1, source_target_pairs={{0,1},{1,0},{2,3},{3,2},{4,5},{5,4},{6,7},{7,6},{8,9},{9,8},{10,11... | collective-permute-start | bytes 1179656 | tf_op jit(solution)/shard_map/ppermute | solution.py:110
  64.1 8.1 %collective-permute-start.15 = (f32[8,8,1536]{2,1,0:T(8,128)S(1)}, f32[8,8,1536]{2,1,0:T(8,128)S(1)}, u32[]{:S(2)}, u32[]{:S(2)}) collective-permute-start(f32[8,8,1536]{2,1,0:T(8,128)S(1)} %collective-permute-done.10), channel_id=1, source_target_pairs={{0,1},{1,0},{2,3},{3,2},{4,5},{5,4},{6,7},{7,6},{8,9},{9,8},{10,11... | collective-permute-start | bytes 1179656 | tf_op jit(solution)/shard_map/ppermute | solution.py:110
  68.3 5.4 %collective-permute-start.11 = (f32[8,8,1536]{2,1,0:T(8,128)S(1)}, f32[8,8,1536]{2,1,0:T(8,128)S(1)}, u32[]{:S(2)}, u32[]{:S(2)}) collective-permute-start(f32[8,8,1536]{2,1,0:T(8,128)S(1)} %collective-permute-done.9), channel_id=1, source_target_pairs={{0,1},{1,0},{2,3},{3,2},{4,5},{5,4},{6,7},{7,6},{8,9},{9,8},{10,11... | collective-permute-start | bytes 1179656 | tf_op jit(solution)/shard_map/ppermute | solution.py:110
  70.9 2.8 %collective-permute-start.13 = (f32[8,8,1536]{2,1,0:T(8,128)S(1)}, f32[8,8,1536]{2,1,0:T(8,128)S(1)}, u32[]{:S(2)}, u32[]{:S(2)}) collective-permute-start(f32[8,8,1536]{2,1,0:T(8,128)S(1)} %collective-permute-done.12), channel_id=1, source_target_pairs={{0,1},{1,0},{2,3},{3,2},{4,5},{5,4},{6,7},{7,6},{8,9},{9,8},{10,11... | collective-permute-start | bytes 1179656 | tf_op jit(solution)/shard_map/ppermute | solution.py:110

commit v6 on v5

--- a/solution.py
+++ b/solution.py
@@ -34,7 +34,7 @@
 
 
 SECOND = [
-    [place(core, along, pair, across, far) for across in range(4) for pair in range(2)]
+    [place(core, along, pair, across, far) for pair in range(2) for across in range(4)]
     for core in range(2) for along in range(4) for far in range(4)
 ]
 

time: 75 us -> 74.7 us (level)
  waiting for transfers between devices: 14.2 us -> 16.6 us
  starting transfers between devices: 31.7 us -> 29.4 us
    ppermute x8, starting transfers between devices: 18.3 us -> 15.1 us  [across_cores(): return lax.ppermute(x, AXES, [(i, i ^ 1) for i in range(256)])]
    ppermute x3, waiting for transfers between devices: 0.01 us -> 2.94 us  [on_device(): chunks.update({(True, d): lax.ppermute(mine, AXES, ring(d)) for d in BACK})]
  transfers between devices with their start and end apart: 16 -> 16, of which waited for: 6 -> 7; matrix products, arithmetic and copies ran while one was open for 0% -> 0% of each run, Pallas kernels for 4% -> 4%
where the time goes in v6:
time: 74.7 us; the launch traced here: 74.6 us
  starting transfers between devices  29.4 us (39%)
  blocking collectives  20.4 us (27%)
  waiting for transfers between devices  16.6 us (22%)
  Pallas kernels  4.3 us (6%)
  other arithmetic  3.12 us (4%)
    all_to_all x2, blocking collectives, exchange(): return lax.all_to_all(x, AXES, 0, 0, axis_index_groups=groups, tiled=True)  20.4 us
    ppermute x8, starting transfers between devices, across_cores(): return lax.ppermute(x, AXES, [(i, i ^ 1) for i in range(256)])  15.1 us
    ppermute x3, waiting for transfers between devices, on_device(): other = [lax.ppermute(chunk, AXES, ring(d)) for chunk, d in zip(sums, WAYS)]  9.72 us
    ppermute x1, starting transfers between devices, far_sum(): return x + lax.ppermute(x, AXES, far_pairs(lambda far: far ^ 3))  4.67 us
    pallas_call x3, Pallas kernels, place_chunks(): pl.pallas_call(functools.partial(place_kernel, which), in_specs=[anywhere...  3.71 us
    ppermute x3, starting transfers between devices, on_device(): chunks.update({(True, d): lax.ppermute(mine, AXES, ring(d)) for d in BACK})  3.65 us
    ppermute x1, starting transfers between devices, far_sum(): x = x + lax.ppermute(x, AXES, far_pairs(lambda far: far ^ 1))  3.08 us
    ppermute x3, waiting for transfers between devices, on_device(): chunks.update({(True, d): lax.ppermute(mine, AXES, ring(d)) for d in BACK})  2.94 us
  transfers between devices with their start and end apart: 16, of which 7 were waited for; matrix products, arithmetic and copies ran while one was open for 0% of the time, Pallas kernels for 4%

profile of v6, /device:TPU:1, one launch (start us, length us, event | category | flops | bytes accessed | tf_op | source)
XLA Modules:
  0.0 74.6 jit_solution(1558427252221113879)
XLA Ops:
  0.6 2.8 %fusion.6 = (f32[128,2048]{1,0:T(8,128)S(1)}, f32[128,2048]{1,0:T(8,128)S(1)}, f32[128,2048]{1,0:T(8,128)S(1)}) fusion(f32[1,1,128,2048]{3,2,1,0:T(8,128)} %param.4, f32[1,1,128,2048]{3,2,1,0:T(8,128)} %param.7, f32[1,1,128,2048]{3,2,1,0:T(8,128)} %param.6, f32[1,1,128,2048]{3,2,1,0:T(8,128)} %param.5), kind=kLoop, calls=%fused_computation.8 | loop fusion | flops 4194304 | bytes 7340032 | tf_op jit(solution)/shard_map/sub | solution.py:132
  3.5 0.3 lay_chunks.3
  3.8 3.3 %collective-permute-start.1 = (f32[8,8,1536]{2,1,0:T(8,128)S(1)}, f32[8,8,1536]{2,1,0:T(8,128)S(1)}, u32[]{:S(2)}, u32[]{:S(2)}) collective-permute-start(f32[8,8,1536]{2,1,0:T(8,128)S(1)} %get-tuple-element.27), channel_id=1, source_target_pairs={{0,1},{1,0},{2,3},{3,2},{4,5},{5,4},{6,7},{7,6},{8,9},{9,8},{10,11... | collective-permute-start | bytes 1179656 | tf_op jit(solution)/shard_map/ppermute | solution.py:110
  7.1 0.1 collective-permute-start.5
  7.2 0.4 collective-permute-start.3
  7.6 0.1 collective-permute-start
  7.7 0.3 lay_chunks.2
  8.0 0.5 collective-permute-done.1
  8.5 1.3 %collective-permute-start.2 = (f32[8,8,1536]{2,1,0:T(8,128)S(1)}, f32[8,8,1536]{2,1,0:T(8,128)S(1)}, u32[]{:S(2)}, u32[]{:S(2)}) collective-permute-start(f32[8,8,1536]{2,1,0:T(8,128)S(1)} %add.48), channel_id=1, source_target_pairs={{0,8},{64,72},{128,136},{192,200},{2,10},{66,74},{130,138},{194,20... | collective-permute-start | bytes 1179656 | tf_op jit(solution)/shard_map/ppermute | solution.py:167
  9.8 0.0 collective-permute-done.5
  9.8 0.9 %collective-permute-start.6 = (f32[8,8,1536]{2,1,0:T(8,128)S(1)}, f32[8,8,1536]{2,1,0:T(8,128)S(1)}, u32[]{:S(2)}, u32[]{:S(2)}) collective-permute-start(f32[8,8,1536]{2,1,0:T(8,128)S(1)} %add.51), channel_id=1, source_target_pairs={{0,24},{64,88},{128,152},{192,216},{2,26},{66,90},{130,154},{194,2... | collective-permute-start | bytes 1179656 | tf_op jit(solution)/shard_map/ppermute | solution.py:167
  10.7 0.0 collective-permute-done.3
  10.7 0.1 add.50
  10.7 0.8 %collective-permute-start.4 = (f32[8,8,1536]{2,1,0:T(8,128)S(1)}, f32[8,8,1536]{2,1,0:T(8,128)S(1)}, u32[]{:S(2)}, u32[]{:S(2)}) collective-permute-start(f32[8,8,1536]{2,1,0:T(8,128)S(1)} %add.50), channel_id=1, source_target_pairs={{0,16},{64,80},{128,144},{192,208},{2,18},{66,82},{130,146},{194,2... | collective-permute-start | bytes 1179656 | tf_op jit(solution)/shard_map/ppermute | solution.py:167
  11.5 0.0 collective-permute-done
  11.5 5.6 %collective-permute-done.2 = f32[8,8,1536]{2,1,0:T(8,128)S(1)} collective-permute-done((f32[8,8,1536]{2,1,0:T(8,128)S(1)}, f32[8,8,1536]{2,1,0:T(8,128)S(1)}, u32[]{:S(2)}, u32[]{:S(2)}) %collective-permute-start.2) | collective-permute-done | bytes 393248 | tf_op jit(solution)/shard_map/ppermute | solution.py:167
  17.1 2.8 %collective-permute-done.6 = f32[8,8,1536]{2,1,0:T(8,128)S(1)} collective-permute-done((f32[8,8,1536]{2,1,0:T(8,128)S(1)}, f32[8,8,1536]{2,1,0:T(8,128)S(1)}, u32[]{:S(2)}, u32[]{:S(2)}) %collective-permute-start.6) | collective-permute-done | bytes 393248 | tf_op jit(solution)/shard_map/ppermute | solution.py:167
  19.9 1.4 %collective-permute-done.4 = f32[8,8,1536]{2,1,0:T(8,128)S(1)} collective-permute-done((f32[8,8,1536]{2,1,0:T(8,128)S(1)}, f32[8,8,1536]{2,1,0:T(8,128)S(1)}, u32[]{:S(2)}, u32[]{:S(2)}) %collective-permute-start.4) | collective-permute-done | bytes 393248 | tf_op jit(solution)/shard_map/ppermute | solution.py:167
  21.2 0.1 add_add_fusion
  21.3 10.7 %all_to_all.10 = f32[8,8,1536]{2,1,0:T(8,128)S(1)} all-to-all(f32[8,8,1536]{2,1,0:T(8,128)S(1)} %add_add_fusion), channel_id=1, replica_groups={{0,2,4,6,32,34,36,38},{64,66,68,70,96,98,100,102},{128,130,132,134,160,..., dimensions={0} | all-to-all | bytes 786432 | tf_op jit(solution)/shard_map/all_to_all | solution.py:114
  32.0 3.1 %collective-permute-start.7 = (f32[8,1536]{1,0:T(8,128)S(1)}, f32[8,1536]{1,0:T(8,128)S(1)}, u32[]{:S(2)}, u32[]{:S(2)}) collective-permute-start(f32[8,1536]{1,0:T(8,128)S(1)} %reduce_sum.9), channel_id=1, source_target_pairs={{0,64},{2,66},{4,68},{6,70},{16,80},{18,82},{20,84},{22,86},{8,72}... | collective-permute-start | bytes 147464 | tf_op jit(solution)/shard_map/ppermute | solution.py:122
  35.1 1.5 %collective-permute-done.7 = f32[8,1536]{1,0:T(8,128)S(1)} collective-permute-done((f32[8,1536]{1,0:T(8,128)S(1)}, f32[8,1536]{1,0:T(8,128)S(1)}, u32[]{:S(2)}, u32[]{:S(2)}) %collective-permute-start.7) | collective-permute-done | bytes 49184 | tf_op jit(solution)/shard_map/ppermute | solution.py:122
  36.6 4.7 %collective-permute-start.8 = (f32[8,1536]{1,0:T(8,128)S(1)}, f32[8,1536]{1,0:T(8,128)S(1)}, u32[]{:S(2)}, u32[]{:S(2)}) collective-permute-start(f32[8,1536]{1,0:T(8,128)S(1)} %add.54), channel_id=1, source_target_pairs={{0,192},{2,194},{4,196},{6,198},{16,208},{18,210},{20,212},{22,214... | collective-permute-start | bytes 147464 | tf_op jit(solution)/shard_map/ppermute | solution.py:123
  41.3 2.0 %collective-permute-done.8 = f32[8,1536]{1,0:T(8,128)S(1)} collective-permute-done((f32[8,1536]{1,0:T(8,128)S(1)}, f32[8,1536]{1,0:T(8,128)S(1)}, u32[]{:S(2)}, u32[]{:S(2)}) %collective-permute-start.8) | collective-permute-done | bytes 49184 | tf_op jit(solution)/shard_map/ppermute | solution.py:123
  43.3 9.7 %all_to_all.11 = f32[8,8,1536]{2,1,0:T(8,128)S(1)} all-to-all(f32[8,8,1536]{2,1,0:T(8,128)S(1)} %broadcast_in_dim.2), channel_id=1, replica_groups={{0,2,4,6,32,34,36,38},{64,66,68,70,96,98,100,102},{128,130,132,134,160,..., dimensions={0} | all-to-all | bytes 786432 | tf_op jit(solution)/shard_map/all_to_all | solution.py:114
  53.1 0.3 collective-permute-start.10
  53.3 2.4 %collective-permute-start.9 = (f32[8,8,1536]{2,1,0:T(8,128)S(1)}, f32[8,8,1536]{2,1,0:T(8,128)S(1)}, u32[]{:S(2)}, u32[]{:S(2)}) collective-permute-start(f32[8,8,1536]{2,1,0:T(8,128)S(1)} %all_to_all.11), channel_id=1, source_target_pairs={{0,24},{64,88},{128,152},{192,216},{2,26},{66,90},{130,154},{194,2... | collective-permute-start | bytes 1179656 | tf_op jit(solution)/shard_map/ppermute | solution.py:173
  55.7 1.0 %collective-permute-start.12 = (f32[8,8,1536]{2,1,0:T(8,128)S(1)}, f32[8,8,1536]{2,1,0:T(8,128)S(1)}, u32[]{:S(2)}, u32[]{:S(2)}) collective-permute-start(f32[8,8,1536]{2,1,0:T(8,128)S(1)} %all_to_all.11), channel_id=1, source_target_pairs={{0,8},{64,72},{128,136},{192,200},{2,10},{66,74},{130,138},{194,20... | collective-permute-start | bytes 1179656 | tf_op jit(solution)/shard_map/ppermute | solution.py:173
  56.7 6.1 %collective-permute-start.14 = (f32[8,8,1536]{2,1,0:T(8,128)S(1)}, f32[8,8,1536]{2,1,0:T(8,128)S(1)}, u32[]{:S(2)}, u32[]{:S(2)}) collective-permute-start(f32[8,8,1536]{2,1,0:T(8,128)S(1)} %all_to_all.11), channel_id=1, source_target_pairs={{0,1},{1,0},{2,3},{3,2},{4,5},{5,4},{6,7},{7,6},{8,9},{9,8},{10,11... | collective-permute-start | bytes 1179656 | tf_op jit(solution)/shard_map/ppermute | solution.py:110
  62.8 2.9 %collective-permute-done.10 = f32[8,8,1536]{2,1,0:T(8,128)S(1)} collective-permute-done((f32[8,8,1536]{2,1,0:T(8,128)S(1)}, f32[8,8,1536]{2,1,0:T(8,128)S(1)}, u32[]{:S(2)}, u32[]{:S(2)}) %collective-permute-start.10) | collective-permute-done | bytes 393248 | tf_op jit(solution)/shard_map/ppermute | solution.py:173
  65.8 1.1 %place_chunks.3 = (f32[16,8,2048]{2,1,0:T(8,128)}, f32[16,8,2048]{2,1,0:T(8,128)}, f32[16,8,2048]{2,1,0:T(8,128)}) custom-call(f32[2,4,8,1536]{3,2,1,0:T(8,128)S(1)} %bitcast.29, f32[2,4,8,1536]{3,2,1,0:T(8,128)S(1)} %bitcast.34), custom_call_target="tpu_custom_call" | custom-call | tf_op jit(solution)/shard_map/place_chunks/pallas_call | solution.py:97
  66.8 1.2 %collective-permute-start.15 = (f32[8,8,1536]{2,1,0:T(8,128)S(1)}, f32[8,8,1536]{2,1,0:T(8,128)S(1)}, u32[]{:S(2)}, u32[]{:S(2)}) collective-permute-start(f32[8,8,1536]{2,1,0:T(8,128)S(1)} %collective-permute-done.10), channel_id=1, source_target_pairs={{0,1},{1,0},{2,3},{3,2},{4,5},{5,4},{6,7},{7,6},{8,9},{9,8},{10,11... | collective-permute-start | bytes 1179656 | tf_op jit(solution)/shard_map/ppermute | solution.py:110
  68.0 0.0 collective-permute-done.9
  68.0 2.6 %collective-permute-start.11 = (f32[8,8,1536]{2,1,0:T(8,128)S(1)}, f32[8,8,1536]{2,1,0:T(8,128)S(1)}, u32[]{:S(2)}, u32[]{:S(2)}) collective-permute-start(f32[8,8,1536]{2,1,0:T(8,128)S(1)} %collective-permute-done.9), channel_id=1, source_target_pairs={{0,1},{1,0},{2,3},{3,2},{4,5},{5,4},{6,7},{7,6},{8,9},{9,8},{10,11... | collective-permute-start | bytes 1179656 | tf_op jit(solution)/shard_map/ppermute | solution.py:110
  70.6 0.0 collective-permute-done.12
  70.6 1.2 %collective-permute-start.13 = (f32[8,8,1536]{2,1,0:T(8,128)S(1)}, f32[8,8,1536]{2,1,0:T(8,128)S(1)}, u32[]{:S(2)}, u32[]{:S(2)}) collective-permute-start(f32[8,8,1536]{2,1,0:T(8,128)S(1)} %collective-permute-done.12), channel_id=1, source_target_pairs={{0,1},{1,0},{2,3},{3,2},{4,5},{5,4},{6,7},{7,6},{8,9},{9,8},{10,11... | collective-permute-start | bytes 1179656 | tf_op jit(solution)/shard_map/ppermute | solution.py:110
  71.9 0.0 collective-permute-done.14
  71.9 0.0 collective-permute-done.15
  71.9 1.5 %place_chunks.4 = (f32[16,8,2048]{2,1,0:T(8,128)}, f32[16,8,2048]{2,1,0:T(8,128)}, f32[16,8,2048]{2,1,0:T(8,128)}) custom-call(f32[2,4,8,1536]{3,2,1,0:T(8,128)S(1)} %bitcast.30, f32[2,4,8,1536]{3,2,1,0:T(8,128)S(1)} %bitcast.31, f32[2,4,8,1536]{3,2,1,0:T(8,128)S(1)} %bitcast.32, ...), custom_call_target="tpu_custom_call", output_to_operand_aliasing={{0}: (4, {}), {1}: (5, {}), {2}: (6, {})} | custom-call | tf_op jit(solution)/shard_map/place_chunks/pallas_call | solution.py:97
  73.4 0.0 collective-permute-done.11
  73.5 0.0 collective-permute-done.13
  73.5 1.1 %place_chunks.5 = (f32[16,8,2048]{2,1,0:T(8,128)}, f32[16,8,2048]{2,1,0:T(8,128)}, f32[16,8,2048]{2,1,0:T(8,128)}) custom-call(f32[2,4,8,1536]{3,2,1,0:T(8,128)S(1)} %bitcast.35, f32[2,4,8,1536]{3,2,1,0:T(8,128)S(1)} %bitcast.36, f32[16,8,2048]{2,1,0:T(8,128)} %get-tuple-element.39.refs_2_, ...), custom_call_target="tpu_custom_call", output_to_operand_aliasing={{0}: (2, {}), {1}: (3, {}), {2}: (4, {})} | custom-call | tf_op jit(solution)/shard_map/place_chunks/pallas_call | solution.py:97
  (6 shorter events, 0.2 us)
Async XLA Ops:
  3.8 4.7 %collective-permute-start.1 = (f32[8,8,1536]{2,1,0:T(8,128)S(1)}, f32[8,8,1536]{2,1,0:T(8,128)S(1)}, u32[]{:S(2)}, u32[]{:S(2)}) collective-permute-start(f32[8,8,1536]{2,1,0:T(8,128)S(1)} %get-tuple-element.27), channel_id=1, source_target_pairs={{0,1},{1,0},{2,3},{3,2},{4,5},{5,4},{6,7},{7,6},{8,9},{9,8},{10,11... | collective-permute-start | bytes 1179656 | tf_op jit(solution)/shard_map/ppermute | solution.py:110
  7.1 2.7 %collective-permute-start.5 = (f32[8,8,1536]{2,1,0:T(8,128)S(1)}, f32[8,8,1536]{2,1,0:T(8,128)S(1)}, u32[]{:S(2)}, u32[]{:S(2)}) collective-permute-start(f32[8,8,1536]{2,1,0:T(8,128)S(1)} %get-tuple-element.31), channel_id=1, source_target_pairs={{0,1},{1,0},{2,3},{3,2},{4,5},{5,4},{6,7},{7,6},{8,9},{9,8},{10,11... | collective-permute-start | bytes 1179656 | tf_op jit(solution)/shard_map/ppermute | solution.py:110
  7.2 3.5 %collective-permute-start.3 = (f32[8,8,1536]{2,1,0:T(8,128)S(1)}, f32[8,8,1536]{2,1,0:T(8,128)S(1)}, u32[]{:S(2)}, u32[]{:S(2)}) collective-permute-start(f32[8,8,1536]{2,1,0:T(8,128)S(1)} %get-tuple-element.29), channel_id=1, source_target_pairs={{0,1},{1,0},{2,3},{3,2},{4,5},{5,4},{6,7},{7,6},{8,9},{9,8},{10,11... | collective-permute-start | bytes 1179656 | tf_op jit(solution)/shard_map/ppermute | solution.py:110
  7.6 3.9 %collective-permute-start = (f32[8,8,1536]{2,1,0:T(8,128)S(1)}, f32[8,8,1536]{2,1,0:T(8,128)S(1)}, u32[]{:S(2)}, u32[]{:S(2)}) collective-permute-start(f32[8,8,1536]{2,1,0:T(8,128)S(1)} %get-tuple-element.25), channel_id=1, source_target_pairs={{0,1},{1,0},{2,3},{3,2},{4,5},{5,4},{6,7},{7,6},{8,9},{9,8},{10,11... | collective-permute-start | bytes 1179656 | tf_op jit(solution)/shard_map/ppermute | solution.py:110
  8.5 8.6 %collective-permute-start.2 = (f32[8,8,1536]{2,1,0:T(8,128)S(1)}, f32[8,8,1536]{2,1,0:T(8,128)S(1)}, u32[]{:S(2)}, u32[]{:S(2)}) collective-permute-start(f32[8,8,1536]{2,1,0:T(8,128)S(1)} %add.48), channel_id=1, source_target_pairs={{0,8},{64,72},{128,136},{192,200},{2,10},{66,74},{130,138},{194,20... | collective-permute-start | bytes 1179656 | tf_op jit(solution)/shard_map/ppermute | solution.py:167
  9.8 10.1 %collective-permute-start.6 = (f32[8,8,1536]{2,1,0:T(8,128)S(1)}, f32[8,8,1536]{2,1,0:T(8,128)S(1)}, u32[]{:S(2)}, u32[]{:S(2)}) collective-permute-start(f32[8,8,1536]{2,1,0:T(8,128)S(1)} %add.51), channel_id=1, source_target_pairs={{0,24},{64,88},{128,152},{192,216},{2,26},{66,90},{130,154},{194,2... | collective-permute-start | bytes 1179656 | tf_op jit(solution)/shard_map/ppermute | solution.py:167
  10.7 10.5 %collective-permute-start.4 = (f32[8,8,1536]{2,1,0:T(8,128)S(1)}, f32[8,8,1536]{2,1,0:T(8,128)S(1)}, u32[]{:S(2)}, u32[]{:S(2)}) collective-permute-start(f32[8,8,1536]{2,1,0:T(8,128)S(1)} %add.50), channel_id=1, source_target_pairs={{0,16},{64,80},{128,144},{192,208},{2,18},{66,82},{130,146},{194,2... | collective-permute-start | bytes 1179656 | tf_op jit(solution)/shard_map/ppermute | solution.py:167
  32.0 4.6 %collective-permute-start.7 = (f32[8,1536]{1,0:T(8,128)S(1)}, f32[8,1536]{1,0:T(8,128)S(1)}, u32[]{:S(2)}, u32[]{:S(2)}) collective-permute-start(f32[8,1536]{1,0:T(8,128)S(1)} %reduce_sum.9), channel_id=1, source_target_pairs={{0,64},{2,66},{4,68},{6,70},{16,80},{18,82},{20,84},{22,86},{8,72}... | collective-permute-start | bytes 147464 | tf_op jit(solution)/shard_map/ppermute | solution.py:122
  36.6 6.7 %collective-permute-start.8 = (f32[8,1536]{1,0:T(8,128)S(1)}, f32[8,1536]{1,0:T(8,128)S(1)}, u32[]{:S(2)}, u32[]{:S(2)}) collective-permute-start(f32[8,1536]{1,0:T(8,128)S(1)} %add.54), channel_id=1, source_target_pairs={{0,192},{2,194},{4,196},{6,198},{16,208},{18,210},{20,212},{22,214... | collective-permute-start | bytes 147464 | tf_op jit(solution)/shard_map/ppermute | solution.py:123
  53.1 12.7 %collective-permute-start.10 = (f32[8,8,1536]{2,1,0:T(8,128)S(1)}, f32[8,8,1536]{2,1,0:T(8,128)S(1)}, u32[]{:S(2)}, u32[]{:S(2)}) collective-permute-start(f32[8,8,1536]{2,1,0:T(8,128)S(1)} %all_to_all.11), channel_id=1, source_target_pairs={{0,16},{64,80},{128,144},{192,208},{2,18},{66,82},{130,146},{194,2... | collective-permute-start | bytes 1179656 | tf_op jit(solution)/shard_map/ppermute | solution.py:173
  53.3 14.7 %collective-permute-start.9 = (f32[8,8,1536]{2,1,0:T(8,128)S(1)}, f32[8,8,1536]{2,1,0:T(8,128)S(1)}, u32[]{:S(2)}, u32[]{:S(2)}) collective-permute-start(f32[8,8,1536]{2,1,0:T(8,128)S(1)} %all_to_all.11), channel_id=1, source_target_pairs={{0,24},{64,88},{128,152},{192,216},{2,26},{66,90},{130,154},{194,2... | collective-permute-start | bytes 1179656 | tf_op jit(solution)/shard_map/ppermute | solution.py:173
  55.7 14.9 %collective-permute-start.12 = (f32[8,8,1536]{2,1,0:T(8,128)S(1)}, f32[8,8,1536]{2,1,0:T(8,128)S(1)}, u32[]{:S(2)}, u32[]{:S(2)}) collective-permute-start(f32[8,8,1536]{2,1,0:T(8,128)S(1)} %all_to_all.11), channel_id=1, source_target_pairs={{0,8},{64,72},{128,136},{192,200},{2,10},{66,74},{130,138},{194,20... | collective-permute-start | bytes 1179656 | tf_op jit(solution)/shard_map/ppermute | solution.py:173
  56.7 15.2 %collective-permute-start.14 = (f32[8,8,1536]{2,1,0:T(8,128)S(1)}, f32[8,8,1536]{2,1,0:T(8,128)S(1)}, u32[]{:S(2)}, u32[]{:S(2)}) collective-permute-start(f32[8,8,1536]{2,1,0:T(8,128)S(1)} %all_to_all.11), channel_id=1, source_target_pairs={{0,1},{1,0},{2,3},{3,2},{4,5},{5,4},{6,7},{7,6},{8,9},{9,8},{10,11... | collective-permute-start | bytes 1179656 | tf_op jit(solution)/shard_map/ppermute | solution.py:110
  66.8 5.1 %collective-permute-start.15 = (f32[8,8,1536]{2,1,0:T(8,128)S(1)}, f32[8,8,1536]{2,1,0:T(8,128)S(1)}, u32[]{:S(2)}, u32[]{:S(2)}) collective-permute-start(f32[8,8,1536]{2,1,0:T(8,128)S(1)} %collective-permute-done.10), channel_id=1, source_target_pairs={{0,1},{1,0},{2,3},{3,2},{4,5},{5,4},{6,7},{7,6},{8,9},{9,8},{10,11... | collective-permute-start | bytes 1179656 | tf_op jit(solution)/shard_map/ppermute | solution.py:110
  68.0 5.4 %collective-permute-start.11 = (f32[8,8,1536]{2,1,0:T(8,128)S(1)}, f32[8,8,1536]{2,1,0:T(8,128)S(1)}, u32[]{:S(2)}, u32[]{:S(2)}) collective-permute-start(f32[8,8,1536]{2,1,0:T(8,128)S(1)} %collective-permute-done.9), channel_id=1, source_target_pairs={{0,1},{1,0},{2,3},{3,2},{4,5},{5,4},{6,7},{7,6},{8,9},{9,8},{10,11... | collective-permute-start | bytes 1179656 | tf_op jit(solution)/shard_map/ppermute | solution.py:110
  70.6 2.8 %collective-permute-start.13 = (f32[8,8,1536]{2,1,0:T(8,128)S(1)}, f32[8,8,1536]{2,1,0:T(8,128)S(1)}, u32[]{:S(2)}, u32[]{:S(2)}) collective-permute-start(f32[8,8,1536]{2,1,0:T(8,128)S(1)} %collective-permute-done.12), channel_id=1, source_target_pairs={{0,1},{1,0},{2,3},{3,2},{4,5},{5,4},{6,7},{7,6},{8,9},{9,8},{10,11... | collective-permute-start | bytes 1179656 | tf_op jit(solution)/shard_map/ppermute | solution.py:110

commit v7 on v6

--- a/solution.py
+++ b/solution.py
@@ -12,7 +12,7 @@
 
 AXES = ("row", "col")
 SHIFT = (0, 0)
-WAYS = (2, 1, 3)
+WAYS = (2, 3, 1)
 BACK = (1, 3, 2)
 SPLIT = 6
 

time: 74.7 us -> 74.7 us (level)
  waiting for transfers between devices: 16.6 us -> 12.6 us
  starting transfers between devices: 29.4 us -> 33.1 us
    ppermute x8, starting transfers between devices: 15.1 us -> 18.5 us  [across_cores(): return lax.ppermute(x, AXES, [(i, i ^ 1) for i in range(256)])]
    ppermute x3, waiting for transfers between devices: 2.94 us -> 0.01 us  [on_device(): chunks.update({(True, d): lax.ppermute(mine, AXES, ring(d)) for d in BACK})]
    ppermute x3, starting transfers between devices: 2.89 us -> 4.1 us  [on_device(): other = [lax.ppermute(chunk, AXES, ring(d)) for chunk, d in zip(sums, WAYS)]]
    ppermute x3, waiting for transfers between devices: 9.72 us -> 8.52 us  [on_device(): other = [lax.ppermute(chunk, AXES, ring(d)) for chunk, d in zip(sums, WAYS)]]
    ppermute x3, starting transfers between devices: 3.65 us -> 2.8 us  [on_device(): chunks.update({(True, d): lax.ppermute(mine, AXES, ring(d)) for d in BACK})]
  transfers between devices with their start and end apart: 16 -> 16, of which waited for: 7 -> 5; matrix products, arithmetic and copies ran while one was open for 0% -> 0% of each run, Pallas kernels for 4% -> 4%
where the time goes in v7:
time: 74.7 us; the launch traced here: 74.6 us
  starting transfers between devices  33.1 us (44%)
  blocking collectives  20.7 us (28%)
  waiting for transfers between devices  12.6 us (17%)
  Pallas kernels  4.3 us (6%)
  other arithmetic  3.12 us (4%)
    all_to_all x2, blocking collectives, exchange(): return lax.all_to_all(x, AXES, 0, 0, axis_index_groups=groups, tiled=True)  20.7 us
    ppermute x8, starting transfers between devices, across_cores(): return lax.ppermute(x, AXES, [(i, i ^ 1) for i in range(256)])  18.5 us
    ppermute x3, waiting for transfers between devices, on_device(): other = [lax.ppermute(chunk, AXES, ring(d)) for chunk, d in zip(sums, WAYS)]  8.52 us
    ppermute x1, starting transfers between devices, far_sum(): return x + lax.ppermute(x, AXES, far_pairs(lambda far: far ^ 3))  4.62 us
    ppermute x3, starting transfers between devices, on_device(): other = [lax.ppermute(chunk, AXES, ring(d)) for chunk, d in zip(sums, WAYS)]  4.1 us
    pallas_call x3, Pallas kernels, place_chunks(): pl.pallas_call(functools.partial(place_kernel, which), in_specs=[anywhere...  3.71 us
    ppermute x1, starting transfers between devices, far_sum(): x = x + lax.ppermute(x, AXES, far_pairs(lambda far: far ^ 1))  3.08 us
    sub x1, other arithmetic, adam(): return (old - 0.003 * (first / bottom + 0.1 * old), first, second)  2.83 us
  transfers between devices with their start and end apart: 16, of which 5 were waited for; matrix products, arithmetic and copies ran while one was open for 0% of the time, Pallas kernels for 4%

profile of v7, /device:TPU:1, one launch (start us, length us, event | category | flops | bytes accessed | tf_op | source)
XLA Modules:
  0.0 74.6 jit_solution(11356260725056550177)
XLA Ops:
  0.6 2.8 %fusion.6 = (f32[128,2048]{1,0:T(8,128)S(1)}, f32[128,2048]{1,0:T(8,128)S(1)}, f32[128,2048]{1,0:T(8,128)S(1)}) fusion(f32[1,1,128,2048]{3,2,1,0:T(8,128)} %param.4, f32[1,1,128,2048]{3,2,1,0:T(8,128)} %param.7, f32[1,1,128,2048]{3,2,1,0:T(8,128)} %param.6, f32[1,1,128,2048]{3,2,1,0:T(8,128)} %param.5), kind=kLoop, calls=%fused_computation.8 | loop fusion | flops 4194304 | bytes 7340032 | tf_op jit(solution)/shard_map/sub | solution.py:132
  3.5 0.3 lay_chunks.3
  3.8 3.3 %collective-permute-start.1 = (f32[8,8,1536]{2,1,0:T(8,128)S(1)}, f32[8,8,1536]{2,1,0:T(8,128)S(1)}, u32[]{:S(2)}, u32[]{:S(2)}) collective-permute-start(f32[8,8,1536]{2,1,0:T(8,128)S(1)} %get-tuple-element.27), channel_id=1, source_target_pairs={{0,1},{1,0},{2,3},{3,2},{4,5},{5,4},{6,7},{7,6},{8,9},{9,8},{10,11... | collective-permute-start | bytes 1179656 | tf_op jit(solution)/shard_map/ppermute | solution.py:110
  7.1 0.1 collective-permute-start.5
  7.2 0.4 collective-permute-start.3
  7.6 0.1 collective-permute-start
  7.7 0.3 lay_chunks.2
  8.0 0.5 collective-permute-done.1
  8.5 1.3 %collective-permute-start.2 = (f32[8,8,1536]{2,1,0:T(8,128)S(1)}, f32[8,8,1536]{2,1,0:T(8,128)S(1)}, u32[]{:S(2)}, u32[]{:S(2)}) collective-permute-start(f32[8,8,1536]{2,1,0:T(8,128)S(1)} %add.48), channel_id=1, source_target_pairs={{0,8},{64,72},{128,136},{192,200},{2,10},{66,74},{130,138},{194,20... | collective-permute-start | bytes 1179656 | tf_op jit(solution)/shard_map/ppermute | solution.py:167
  9.8 0.0 collective-permute-done.5
  9.8 0.5 collective-permute-start.6
  10.3 0.0 collective-permute-done.3
  10.3 0.1 add.50
  10.4 2.4 %collective-permute-start.4 = (f32[8,8,1536]{2,1,0:T(8,128)S(1)}, f32[8,8,1536]{2,1,0:T(8,128)S(1)}, u32[]{:S(2)}, u32[]{:S(2)}) collective-permute-start(f32[8,8,1536]{2,1,0:T(8,128)S(1)} %add.50), channel_id=1, source_target_pairs={{0,24},{64,88},{128,152},{192,216},{2,26},{66,90},{130,154},{194,2... | collective-permute-start | bytes 1179656 | tf_op jit(solution)/shard_map/ppermute | solution.py:167
  12.7 0.0 collective-permute-done
  12.7 4.3 %collective-permute-done.2 = f32[8,8,1536]{2,1,0:T(8,128)S(1)} collective-permute-done((f32[8,8,1536]{2,1,0:T(8,128)S(1)}, f32[8,8,1536]{2,1,0:T(8,128)S(1)}, u32[]{:S(2)}, u32[]{:S(2)}) %collective-permute-start.2) | collective-permute-done | bytes 393248 | tf_op jit(solution)/shard_map/ppermute | solution.py:167
  17.1 4.2 %collective-permute-done.6 = f32[8,8,1536]{2,1,0:T(8,128)S(1)} collective-permute-done((f32[8,8,1536]{2,1,0:T(8,128)S(1)}, f32[8,8,1536]{2,1,0:T(8,128)S(1)}, u32[]{:S(2)}, u32[]{:S(2)}) %collective-permute-start.6) | collective-permute-done | bytes 393248 | tf_op jit(solution)/shard_map/ppermute | solution.py:167
  21.2 0.0 collective-permute-done.4
  21.2 0.1 add_add_fusion
  21.4 10.6 %all_to_all.10 = f32[8,8,1536]{2,1,0:T(8,128)S(1)} all-to-all(f32[8,8,1536]{2,1,0:T(8,128)S(1)} %add_add_fusion), channel_id=1, replica_groups={{0,2,4,6,32,34,36,38},{64,66,68,70,96,98,100,102},{128,130,132,134,160,..., dimensions={0} | all-to-all | bytes 786432 | tf_op jit(solution)/shard_map/all_to_all | solution.py:114
  32.0 3.1 %collective-permute-start.7 = (f32[8,1536]{1,0:T(8,128)S(1)}, f32[8,1536]{1,0:T(8,128)S(1)}, u32[]{:S(2)}, u32[]{:S(2)}) collective-permute-start(f32[8,1536]{1,0:T(8,128)S(1)} %reduce_sum.9), channel_id=1, source_target_pairs={{0,64},{2,66},{4,68},{6,70},{16,80},{18,82},{20,84},{22,86},{8,72}... | collective-permute-start | bytes 147464 | tf_op jit(solution)/shard_map/ppermute | solution.py:122
  35.1 1.5 %collective-permute-done.7 = f32[8,1536]{1,0:T(8,128)S(1)} collective-permute-done((f32[8,1536]{1,0:T(8,128)S(1)}, f32[8,1536]{1,0:T(8,128)S(1)}, u32[]{:S(2)}, u32[]{:S(2)}) %collective-permute-start.7) | collective-permute-done | bytes 49184 | tf_op jit(solution)/shard_map/ppermute | solution.py:122
  36.6 4.6 %collective-permute-start.8 = (f32[8,1536]{1,0:T(8,128)S(1)}, f32[8,1536]{1,0:T(8,128)S(1)}, u32[]{:S(2)}, u32[]{:S(2)}) collective-permute-start(f32[8,1536]{1,0:T(8,128)S(1)} %add.54), channel_id=1, source_target_pairs={{0,192},{2,194},{4,196},{6,198},{16,208},{18,210},{20,212},{22,214... | collective-permute-start | bytes 147464 | tf_op jit(solution)/shard_map/ppermute | solution.py:123
  41.2 2.1 %collective-permute-done.8 = f32[8,1536]{1,0:T(8,128)S(1)} collective-permute-done((f32[8,1536]{1,0:T(8,128)S(1)}, f32[8,1536]{1,0:T(8,128)S(1)}, u32[]{:S(2)}, u32[]{:S(2)}) %collective-permute-start.8) | collective-permute-done | bytes 49184 | tf_op jit(solution)/shard_map/ppermute | solution.py:123
  43.3 10.1 %all_to_all.11 = f32[8,8,1536]{2,1,0:T(8,128)S(1)} all-to-all(f32[8,8,1536]{2,1,0:T(8,128)S(1)} %broadcast_in_dim.2), channel_id=1, replica_groups={{0,2,4,6,32,34,36,38},{64,66,68,70,96,98,100,102},{128,130,132,134,160,..., dimensions={0} | all-to-all | bytes 786432 | tf_op jit(solution)/shard_map/all_to_all | solution.py:114
  53.4 0.4 collective-permute-start.10
  53.8 2.2 %collective-permute-start.9 = (f32[8,8,1536]{2,1,0:T(8,128)S(1)}, f32[8,8,1536]{2,1,0:T(8,128)S(1)}, u32[]{:S(2)}, u32[]{:S(2)}) collective-permute-start(f32[8,8,1536]{2,1,0:T(8,128)S(1)} %all_to_all.11), channel_id=1, source_target_pairs={{0,24},{64,88},{128,152},{192,216},{2,26},{66,90},{130,154},{194,2... | collective-permute-start | bytes 1179656 | tf_op jit(solution)/shard_map/ppermute | solution.py:173
  56.1 0.1 collective-permute-start.12
  56.2 6.4 %collective-permute-start.14 = (f32[8,8,1536]{2,1,0:T(8,128)S(1)}, f32[8,8,1536]{2,1,0:T(8,128)S(1)}, u32[]{:S(2)}, u32[]{:S(2)}) collective-permute-start(f32[8,8,1536]{2,1,0:T(8,128)S(1)} %all_to_all.11), channel_id=1, source_target_pairs={{0,1},{1,0},{2,3},{3,2},{4,5},{5,4},{6,7},{7,6},{8,9},{9,8},{10,11... | collective-permute-start | bytes 1179656 | tf_op jit(solution)/shard_map/ppermute | solution.py:110
  62.6 0.0 collective-permute-done.10
  62.6 1.1 %place_chunks.3 = (f32[16,8,2048]{2,1,0:T(8,128)}, f32[16,8,2048]{2,1,0:T(8,128)}, f32[16,8,2048]{2,1,0:T(8,128)}) custom-call(f32[2,4,8,1536]{3,2,1,0:T(8,128)S(1)} %bitcast.29, f32[2,4,8,1536]{3,2,1,0:T(8,128)S(1)} %bitcast.34), custom_call_target="tpu_custom_call" | custom-call | tf_op jit(solution)/shard_map/place_chunks/pallas_call | solution.py:97
  63.7 4.2 %collective-permute-start.15 = (f32[8,8,1536]{2,1,0:T(8,128)S(1)}, f32[8,8,1536]{2,1,0:T(8,128)S(1)}, u32[]{:S(2)}, u32[]{:S(2)}) collective-permute-start(f32[8,8,1536]{2,1,0:T(8,128)S(1)} %collective-permute-done.10), channel_id=1, source_target_pairs={{0,1},{1,0},{2,3},{3,2},{4,5},{5,4},{6,7},{7,6},{8,9},{9,8},{10,11... | collective-permute-start | bytes 1179656 | tf_op jit(solution)/shard_map/ppermute | solution.py:110
  67.9 0.0 collective-permute-done.9
  67.9 0.1 collective-permute-start.11
  68.0 0.0 collective-permute-done.12
  68.0 3.9 %collective-permute-start.13 = (f32[8,8,1536]{2,1,0:T(8,128)S(1)}, f32[8,8,1536]{2,1,0:T(8,128)S(1)}, u32[]{:S(2)}, u32[]{:S(2)}) collective-permute-start(f32[8,8,1536]{2,1,0:T(8,128)S(1)} %collective-permute-done.12), channel_id=1, source_target_pairs={{0,1},{1,0},{2,3},{3,2},{4,5},{5,4},{6,7},{7,6},{8,9},{9,8},{10,11... | collective-permute-start | bytes 1179656 | tf_op jit(solution)/shard_map/ppermute | solution.py:110
  71.9 0.0 collective-permute-done.14
  71.9 0.0 collective-permute-done.15
  71.9 1.5 %place_chunks.4 = (f32[16,8,2048]{2,1,0:T(8,128)}, f32[16,8,2048]{2,1,0:T(8,128)}, f32[16,8,2048]{2,1,0:T(8,128)}) custom-call(f32[2,4,8,1536]{3,2,1,0:T(8,128)S(1)} %bitcast.30, f32[2,4,8,1536]{3,2,1,0:T(8,128)S(1)} %bitcast.31, f32[2,4,8,1536]{3,2,1,0:T(8,128)S(1)} %bitcast.32, ...), custom_call_target="tpu_custom_call", output_to_operand_aliasing={{0}: (4, {}), {1}: (5, {}), {2}: (6, {})} | custom-call | tf_op jit(solution)/shard_map/place_chunks/pallas_call | solution.py:97
  73.4 0.0 collective-permute-done.11
  73.4 0.0 collective-permute-done.13
  73.5 1.1 %place_chunks.5 = (f32[16,8,2048]{2,1,0:T(8,128)}, f32[16,8,2048]{2,1,0:T(8,128)}, f32[16,8,2048]{2,1,0:T(8,128)}) custom-call(f32[2,4,8,1536]{3,2,1,0:T(8,128)S(1)} %bitcast.35, f32[2,4,8,1536]{3,2,1,0:T(8,128)S(1)} %bitcast.36, f32[16,8,2048]{2,1,0:T(8,128)} %get-tuple-element.39.refs_2_, ...), custom_call_target="tpu_custom_call", output_to_operand_aliasing={{0}: (2, {}), {1}: (3, {}), {2}: (4, {})} | custom-call | tf_op jit(solution)/shard_map/place_chunks/pallas_call | solution.py:97
  (6 shorter events, 0.2 us)
Async XLA Ops:
  3.8 4.7 %collective-permute-start.1 = (f32[8,8,1536]{2,1,0:T(8,128)S(1)}, f32[8,8,1536]{2,1,0:T(8,128)S(1)}, u32[]{:S(2)}, u32[]{:S(2)}) collective-permute-start(f32[8,8,1536]{2,1,0:T(8,128)S(1)} %get-tuple-element.27), channel_id=1, source_target_pairs={{0,1},{1,0},{2,3},{3,2},{4,5},{5,4},{6,7},{7,6},{8,9},{9,8},{10,11... | collective-permute-start | bytes 1179656 | tf_op jit(solution)/shard_map/ppermute | solution.py:110
  7.1 2.7 %collective-permute-start.5 = (f32[8,8,1536]{2,1,0:T(8,128)S(1)}, f32[8,8,1536]{2,1,0:T(8,128)S(1)}, u32[]{:S(2)}, u32[]{:S(2)}) collective-permute-start(f32[8,8,1536]{2,1,0:T(8,128)S(1)} %get-tuple-element.31), channel_id=1, source_target_pairs={{0,1},{1,0},{2,3},{3,2},{4,5},{5,4},{6,7},{7,6},{8,9},{9,8},{10,11... | collective-permute-start | bytes 1179656 | tf_op jit(solution)/shard_map/ppermute | solution.py:110
  7.2 3.1 %collective-permute-start.3 = (f32[8,8,1536]{2,1,0:T(8,128)S(1)}, f32[8,8,1536]{2,1,0:T(8,128)S(1)}, u32[]{:S(2)}, u32[]{:S(2)}) collective-permute-start(f32[8,8,1536]{2,1,0:T(8,128)S(1)} %get-tuple-element.29), channel_id=1, source_target_pairs={{0,1},{1,0},{2,3},{3,2},{4,5},{5,4},{6,7},{7,6},{8,9},{9,8},{10,11... | collective-permute-start | bytes 1179656 | tf_op jit(solution)/shard_map/ppermute | solution.py:110
  7.6 5.1 %collective-permute-start = (f32[8,8,1536]{2,1,0:T(8,128)S(1)}, f32[8,8,1536]{2,1,0:T(8,128)S(1)}, u32[]{:S(2)}, u32[]{:S(2)}) collective-permute-start(f32[8,8,1536]{2,1,0:T(8,128)S(1)} %get-tuple-element.25), channel_id=1, source_target_pairs={{0,1},{1,0},{2,3},{3,2},{4,5},{5,4},{6,7},{7,6},{8,9},{9,8},{10,11... | collective-permute-start | bytes 1179656 | tf_op jit(solution)/shard_map/ppermute | solution.py:110
  8.5 8.6 %collective-permute-start.2 = (f32[8,8,1536]{2,1,0:T(8,128)S(1)}, f32[8,8,1536]{2,1,0:T(8,128)S(1)}, u32[]{:S(2)}, u32[]{:S(2)}) collective-permute-start(f32[8,8,1536]{2,1,0:T(8,128)S(1)} %add.48), channel_id=1, source_target_pairs={{0,8},{64,72},{128,136},{192,200},{2,10},{66,74},{130,138},{194,20... | collective-permute-start | bytes 1179656 | tf_op jit(solution)/shard_map/ppermute | solution.py:167
  9.8 11.4 %collective-permute-start.6 = (f32[8,8,1536]{2,1,0:T(8,128)S(1)}, f32[8,8,1536]{2,1,0:T(8,128)S(1)}, u32[]{:S(2)}, u32[]{:S(2)}) collective-permute-start(f32[8,8,1536]{2,1,0:T(8,128)S(1)} %add.51), channel_id=1, source_target_pairs={{0,16},{64,80},{128,144},{192,208},{2,18},{66,82},{130,146},{194,2... | collective-permute-start | bytes 1179656 | tf_op jit(solution)/shard_map/ppermute | solution.py:167
  10.4 10.9 %collective-permute-start.4 = (f32[8,8,1536]{2,1,0:T(8,128)S(1)}, f32[8,8,1536]{2,1,0:T(8,128)S(1)}, u32[]{:S(2)}, u32[]{:S(2)}) collective-permute-start(f32[8,8,1536]{2,1,0:T(8,128)S(1)} %add.50), channel_id=1, source_target_pairs={{0,24},{64,88},{128,152},{192,216},{2,26},{66,90},{130,154},{194,2... | collective-permute-start | bytes 1179656 | tf_op jit(solution)/shard_map/ppermute | solution.py:167
  32.0 4.6 %collective-permute-start.7 = (f32[8,1536]{1,0:T(8,128)S(1)}, f32[8,1536]{1,0:T(8,128)S(1)}, u32[]{:S(2)}, u32[]{:S(2)}) collective-permute-start(f32[8,1536]{1,0:T(8,128)S(1)} %reduce_sum.9), channel_id=1, source_target_pairs={{0,64},{2,66},{4,68},{6,70},{16,80},{18,82},{20,84},{22,86},{8,72}... | collective-permute-start | bytes 147464 | tf_op jit(solution)/shard_map/ppermute | solution.py:122
  36.6 6.7 %collective-permute-start.8 = (f32[8,1536]{1,0:T(8,128)S(1)}, f32[8,1536]{1,0:T(8,128)S(1)}, u32[]{:S(2)}, u32[]{:S(2)}) collective-permute-start(f32[8,1536]{1,0:T(8,128)S(1)} %add.54), channel_id=1, source_target_pairs={{0,192},{2,194},{4,196},{6,198},{16,208},{18,210},{20,212},{22,214... | collective-permute-start | bytes 147464 | tf_op jit(solution)/shard_map/ppermute | solution.py:123
  53.4 9.2 %collective-permute-start.10 = (f32[8,8,1536]{2,1,0:T(8,128)S(1)}, f32[8,8,1536]{2,1,0:T(8,128)S(1)}, u32[]{:S(2)}, u32[]{:S(2)}) collective-permute-start(f32[8,8,1536]{2,1,0:T(8,128)S(1)} %all_to_all.11), channel_id=1, source_target_pairs={{0,16},{64,80},{128,144},{192,208},{2,18},{66,82},{130,146},{194,2... | collective-permute-start | bytes 1179656 | tf_op jit(solution)/shard_map/ppermute | solution.py:173
  53.8 14.1 %collective-permute-start.9 = (f32[8,8,1536]{2,1,0:T(8,128)S(1)}, f32[8,8,1536]{2,1,0:T(8,128)S(1)}, u32[]{:S(2)}, u32[]{:S(2)}) collective-permute-start(f32[8,8,1536]{2,1,0:T(8,128)S(1)} %all_to_all.11), channel_id=1, source_target_pairs={{0,24},{64,88},{128,152},{192,216},{2,26},{66,90},{130,154},{194,2... | collective-permute-start | bytes 1179656 | tf_op jit(solution)/shard_map/ppermute | solution.py:173
  56.1 11.9 %collective-permute-start.12 = (f32[8,8,1536]{2,1,0:T(8,128)S(1)}, f32[8,8,1536]{2,1,0:T(8,128)S(1)}, u32[]{:S(2)}, u32[]{:S(2)}) collective-permute-start(f32[8,8,1536]{2,1,0:T(8,128)S(1)} %all_to_all.11), channel_id=1, source_target_pairs={{0,8},{64,72},{128,136},{192,200},{2,10},{66,74},{130,138},{194,20... | collective-permute-start | bytes 1179656 | tf_op jit(solution)/shard_map/ppermute | solution.py:173
  56.2 15.7 %collective-permute-start.14 = (f32[8,8,1536]{2,1,0:T(8,128)S(1)}, f32[8,8,1536]{2,1,0:T(8,128)S(1)}, u32[]{:S(2)}, u32[]{:S(2)}) collective-permute-start(f32[8,8,1536]{2,1,0:T(8,128)S(1)} %all_to_all.11), channel_id=1, source_target_pairs={{0,1},{1,0},{2,3},{3,2},{4,5},{5,4},{6,7},{7,6},{8,9},{9,8},{10,11... | collective-permute-start | bytes 1179656 | tf_op jit(solution)/shard_map/ppermute | solution.py:110
  63.7 8.2 %collective-permute-start.15 = (f32[8,8,1536]{2,1,0:T(8,128)S(1)}, f32[8,8,1536]{2,1,0:T(8,128)S(1)}, u32[]{:S(2)}, u32[]{:S(2)}) collective-permute-start(f32[8,8,1536]{2,1,0:T(8,128)S(1)} %collective-permute-done.10), channel_id=1, source_target_pairs={{0,1},{1,0},{2,3},{3,2},{4,5},{5,4},{6,7},{7,6},{8,9},{9,8},{10,11... | collective-permute-start | bytes 1179656 | tf_op jit(solution)/shard_map/ppermute | solution.py:110
  67.9 5.5 %collective-permute-start.11 = (f32[8,8,1536]{2,1,0:T(8,128)S(1)}, f32[8,8,1536]{2,1,0:T(8,128)S(1)}, u32[]{:S(2)}, u32[]{:S(2)}) collective-permute-start(f32[8,8,1536]{2,1,0:T(8,128)S(1)} %collective-permute-done.9), channel_id=1, source_target_pairs={{0,1},{1,0},{2,3},{3,2},{4,5},{5,4},{6,7},{7,6},{8,9},{9,8},{10,11... | collective-permute-start | bytes 1179656 | tf_op jit(solution)/shard_map/ppermute | solution.py:110
  68.0 5.4 %collective-permute-start.13 = (f32[8,8,1536]{2,1,0:T(8,128)S(1)}, f32[8,8,1536]{2,1,0:T(8,128)S(1)}, u32[]{:S(2)}, u32[]{:S(2)}) collective-permute-start(f32[8,8,1536]{2,1,0:T(8,128)S(1)} %collective-permute-done.12), channel_id=1, source_target_pairs={{0,1},{1,0},{2,3},{3,2},{4,5},{5,4},{6,7},{7,6},{8,9},{9,8},{10,11... | collective-permute-start | bytes 1179656 | tf_op jit(solution)/shard_map/ppermute | solution.py:110
